TPU v7x, 128 devices: a whole 4x4x4 slice. The times are simulated.
128 devices in a mesh: wide: 16 (over x_lo, y, core), narrow: 8 (over x_hi, z).
Axes of the slice: x: 4 (x_hi: 2, x_lo: 2; x = x_hi * 2 + x_lo), y: 4, z: 4, core: 2. Of those that a mesh axis runs over, the one named last changes fastest.
Arguments:
- node_features: bfloat16 [131072, 128], P(('wide', 'narrow')), may hold values from -6 to 6
- tile_values: bfloat16 [65536, 128, 128], P(('wide', 'narrow')), may hold values from -0.1875 to 0.1875
- tile_rows: int32 [65536], P(('wide', 'narrow')), may hold values from 0 to 63, as said below
- tile_cols: int32 [65536], P(('wide', 'narrow')), may hold values from 0 to 127, as said below
- tile_count: int32 [128], P(('wide', 'narrow')), may hold values from 64 to 512, as said below
- weight_self: bfloat16 [128, 256], replicated, may hold values from -0.5 to 0.5
- weight_neigh: bfloat16 [128, 256], replicated, may hold values from -0.5 to 0.5
- bias_vector: float32 [256], replicated, may hold values from -3 to 3
- grad_output: bfloat16 [131072, 256], P(('wide', 'narrow')), may hold values from -6 to 6
Outputs:
- node_output: bfloat16 [131072, 256], P(('wide', 'narrow'))
- grad_input: bfloat16 [131072, 128], P(('wide', 'narrow'))
- grad_self: float32 [128, 256], replicated
- grad_neigh: float32 [128, 256], replicated
- grad_bias: float32 [256], replicated
Inputs may be any that keep to these rules, and one draw needn't show every extreme that they name: `tile_rows`: each device's 512 slots name distinct tiles in ascending order of row tile, then column tile. `tile_cols`: column tile c lies in the panel of device (c // 8, n) of the column group. `tile_count`: some device has all 512 slots live.
All inputs are finite; a program needn't handle non-finite values.
Results may differ from a plain program's by a relative error of at most 0.029.
Values may be sent and summed in bfloat16 or wider, within the bound.
No kernel may reach another device: no remote copies, remote signals or barrier semaphores. Data moves between devices by JAX's collectives and lax.ppermute only.
A program may use at most 256 MiB of HBM per device.

v0:
```python
import jax
import jax.numpy as jnp
from jax import lax
from jax.sharding import PartitionSpec as P


def tile_products(values, index_in, source, transpose):
    tile_size = values.shape[1]
    features = source.shape[1]
    in_tiles = source.shape[0] // tile_size
    blocks = source.reshape(in_tiles, tile_size * features)
    select = (index_in[:, None] == jnp.arange(in_tiles, dtype=jnp.int32)[None, :]).astype(
        jnp.bfloat16
    )
    picked = jnp.dot(select, blocks, preferred_element_type=jnp.float32).astype(jnp.bfloat16)
    picked = picked.reshape(values.shape[0], tile_size, features)
    pattern = "tji,tjf->tif" if transpose else "tij,tjf->tif"
    return jnp.einsum(pattern, values, picked, preferred_element_type=jnp.float32)


def split_parts(products):
    flat = products.reshape(products.shape[0], -1)
    upper = flat.astype(jnp.bfloat16)
    lower = (flat - upper.astype(jnp.float32)).astype(jnp.bfloat16)
    return (upper, lower)


def add_tiles(parts, index_out, present, out_tiles, tile_size):
    upper, lower = parts
    wanted = jnp.arange(out_tiles, dtype=jnp.int32)
    select = ((index_out[None, :] == wanted[:, None]) & present[None, :]).astype(jnp.bfloat16)
    totals = jnp.dot(select, upper, preferred_element_type=jnp.float32)
    totals = totals + jnp.dot(select, lower, preferred_element_type=jnp.float32)
    return totals.reshape(out_tiles * tile_size, -1)


def contract_rows(left, right):
    return lax.dot_general(
        left, right, (((0,), (0,)), ((), ())), preferred_element_type=jnp.float32
    )


def contract_cols(left, right):
    return lax.dot_general(
        left, right, (((1,), (1,)), ((), ())), preferred_element_type=jnp.float32
    )


def local(
    node_features,
    tile_values,
    tile_rows,
    tile_cols,
    tile_count,
    weight_self,
    weight_neigh,
    bias_vector,
    grad_output,
):
    tile_size = tile_values.shape[1]
    own_nodes = node_features.shape[0]
    wide_count = lax.axis_size("wide")
    narrow_count = lax.axis_size("narrow")
    row_tiles = narrow_count * own_nodes // tile_size
    col_tiles = wide_count * own_nodes // tile_size
    present = jnp.arange(tile_values.shape[0]) < tile_count[0]
    panels = lax.all_gather(node_features, "wide", axis=0, tiled=True)
    forward_parts = split_parts(tile_products(tile_values, tile_cols, panels, False))
    partial_agg = add_tiles(forward_parts, tile_rows, present, row_tiles, tile_size)
    own_agg = lax.psum_scatter(
        partial_agg.astype(jnp.bfloat16), "narrow", scatter_dimension=0, tiled=True
    )
    preact = jnp.dot(node_features, weight_self, preferred_element_type=jnp.float32)
    preact = (
        preact + jnp.dot(own_agg, weight_neigh, preferred_element_type=jnp.float32) + bias_vector
    )
    sigma = jax.nn.sigmoid(preact)
    output = (preact * sigma).astype(jnp.bfloat16)
    grad_pre = (grad_output.astype(jnp.float32) * sigma * (1.0 + preact * (1.0 - sigma))).astype(
        jnp.bfloat16
    )
    grad_agg = contract_cols(grad_pre, weight_neigh).astype(jnp.bfloat16)
    node_output, grad_pre, grad_agg = (output, grad_pre, grad_agg)
    stripe_grad = lax.all_gather(grad_agg, "narrow", axis=0, tiled=True)
    local_terms = (
        contract_rows(node_features, grad_pre),
        contract_rows(own_agg, grad_pre),
        jnp.sum(grad_pre.astype(jnp.float32), axis=0),
    )
    back_parts = split_parts(tile_products(tile_values, tile_rows, stripe_grad, True))
    full_column = add_tiles(back_parts, tile_cols, present, col_tiles, tile_size)
    grad_column = lax.psum_scatter(
        full_column.astype(jnp.bfloat16), "wide", scatter_dimension=0, tiled=True
    ).astype(jnp.float32)
    totals = lax.psum((local_terms[0], local_terms[1], local_terms[2]), ("wide", "narrow"))
    grad_input = (contract_cols(grad_pre, weight_self) + grad_column).astype(jnp.bfloat16)
    scale = float(own_nodes * wide_count * narrow_count) ** (-0.5)
    return (node_output, grad_input, totals[0] * scale, totals[1] * scale, totals[2] * scale)


def solution(mesh):
    placed = (
        P(("wide", "narrow"), None),
        P(("wide", "narrow"), None, None),
        P(("wide", "narrow")),
        P(("wide", "narrow")),
        P(("wide", "narrow")),
        P(),
        P(),
        P(),
        P(("wide", "narrow"), None),
    )
    return jax.shard_map(
        local,
        mesh=mesh,
        in_specs=placed,
        out_specs=(P(("wide", "narrow"), None), P(("wide", "narrow"), None), P(), P(), P()),
        check_vma=False,
    )
```

profile of v0, /device:TPU:0, one launch (start us, length us, event | category | flops | bytes accessed | tf_op | source)
XLA Modules:
  0.0 535.6 jit_solution(16979682063546649474)
XLA Ops:
  7.2 0.0 copy-start
  7.2 0.0 all-gather.3.cloned.1.call-start
  7.2 0.7 all-gather.3.cloned.1.call-update
  7.9 0.0 reduce-scatter.3.cloned.1.call-start
  8.6 41.0 %all-gather.3.cloned.1.call-done = bf16[16384,128]{1,0:T(8,128)(2,1)} async-done(((bf16[1024,128]{1,0:T(8,128)(2,1)}), bf16[16384,128]{1,0:T(8,128)(2,1)}) %all-gather.3.cloned.1.call-update) | async-done | bytes 4194320 | tf_op jit(solution)/shard_map/all_gather | solution.py:67
  49.6 7.3 %reshape.41 = bf16[128,16384]{1,0:T(8,128)(2,1)} reshape(bf16[16384,128]{1,0:T(8,128)(2,1)} %all-gather.3.cloned.1.call-done) | data formatting | bytes 8388608 | tf_op jit(solution)/shard_map/reshape | solution.py:11
  56.9 7.0 %fusion.5 = bf16[64,8,128,128]{3,1,2,0:T(8,128)(2,1)S(1)} fusion(bf16[128,16384]{1,0:T(8,128)(2,1)} %reshape.41, s32[512]{0:T(512)} %param.12), kind=kOutput, calls=%fused_computation.15 | convolution fusion | flops 2155937792 | bytes 20973568 | tf_op jit(solution)/shard_map/dot_general | solution.py:15
  63.9 8.3 %copy.29 = bf16[64,8,128,128]{3,2,1,0:T(8,128)(2,1)} copy(bf16[64,8,128,128]{3,1,2,0:T(8,128)(2,1)S(1)} %fusion.5) | data formatting | bytes 33554432
  72.2 25.2 %convolution_bitcast_fusion.1 = f32[512,128,128]{1,2,0:T(8,128)} fusion(bf16[512,128,128]{2,1,0:T(8,128)(2,1)} %bitcast.48, bf16[512,128,128]{2,1,0:T(8,128)(2,1)} %param.10), kind=kOutput, calls=%fused_computation.13 | convolution fusion | flops 2147483648 | bytes 67108864 | tf_op jit(solution)/shard_map/tij,tjf->tif/dot_general | solution.py:18
  97.4 34.8 %copy.20 = f32[512,128,128]{0,2,1:T(8,128)} copy(f32[512,128,128]{1,2,0:T(8,128)} %convolution_bitcast_fusion.1) | data formatting | bytes 67108864 | tf_op jit(solution)/shard_map/tij,tjf->tif/dot_general | solution.py:18
  132.2 0.0 copy-start.3
  132.2 23.6 %fusion.1 = (bf16[512,16384]{0,1:T(8,128)(2,1)}, bf16[512,16384]{0,1:T(8,128)(2,1)}) fusion(f32[512,128,128]{0,2,1:T(8,128)} %copy.20), kind=kLoop, calls=%fused_computation.5 | loop fusion | flops 33554432 | bytes 67108864 | tf_op jit(solution)/shard_map/convert_element_type | solution.py:24
  155.8 0.0 copy-done.3
  155.8 12.8 %fusion.18 = f32[64,16384]{1,0:T(8,128)} fusion(bf16[512,16384]{0,1:T(8,128)(2,1)} %get-tuple-element.22, s32[512]{0:T(512)S(1)} %copy-done.3, pred[512]{0:T(512)(128)(4,1)S(1)} %iota_compare_fusion.6), kind=kOutput, calls=%fused_computation.37 | convolution fusion | flops 1073807360 | bytes 20974080 | tf_op jit(solution)/shard_map/dot_general | solution.py:32
  168.6 0.0 copy-start.2
  168.6 0.0 copy-start.5
  168.6 0.0 copy-start.6
  168.6 0.0 copy-start.7
  168.6 12.2 %fusion.3 = bf16[64,16384]{1,0:T(8,128)(2,1)S(1)} fusion(f32[64,16384]{1,0:T(8,128)} %fusion.18, bf16[512,16384]{0,1:T(8,128)(2,1)} %get-tuple-element.21, s32[512]{0:T(512)S(1)} %copy-done.3, pred[512]{0:T(512)(128)(4,1)S(1)} %iota_compare_fusion.6), kind=kOutput, calls=%fused_computation.11 | convolution fusion | flops 1075904512 | bytes 23071232 | tf_op jit(solution)/shard_map/dot_general | solution.py:33
  180.8 2.4 convert_element_type.66
  183.1 0.0 reduce-scatter.3.cloned.1.call-update
  183.2 0.0 all-gather.5.cloned.1.call-start
  183.2 0.0 copy-done.2
  183.2 0.0 copy-done.5
  183.2 0.3 fusion.26
  183.5 74.9 %reduce-scatter.3.cloned.1.call-done = bf16[1024,128]{1,0:T(8,128)(2,1)} async-done(((bf16[8192,128]{1,0:T(8,128)(2,1)}), bf16[1024,128]{1,0:T(8,128)(2,1)}) %reduce-scatter.3.cloned.1.call-update) | async-done | bytes 262160 | tf_op jit(solution)/shard_map/reduce_scatter | solution.py:70
  258.4 0.0 copy-done
  258.4 0.0 copy-done.6
  258.4 0.0 copy-done.7
  258.5 2.4 convert_reduce_fusion
  260.9 1.0 convolution_convert_fusion.2
  261.9 0.0 all-gather.5.cloned.1.call-update
  261.9 0.0 all-reduce.3.cloned.1.call-start
  262.0 1.0 convolution_bitcast_fusion.2
  262.9 2.0 fusion.27
  264.9 0.0 all-reduce.3.cloned.1.call-update
  264.9 0.2 reduce-scatter.5.cloned.1.call-start
  265.2 49.9 %all-gather.5.cloned.1.call-done = bf16[8192,128]{1,0:T(8,128)(2,1)} async-done(((bf16[1024,128]{1,0:T(8,128)(2,1)}), bf16[8192,128]{1,0:T(8,128)(2,1)}) %all-gather.5.cloned.1.call-update) | async-done | bytes 2097168 | tf_op jit(solution)/shard_map/all_gather | solution.py:84
  315.0 2.8 reshape.44
  317.8 4.8 fusion.4
  322.6 8.3 %copy.30 = bf16[64,8,128,128]{3,2,1,0:T(8,128)(2,1)} copy(bf16[64,8,128,128]{3,1,2,0:T(8,128)(2,1)S(1)} %fusion.4) | data formatting | bytes 33554432
  330.9 24.7 %convolution_bitcast_fusion = f32[512,128,128]{1,2,0:T(8,128)} fusion(bf16[512,128,128]{2,1,0:T(8,128)(2,1)} %bitcast.49, bf16[512,128,128]{2,1,0:T(8,128)(2,1)} %param.10), kind=kOutput, calls=%fused_computation.12 | convolution fusion | flops 2147483648 | bytes 67108864 | tf_op jit(solution)/shard_map/tji,tjf->tif/dot_general | solution.py:18
  355.6 34.8 %copy.22 = f32[512,128,128]{0,2,1:T(8,128)} copy(f32[512,128,128]{1,2,0:T(8,128)} %convolution_bitcast_fusion) | data formatting | bytes 67108864 | tf_op jit(solution)/shard_map/tji,tjf->tif/dot_general | solution.py:18
  390.4 0.0 copy-start.4
  390.4 23.6 %fusion = (bf16[512,16384]{0,1:T(8,128)(2,1)}, bf16[512,16384]{0,1:T(8,128)(2,1)}) fusion(f32[512,128,128]{0,2,1:T(8,128)} %copy.22), kind=kLoop, calls=%fused_computation.2 | loop fusion | flops 33554432 | bytes 67108864 | tf_op jit(solution)/shard_map/convert_element_type | solution.py:24
  414.0 0.0 copy-done.4
  414.0 14.6 %fusion.10 = f32[128,16384]{1,0:T(8,128)} fusion(bf16[512,16384]{0,1:T(8,128)(2,1)} %get-tuple-element.20, s32[512]{0:T(512)S(1)} %copy-done.4, pred[512]{0:T(512)(128)(4,1)S(1)} %iota_compare_fusion.6), kind=kOutput, calls=%fused_computation.30 | convolution fusion | flops 2147614720 | bytes 25168384 | tf_op jit(solution)/shard_map/dot_general | solution.py:32
  428.6 0.0 copy-start.1
  428.6 12.5 %fusion.2 = bf16[128,16384]{1,0:T(8,128)(2,1)} fusion(f32[128,16384]{1,0:T(8,128)} %fusion.10, bf16[512,16384]{0,1:T(8,128)(2,1)} %get-tuple-element.19, s32[512]{0:T(512)S(1)} %copy-done.4, pred[512]{0:T(512)(128)(4,1)S(1)} %iota_compare_fusion.6), kind=kOutput, calls=%fused_computation.9 | convolution fusion | flops 2151809024 | bytes 29362688 | tf_op jit(solution)/shard_map/dot_general | solution.py:33
  441.1 7.4 %convert_element_type.76 = bf16[16384,128]{1,0:T(8,128)(2,1)} reshape(bf16[128,16384]{1,0:T(8,128)(2,1)} %fusion.2) | data formatting | bytes 8388608 | tf_op jit(solution)/shard_map/convert_element_type | solution.py:93
  448.5 0.0 reduce-scatter.5.cloned.1.call-update
  448.5 66.4 %psum.23 = f32[256]{0:T(256)S(1)} all-reduce(f32[256]{0:T(256)S(1)} %get-tuple-element.17), channel_id=1, replica_groups=mesh['wide'=16,'narrow'=8] {'wide','narrow'}, use_global_device_ids=true, to_apply=%region_5.0 | all-reduce | flops 256 | bytes 2048 | tf_op jit(solution)/shard_map/psum | solution.py:95
  514.9 0.6 broadcast_multiply_fusion.2
  515.5 0.0 all-reduce.3.cloned.1.call-done
  515.5 1.0 broadcast_multiply_fusion
  516.5 0.8 copy.25
  517.3 0.8 copy.24
  518.0 9.1 %reduce-scatter.5.cloned.1.call-done = bf16[1024,128]{1,0:T(8,128)(2,1)} async-done(((bf16[16384,128]{1,0:T(8,128)(2,1)}), bf16[1024,128]{1,0:T(8,128)(2,1)}) %reduce-scatter.5.cloned.1.call-update) | async-done | bytes 262160 | tf_op jit(solution)/shard_map/reduce_scatter | solution.py:92
  527.1 1.9 fusion.7
  529.0 0.0 copy-done.1
  (1 shorter events, 0.0 us)
Async XLA Ops:
  7.2 251.3 %copy-start = (bf16[128,256]{1,0:T(8,128)(2,1)S(1)}, bf16[128,256]{1,0:T(8,128)(2,1)}, u32[]{:S(2)}) copy-start(bf16[128,256]{1,0:T(8,128)(2,1)} %param.15) | copy-start | bytes 196612
  7.2 42.4 %all-gather.3.cloned.1.call-start = ((), (), s32[]{:S(2)}) async-start(), calls=%async_computation.2 | async-start | bytes 4456448 | tf_op jit(solution)/shard_map/all_gather | solution.py:67
  7.9 250.5 %reduce-scatter.3.cloned.1.call-start = ((), (), s32[]{:S(2)}) async-start(), calls=%async_computation.3 | async-start | bytes 2359296 | tf_op jit(solution)/shard_map/reduce_scatter | solution.py:70
  132.2 23.6 %copy-start.3 = (s32[512]{0:T(512)S(1)}, s32[512]{0:T(512)}, u32[]{:S(2)}) copy-start(s32[512]{0:T(512)} %param.11) | copy-start | bytes 6148
  168.6 14.6 %copy-start.2 = (bf16[1024,128]{1,0:T(8,128)(2,1)S(1)}, bf16[1024,128]{1,0:T(8,128)(2,1)}, u32[]{:S(2)}) copy-start(bf16[1024,128]{1,0:T(8,128)(2,1)} %param.9) | copy-start | bytes 786436
  168.6 14.6 %copy-start.5 = (bf16[128,256]{1,0:T(8,128)(2,1)S(1)}, bf16[128,256]{1,0:T(8,128)(2,1)}, u32[]{:S(2)}) copy-start(bf16[128,256]{1,0:T(8,128)(2,1)} %param.14) | copy-start | bytes 196612
  168.6 89.8 %copy-start.6 = (bf16[1024,256]{1,0:T(8,128)(2,1)S(1)}, bf16[1024,256]{1,0:T(8,128)(2,1)}, u32[]{:S(2)}) copy-start(bf16[1024,256]{1,0:T(8,128)(2,1)} %param.17) | copy-start | bytes 1572868
  168.6 89.8 %copy-start.7 = (f32[256]{0:T(256)S(1)}, f32[256]{0:T(256)}, u32[]{:S(2)}) copy-start(f32[256]{0:T(256)} %param.16) | copy-start | bytes 3076
  183.2 131.8 %all-gather.5.cloned.1.call-start = ((), (), s32[]{:S(2)}) async-start(), calls=%async_computation.4 | async-start | bytes 2359296 | tf_op jit(solution)/shard_map/all_gather | solution.py:84
  261.9 253.6 %all-reduce.3.cloned.1.call-start = ((), (), s32[]{:S(2)}) async-start(), calls=%async_computation.6 | async-start | bytes 524288 | tf_op jit(solution)/shard_map/psum | solution.py:95
  264.9 262.2 %reduce-scatter.5.cloned.1.call-start = ((), (), s32[]{:S(2)}) async-start(), calls=%async_computation.5 | async-start | bytes 4456448 | tf_op jit(solution)/shard_map/reduce_scatter | solution.py:92
  390.4 23.6 %copy-start.4 = (s32[512]{0:T(512)S(1)}, s32[512]{0:T(512)}, u32[]{:S(2)}) copy-start(s32[512]{0:T(512)} %param.12) | copy-start | bytes 6148
  428.6 100.4 %copy-start.1 = (bf16[128,256]{1,0:T(8,128)(2,1)S(1)}, bf16[128,256]{1,0:T(8,128)(2,1)}, u32[]{:S(2)}) copy-start(bf16[128,256]{1,0:T(8,128)(2,1)} %param.15) | copy-start | bytes 196612
Sparse Core Ops, SparseCore 0:
  9.7 39.8 all-gather.2
  183.3 75.1 reduce-scatter.2
  262.0 52.9 all-gather.4
  320.4 140.3 all-reduce.2
  463.0 64.0 reduce-scatter.4
where the time goes:
time: 537 us; the launch traced here: 536 us
  waiting for transfers between devices  176 us (33%)
  matrix products  122 us (23%)
  local copies, waits for them, and re-layouts  108 us (20%)
  blocking collectives  66.4 us (12%)
  other arithmetic  48.8 us (9%)
  between operations  14.5 us (3%)
    reduce_scatter x1, waiting for transfers between devices, local(): lax.psum_scatter(partial_agg.astype(jnp.bfloat16), 'narrow', scatter_dime...  74.9 us
    dot_general x2, local copies, waits for them, and re-layouts, tile_products(): jnp.einsum(pattern, values, picked, preferred_element_type=jnp.float32)  69.6 us
    psum x1, blocking collectives, local(): lax.psum((local_terms[0], local_terms[1], local_terms[2]), ('wide', 'narr...  66.4 us
    all_gather x1, waiting for transfers between devices, local(): stripe_grad = lax.all_gather(grad_agg, 'narrow', axis=0, tiled=True)  49.9 us
    dot_general x2, matrix products, tile_products(): jnp.einsum(pattern, values, picked, preferred_element_type=jnp.float32)  49.8 us
    convert_element_type x2, other arithmetic, split_parts(): lower = (flat - upper.astype(jnp.float32)).astype(jnp.bfloat16)  47.2 us
    all_gather x1, waiting for transfers between devices, local(): panels = lax.all_gather(node_features, 'wide', axis=0, tiled=True)  41 us
    dot_general x2, matrix products, add_tiles(): totals = jnp.dot(select, upper, preferred_element_type=jnp.float32)  27.4 us
  transfers between devices with their start and end apart: 5, of which 4 were waited for; matrix products, arithmetic and copies ran while one was open for 26% of the time, Pallas kernels for 0%

commit v1 on v0

v1 whole, which is shorter than its diff:
```python
import jax
import jax.numpy as jnp
from jax import lax
from jax.experimental import pallas as pl
from jax.experimental.pallas import tpu as pltpu
from jax.sharding import PartitionSpec as P

TILE = 128
X_LO, Y, CORES = 2, 4, 2
X_HI, Z = 2, 4
PANEL = 8
CHUNK = 32
UNROLL = 32
BATCH = 4
SLICE = 32
VMEM_BYTES = 56 * 1024 * 1024
RELATIVE = [(dx, dy) for dx in (0, 1) for dy in range(4)]


def wide_index(w, dx, dy, dc):
    return ((w >> 3) ^ dx) * 8 + ((((w >> 1) & 3) + dy) & 3) * 2 + ((w & 1) ^ dc)


def narrow_index(n, dx, dz):
    return ((n >> 2) ^ dx) * 4 + (((n & 3) + dz) & 3)


def from_wide(x, dx, dy, dc):
    return lax.ppermute(x, "wide", [(wide_index(w, dx, dy, dc), w) for w in range(16)])


def from_narrow(x, dx, dz):
    return lax.ppermute(x, "narrow", [(narrow_index(n, dx, dz), n) for n in range(8)])


def gather_ring(x, fetch):
    got = {(0, 0): x}
    got[0, 1] = fetch(x, 0, 1)
    got[0, 3] = fetch(x, 0, 3)
    got[1, 0] = fetch(x, 1, 0)
    got[0, 2] = fetch(got[0, 1], 0, 1)
    got[1, 1] = fetch(got[1, 0], 0, 1)
    got[1, 3] = fetch(got[1, 0], 0, 3)
    got[1, 2] = fetch(got[0, 2], 1, 0)
    return [got[key] for key in RELATIVE]


def load_tiles(tiles_hbm, tiles, sems, count):
    chunks = tiles_hbm.shape[0] // CHUNK
    copies = [
        pltpu.make_async_copy(
            tiles_hbm.at[pl.ds(k * CHUNK, CHUNK)], tiles.at[pl.ds(k * CHUNK, CHUNK)], sems.at[k]
        )
        for k in range(chunks)
    ]
    for k, copy in enumerate(copies):

        @pl.when(k * CHUNK < count)
        def _():
            copy.start()


def wait_chunk(tiles_hbm, tiles, sems, k):
    span = pl.ds(k * CHUNK, CHUNK)
    pltpu.make_async_copy(tiles_hbm.at[span], tiles.at[span], sems.at[k]).wait()


def plan_kernel(meta, rows, pairs, total):
    slots, trash = rows.shape[0], meta[3]
    count = meta[0]

    def place(state):
        s, k = state
        row = rows[s]
        after = jnp.minimum(s + 1, slots - 1)
        both = (s + 1 < count) & (rows[after] == row)
        pairs[0, k] = row
        pairs[1, k] = s
        pairs[2, k] = jnp.where(both, s + 1, slots)
        return s + 1 + both.astype(jnp.int32), k + 1

    _, k = lax.while_loop(lambda state: state[0] < count, place, (jnp.int32(0), jnp.int32(0)))
    total[0] = (k + UNROLL - 1) // UNROLL
    for u in range(UNROLL):
        pairs[0, k + u] = trash
        pairs[1, k + u] = slots
        pairs[2, k + u] = slots


def visit_pairs(count, total, pairs, visit, tiles_hbm, tiles, sems):
    last = (count + CHUNK - 1) // CHUNK - 1

    def group(i, arrived):
        needed = jnp.minimum((pairs[1, i * UNROLL + UNROLL - 1] + 1) // CHUNK, last)

        def wait(k, carry):
            wait_chunk(tiles_hbm, tiles, sems, k)
            return carry

        lax.fori_loop(arrived, needed + 1, wait, 0)
        visit([[pairs[j, i * UNROLL + u] for j in range(3)] for u in range(UNROLL)])
        return needed + 1

    lax.fori_loop(0, total[0], group, jnp.int32(0))


def forward_kernel(meta, cols, pairs, total, tiles_hbm, *refs):
    panels_hbm, outs = refs[:16], refs[16:24]
    panels, tiles, acc, panel_sems, tile_sems = refs[24:]
    count, w, n = meta[0], meta[1], meta[2]
    copies = []
    for k in range(16):
        dx, dy = RELATIVE[k % 8]
        owner = wide_index(w, dx, dy, k // 8)
        copies.append(
            pltpu.make_async_copy(
                panels_hbm[k], panels.at[pl.ds(owner * 1024, 1024)], panel_sems.at[k]
            )
        )
    for copy in copies:
        copy.start()
    load_tiles(tiles_hbm, tiles, tile_sems, count)
    acc[...] = jnp.zeros_like(acc)
    tiles[tiles.shape[0] - 1] = jnp.zeros(tiles.shape[1:], tiles.dtype)
    spare = pl.ds(panels.shape[0] - TILE, TILE)
    panels[spare, :] = jnp.zeros((TILE, panels.shape[1]), panels.dtype)
    for copy in copies:
        copy.wait()

    def panel(s):
        column = pl.multiple_of(cols[s] * TILE, TILE)
        return panels[pl.ds(column, TILE), :]

    def visit(group):
        for part in range(0, UNROLL, BATCH):
            products = []
            for row, first, second in group[part : part + BATCH]:
                left = jnp.concatenate([tiles[first], tiles[second]], axis=1)
                right = jnp.concatenate([panel(first), panel(second)], axis=0)
                products.append(jnp.dot(left, right, preferred_element_type=jnp.float32))
            for (row, _, _), product in zip(group[part : part + BATCH], products):
                acc[row] += product

    visit_pairs(count, total, pairs, visit, tiles_hbm, tiles, tile_sems)
    for k, (dx, dz) in enumerate(RELATIVE):
        owner = narrow_index(n, dx, dz)
        block = acc[pl.ds(owner * PANEL, PANEL)]
        outs[k][...] = block.reshape(PANEL * TILE, -1).astype(jnp.bfloat16)


def dense_kernel(
    own, r1, r2, r3, r4, r5, r6, r7, x, ws, wn, bias, grad, output, agg_out, pre_out, back_out
):
    agg = own[...].astype(jnp.float32)
    for r in (r1, r2, r3, r4, r5, r6, r7):
        agg = agg + r[...].astype(jnp.float32)
    agg = agg.astype(jnp.bfloat16)
    agg_out[...] = agg
    preact = jnp.dot(x[...], ws[...], preferred_element_type=jnp.float32)
    preact = preact + jnp.dot(agg, wn[...], preferred_element_type=jnp.float32) + bias[...]
    sigma = jax.nn.sigmoid(preact)
    output[...] = (preact * sigma).astype(jnp.bfloat16)
    pre = grad[...].astype(jnp.float32) * sigma * (1.0 + preact * (1.0 - sigma))
    pre = pre.astype(jnp.bfloat16)
    pre_out[...] = pre
    back = lax.dot_general(
        wn[...], pre, (((1,), (1,)), ((), ())), preferred_element_type=jnp.float32
    )
    back = back.astype(jnp.bfloat16)
    for k in range(back_out.shape[0]):
        back_out[k] = back[:, k * TILE : (k + 1) * TILE]


def weight_kernel(scale, meta, x, agg, pre, ws, far, near, self_term):
    rows = (((0,), (0,)), ((), ()))
    n = meta[2]
    block = pre[...]
    half = [
        scale * lax.dot_general(v[...], block, rows, preferred_element_type=jnp.float32)
        for v in (x, agg)
    ]
    mine = (n >> 2) == 0
    total = scale * jnp.sum(block.astype(jnp.float32), axis=0, keepdims=True)
    total = jnp.broadcast_to(total, (8, total.shape[1]))
    for out, grads in (
        (near, jnp.where(mine, half[0], half[1])),
        (far, jnp.where(mine, half[1], half[0])),
    ):
        for z in range(Z):
            place = (z - n) & 3
            out[place, :SLICE] = grads[z * SLICE : (z + 1) * SLICE]
            out[place, SLICE:] = total
    self_term[...] = lax.dot_general(
        block, ws[...], (((1,), (1,)), ((), ())), preferred_element_type=jnp.float32
    )


def assemble_kernel(meta, s0, s1, s2, s3, other, grad_self, grad_neigh, grad_bias):
    n = meta[2]
    mine = (n >> 2) == 0
    grad_bias[...] = s0[SLICE : SLICE + 1, :]
    for dz, s in enumerate((s0, s1, s2, s3)):
        place = pl.ds(pl.multiple_of(((n + dz) & 3) * SLICE, SLICE), SLICE)
        here, there = s[:SLICE, :], other[dz, :SLICE, :]
        grad_self[place, :] = jnp.where(mine, here, there)
        grad_neigh[place, :] = jnp.where(mine, there, here)


def backward_kernel(meta, cols, pairs, total, tiles_hbm, *refs):
    grads_hbm, (swap, keep) = refs[:8], refs[8:10]
    grads, tiles, acc, grad_sems, tile_sems = refs[10:]
    count, w, n = meta[0], meta[1], meta[2]
    copies = []
    for k, (dx, dz) in enumerate(RELATIVE):
        owner = narrow_index(n, dx, dz)
        copies.append(
            pltpu.make_async_copy(
                grads_hbm[k], grads.at[pl.ds(owner * PANEL, PANEL)], grad_sems.at[k]
            )
        )
    for copy in copies:
        copy.start()
    load_tiles(tiles_hbm, tiles, tile_sems, count)
    acc[...] = jnp.zeros_like(acc)
    tiles[tiles.shape[0] - 1] = jnp.zeros(tiles.shape[1:], tiles.dtype)
    grads[grads.shape[0] - 1] = jnp.zeros(grads.shape[1:], grads.dtype)
    for copy in copies:
        copy.wait()

    def visit(group):
        for part in range(0, UNROLL, BATCH):
            products = []
            for row, first, second in group[part : part + BATCH]:
                right = jnp.concatenate([tiles[first], tiles[second]], axis=1)
                products.append(jnp.dot(grads[row], right, preferred_element_type=jnp.float32))
            for (_, first, second), product in zip(group[part : part + BATCH], products):
                acc[cols[first]] += product[:, :TILE]
                acc[cols[second]] += product[:, TILE:]

    visit_pairs(count, total, pairs, visit, tiles_hbm, tiles, tile_sems)
    for k, (dx, dy) in enumerate(RELATIVE):
        for dc, out in ((0, keep), (1, swap)):
            owner = wide_index(w, dx, dy, dc)
            out[k] = acc[pl.ds(owner * PANEL, PANEL)].astype(jnp.bfloat16)


def final_kernel(keep, swapped, r1, r2, r3, r4, r5, r6, r7, self_term, out):
    for j in range(r1.shape[0]):
        total = keep[0, j].astype(jnp.float32) + swapped[0, j].astype(jnp.float32)
        for r in (r1, r2, r3, r4, r5, r6, r7):
            total = total + r[j].astype(jnp.float32)
        rows = pl.ds(j * TILE, TILE)
        out[rows, :] = (self_term[rows, :] + total.T).astype(jnp.bfloat16)


def local(
    node_features,
    tile_values,
    tile_rows,
    tile_cols,
    tile_count,
    weight_self,
    weight_neigh,
    bias_vector,
    grad_output,
):
    slots = tile_values.shape[0]
    own_nodes, features = node_features.shape
    hidden = weight_self.shape[1]
    wide_count = lax.axis_size("wide")
    narrow_count = lax.axis_size("narrow")
    row_tiles = narrow_count * PANEL
    col_tiles = wide_count * PANEL
    w, n = lax.axis_index("wide"), lax.axis_index("narrow")
    meta = jnp.stack([tile_count[0], w.astype(jnp.int32), n.astype(jnp.int32), row_tiles])
    dead = jnp.full((1,), col_tiles, jnp.int32)
    cols = jnp.concatenate([tile_cols, dead])
    smem = pl.BlockSpec(memory_space=pltpu.SMEM)
    hbm = pl.BlockSpec(memory_space=pl.ANY)
    vmem = pl.BlockSpec(memory_space=pltpu.VMEM)
    scale = float(own_nodes * wide_count * narrow_count) ** (-0.5)
    bf16, f32 = jnp.bfloat16, jnp.float32
    tile_dots = pl.CostEstimate(
        flops=2 * slots * TILE * TILE * features,
        bytes_accessed=2 * slots * TILE * TILE + 6 * 1024 * 1024,
        transcendentals=0,
    )

    with jax.named_scope("gather_features"):
        same_core = gather_ring(node_features, lambda v, dx, dy: from_wide(v, dx, dy, 0))
        other_core = [from_wide(v, 0, 0, 1) for v in same_core]

    with jax.named_scope("plan"):
        pairs, total = pl.pallas_call(
            plan_kernel,
            out_shape=[
                jax.ShapeDtypeStruct((3, (slots + row_tiles) // 2 + UNROLL), jnp.int32),
                jax.ShapeDtypeStruct((1,), jnp.int32),
            ],
            in_specs=[smem] * 2,
            out_specs=[smem] * 2,
            name="plan",
        )(meta, tile_rows)

    with jax.named_scope("aggregate"):
        partial = pl.pallas_call(
            forward_kernel,
            out_shape=[jax.ShapeDtypeStruct((own_nodes, features), bf16)] * 8,
            in_specs=[smem] * 4 + [hbm] * 17,
            out_specs=[vmem] * 8,
            scratch_shapes=[
                pltpu.VMEM(((col_tiles + 1) * TILE, features), bf16),
                pltpu.VMEM((slots + 1, TILE, TILE), bf16),
                pltpu.VMEM((row_tiles + 1, TILE, features), f32),
                pltpu.SemaphoreType.DMA((16,)),
                pltpu.SemaphoreType.DMA((slots // CHUNK,)),
            ],
            compiler_params=pltpu.CompilerParams(vmem_limit_bytes=VMEM_BYTES),
            cost_estimate=tile_dots,
            name="aggregate",
        )(meta, cols, pairs, total, tile_values, *same_core, *other_core)

    with jax.named_scope("scatter_aggregate"):
        received = [
            from_narrow(partial[k], dx, -dz & 3)
            for k, (dx, dz) in enumerate(RELATIVE)
            if k > 0
        ]

    block = own_nodes // 2
    node_spec = pl.BlockSpec((block, features), lambda i: (i, 0))
    hid_spec = pl.BlockSpec((block, hidden), lambda i: (i, 0))
    weight_spec = pl.BlockSpec((features, hidden), lambda i: (0, 0))
    piece_spec = pl.BlockSpec((block // TILE, features, TILE), lambda i: (i, 0, 0))
    with jax.named_scope("dense"):
        output, own_agg, grad_pre, back = pl.pallas_call(
            dense_kernel,
            grid=(own_nodes // block,),
            out_shape=[
                jax.ShapeDtypeStruct((own_nodes, hidden), bf16),
                jax.ShapeDtypeStruct((own_nodes, features), bf16),
                jax.ShapeDtypeStruct((own_nodes, hidden), bf16),
                jax.ShapeDtypeStruct((PANEL, features, TILE), bf16),
            ],
            in_specs=[node_spec] * 9
            + [weight_spec, weight_spec, pl.BlockSpec((1, hidden), lambda i: (0, 0)), hid_spec],
            out_specs=[hid_spec, node_spec, hid_spec, piece_spec],
            compiler_params=pltpu.CompilerParams(vmem_limit_bytes=VMEM_BYTES),
            name="dense",
        )(
            partial[0],
            *received,
            node_features,
            weight_self,
            weight_neigh,
            bias_vector.reshape(1, hidden),
            grad_output,
        )

    with jax.named_scope("gather_gradients"):
        grads = gather_ring(back, from_narrow)

    with jax.named_scope("weight_gradients"):
        slices = jax.ShapeDtypeStruct((Z, SLICE + 8, hidden), f32)
        far, near, self_term = pl.pallas_call(
            lambda *refs: weight_kernel(scale, *refs),
            out_shape=[slices, slices, jax.ShapeDtypeStruct((own_nodes, features), f32)],
            in_specs=[smem] + [vmem] * 4,
            out_specs=[vmem] * 3,
            compiler_params=pltpu.CompilerParams(vmem_limit_bytes=VMEM_BYTES),
            cost_estimate=pl.CostEstimate(
                flops=6 * own_nodes * features * hidden,
                bytes_accessed=2 * 1024 * 1024,
                transcendentals=0,
            ),
            name="weight_gradients",
        )(meta, node_features, own_agg, grad_pre, weight_self)
        near = near + from_narrow(far, 1, 0)
        part = near[0] + sum(from_narrow(near[dz], 0, -dz & 3) for dz in (1, 2, 3))
        grads[-1], part = lax.optimization_barrier((grads[-1], part))
        part = part + sum(from_wide(part, dx, 0, dc) for dx, dc in ((0, 1), (1, 0), (1, 1)))
        part = part + sum(from_wide(part, 0, dy, 0) for dy in (1, 2, 3))

    with jax.named_scope("column_gradients"):
        pieces = jax.ShapeDtypeStruct((8, PANEL, features, TILE), bf16)
        swap, keep = pl.pallas_call(
            backward_kernel,
            out_shape=[pieces, pieces],
            in_specs=[smem] * 4 + [hbm] * 9,
            out_specs=[vmem] * 2,
            scratch_shapes=[
                pltpu.VMEM((row_tiles + 1, features, TILE), bf16),
                pltpu.VMEM((slots + 1, TILE, TILE), bf16),
                pltpu.VMEM((col_tiles + 1, features, TILE), f32),
                pltpu.SemaphoreType.DMA((8,)),
                pltpu.SemaphoreType.DMA((slots // CHUNK,)),
            ],
            compiler_params=pltpu.CompilerParams(vmem_limit_bytes=VMEM_BYTES),
            cost_estimate=tile_dots,
            name="column_gradients",
        )(meta, cols, pairs, total, tile_values, *grads)

    with jax.named_scope("scatter_gradients"):
        swapped = from_wide(swap, 0, 0, 1)
        column = []
        for k, (dx, dy) in enumerate(RELATIVE):
            if k > 0:
                pair = (keep[k].astype(f32) + swapped[k].astype(f32)).astype(bf16)
                column.append(from_wide(pair, dx, -dy & 3, 0))

    with jax.named_scope("spread_weight_gradients"):
        quarters = [part] + [from_narrow(part, 0, dz) for dz in (1, 2, 3)]
        other = from_narrow(jnp.stack(quarters), 1, 0)
        grad_self, grad_neigh, grad_bias = pl.pallas_call(
            assemble_kernel,
            out_shape=[
                jax.ShapeDtypeStruct((features, hidden), f32),
                jax.ShapeDtypeStruct((features, hidden), f32),
                jax.ShapeDtypeStruct((1, hidden), f32),
            ],
            in_specs=[smem] + [vmem] * 5,
            out_specs=[vmem] * 3,
            name="assemble",
        )(meta, *quarters, other)

    with jax.named_scope("grad_input"):
        first_spec = pl.BlockSpec((1, block // TILE, features, TILE), lambda i: (0, i, 0, 0))
        grad_input = pl.pallas_call(
            final_kernel,
            grid=(own_nodes // block,),
            out_shape=jax.ShapeDtypeStruct((own_nodes, features), bf16),
            in_specs=[first_spec] * 2 + [piece_spec] * 7 + [node_spec],
            out_specs=node_spec,
            compiler_params=pltpu.CompilerParams(vmem_limit_bytes=VMEM_BYTES),
            name="grad_input",
        )(keep, swapped, *column, self_term)
    return (output, grad_input, grad_self, grad_neigh, grad_bias[0])


def solution(mesh):
    placed = (
        P(("wide", "narrow"), None),
        P(("wide", "narrow"), None, None),
        P(("wide", "narrow")),
        P(("wide", "narrow")),
        P(("wide", "narrow")),
        P(),
        P(),
        P(),
        P(("wide", "narrow"), None),
    )
    return jax.shard_map(
        local,
        mesh=mesh,
        in_specs=placed,
        out_specs=(P(("wide", "narrow"), None), P(("wide", "narrow"), None), P(), P(), P()),
        check_vma=False,
    )
```

time: 537 us -> 196 us (0.36)
  matrix products: 122 us -> 0 us
  local copies, waits for them, and re-layouts: 108 us -> 2.93 us
  waiting for transfers between devices: 176 us -> 72.5 us
  starting transfers between devices: 0.38 us -> 83.4 us
  blocking collectives: 66.4 us -> 0 us
  other arithmetic: 48.8 us -> 5.69 us
  Pallas kernels: 0 us -> 29.2 us
  between operations: 14.5 us -> 1.75 us
    dot_general x14 -> x0, matrix products: 122 us -> none  [the longest x2 49.8 us: tile_products(): jnp.einsum(pattern, values, picked, preferred_element_type=jnp.float32)]
    all_gather x2 -> x0, waiting for transfers between devices: 90.8 us -> none  [the longest x1 49.9 us: local(): stripe_grad = lax.all_gather(grad_agg, 'narrow', axis=0, tiled=True)]
    reduce_scatter x2 -> x0, waiting for transfers between devices: 84 us -> none  [the longest x1 74.9 us: local(): lax.psum_scatter(partial_agg.astype(jnp.bfloat16), 'narrow', scatter_dime...]
    ppermute x0 -> x51, starting transfers between devices: none -> 83.4 us  [the longest x22 45.1 us: from_narrow(): lax.ppermute(x, 'narrow', [(narrow_index(n, dx, dz), n) for n in range(8)])]
    ppermute x0 -> x51, waiting for transfers between devices: none -> 72.5 us  [the longest x22 40.2 us: from_narrow(): lax.ppermute(x, 'narrow', [(narrow_index(n, dx, dz), n) for n in range(8)])]
    dot_general x2 -> x0, local copies, waits for them, and re-layouts: 69.6 us -> none  [tile_products(): jnp.einsum(pattern, values, picked, preferred_element_type=jnp.float32)]
    psum x1 -> x0, blocking collectives: 66.4 us -> none  [local(): lax.psum((local_terms[0], local_terms[1], local_terms[2]), ('wide', 'narr...]
    convert_element_type x2 -> x1, other arithmetic: 47.2 us -> 2.83 us  [local(): pair = (keep[k].astype(f32) + swapped[k].astype(f32)).astype(bf16)]
  transfers between devices with their start and end apart: 5 -> 51, of which waited for: 4 -> 23; matrix products, arithmetic and copies ran while one was open for 26% -> 3% of each run, Pallas kernels for 0% -> 3%
where the time goes in v1:
time: 196 us
  starting transfers between devices  83.4 us (43%)
  waiting for transfers between devices  72.5 us (37%)
  Pallas kernels  29.2 us (15%)
  other arithmetic  5.69 us (3%)
  local copies, waits for them, and re-layouts  2.93 us (1%)
    ppermute x22, starting transfers between devices, from_narrow(): lax.ppermute(x, 'narrow', [(narrow_index(n, dx, dz), n) for n in range(8)])  45.1 us
    ppermute x22, waiting for transfers between devices, from_narrow(): lax.ppermute(x, 'narrow', [(narrow_index(n, dx, dz), n) for n in range(8)])  40.2 us
    ppermute x29, starting transfers between devices, from_wide(): lax.ppermute(x, 'wide', [(wide_index(w, dx, dy, dc), w) for w in range(16)])  38.3 us
    ppermute x29, waiting for transfers between devices, from_wide(): lax.ppermute(x, 'wide', [(wide_index(w, dx, dy, dc), w) for w in range(16)])  32.3 us
    pallas_call x1, Pallas kernels, local(): pl.pallas_call(backward_kernel, out_shape=[pieces, pieces], in_specs=[sme...  8.41 us
    pallas_call x1, Pallas kernels, local(): pl.pallas_call(forward_kernel, out_shape=[jax.ShapeDtypeStruct((own_nodes...  8.16 us
  transfers between devices with their start and end apart: 51, of which 23 were waited for; matrix products, arithmetic and copies ran while one was open for 3% of the time, Pallas kernels for 3%

profile of v1, /device:TPU:0, one launch (start us, length us, event | category | flops | bytes accessed | tf_op | source)
XLA Modules:
  0.0 195.5 jit_solution(10814961636562720127)
XLA Ops:
  0.6 3.2 %collective-permute-start = (bf16[1024,128]{1,0:T(8,128)(2,1)}, bf16[1024,128]{1,0:T(8,128)(2,1)S(1)}, u32[]{:S(2)}, u32[]{:S(2)}) collective-permute-start(bf16[1024,128]{1,0:T(8,128)(2,1)} %refs_1_.1), channel_id=1, source_target_pairs={{16,0},{24,8},{32,16},{40,24},{48,32},{56,40},{0,48},{8,56},{80,64... | collective-permute-start | bytes 786440 | tf_op jit(solution)/shard_map/gather_features/ppermute | solution.py:29
  3.8 1.5 collective-permute-start.3
  5.3 4.4 %collective-permute-done.refs_1_ = bf16[1024,128]{1,0:T(8,128)(2,1)S(1)} collective-permute-done((bf16[1024,128]{1,0:T(8,128)(2,1)}, bf16[1024,128]{1,0:T(8,128)(2,1)S(1)}, u32[]{:S(2)}, u32[]{:S(2)}) %collective-permute-start) | collective-permute-done | bytes 262176 | tf_op jit(solution)/shard_map/gather_features/ppermute | solution.py:29
  9.7 3.6 %collective-permute-start.1 = (bf16[1024,128]{1,0:T(8,128)(2,1)S(1)}, bf16[1024,128]{1,0:T(8,128)(2,1)S(1)}, u32[]{:S(2)}, u32[]{:S(2)}) collective-permute-start(bf16[1024,128]{1,0:T(8,128)(2,1)S(1)} %collective-permute-done.refs_1_), channel_id=1, source_target_pairs={{16,0},{24,8},{32,16},{40,24},{48,32},{56,40},{0,48},{8,56},{80,64... | collective-permute-start | bytes 786440 | tf_op jit(solution)/shard_map/gather_features/ppermute | solution.py:29
  13.4 1.9 collective-permute-start.6
  15.8 4.2 %collective-permute-done.1.refs_2_ = bf16[1024,128]{1,0:T(8,128)(2,1)S(1)} collective-permute-done((bf16[1024,128]{1,0:T(8,128)(2,1)S(1)}, bf16[1024,128]{1,0:T(8,128)(2,1)S(1)}, u32[]{:S(2)}, u32[]{:S(2)}) %collective-permute-start.1) | collective-permute-done | bytes 262176 | tf_op jit(solution)/shard_map/gather_features/ppermute | solution.py:29
  20.0 1.5 collective-permute-start.5
  21.5 2.1 %collective-permute-done.4.refs_5_ = bf16[1024,128]{1,0:T(8,128)(2,1)S(1)} collective-permute-done((bf16[1024,128]{1,0:T(8,128)(2,1)S(1)}, bf16[1024,128]{1,0:T(8,128)(2,1)S(1)}, u32[]{:S(2)}, u32[]{:S(2)}) %collective-permute-start.4) | collective-permute-done | bytes 262176 | tf_op jit(solution)/shard_map/gather_features/ppermute | solution.py:29
  24.6 1.8 collective-permute-done.5.refs_6_
  27.1 0.6 pad_add_fusion.1.meta.refs_0_
  27.6 2.2 %plan.1 = (s32[3,320]{1,0:T(4,128)}, s32[1]{0:T(128)}) custom-call(s32[4]{0:T(128)} %pad_add_fusion.1.meta.refs_0_, s32[512]{0:T(512)} %rows.1), custom_call_target="tpu_custom_call" | custom-call | tf_op jit(solution)/shard_map/plan/plan/pallas_call | solution.py:294
  29.8 1.3 pad_add_fusion.cols
  32.0 8.2 %aggregate.1 = (bf16[1024,128]{1,0:T(8,128)(2,1)}, bf16[1024,128]{1,0:T(8,128)(2,1)}, bf16[1024,128]{1,0:T(8,128)(2,1)}, bf16[1024,128]{1,0:T(8,128)(2,1)}, bf16...) custom-call(s32[4]{0:T(128)} %pad_add_fusion.1.meta.refs_0_, ...), custom_call_target="tpu_custom_call" | custom-call | flops 2147483648 | bytes 23068672 | tf_op jit(solution)/shard_map/aggregate/aggregate/pallas_call | solution.py:306
  40.2 5.4 %collective-permute-start.15 = (bf16[1024,128]{1,0:T(8,128)(2,1)}, bf16[1024,128]{1,0:T(8,128)(2,1)S(1)}, u32[]{:S(2)}, u32[]{:S(2)}) collective-permute-start(bf16[1024,128]{1,0:T(8,128)(2,1)} %get-tuple-element.32), channel_id=1, source_target_pairs={{3,0},{0,1},{1,2},{2,3},{7,4},{4,5},{5,6},{6,7},{11,8},{8,9},{9,10... | collective-permute-start | bytes 786440 | tf_op jit(solution)/shard_map/scatter_aggregate/ppermute | solution.py:33
  45.6 8.6 %collective-permute-start.16 = (bf16[1024,128]{1,0:T(8,128)(2,1)}, bf16[1024,128]{1,0:T(8,128)(2,1)S(1)}, u32[]{:S(2)}, u32[]{:S(2)}) collective-permute-start(bf16[1024,128]{1,0:T(8,128)(2,1)} %get-tuple-element.33), channel_id=1, source_target_pairs={{2,0},{3,1},{0,2},{1,3},{6,4},{7,5},{4,6},{5,7},{10,8},{11,9},{8,1... | collective-permute-start | bytes 786440 | tf_op jit(solution)/shard_map/scatter_aggregate/ppermute | solution.py:33
  54.2 5.0 %collective-permute-start.19 = (bf16[1024,128]{1,0:T(8,128)(2,1)}, bf16[1024,128]{1,0:T(8,128)(2,1)S(1)}, u32[]{:S(2)}, u32[]{:S(2)}) collective-permute-start(bf16[1024,128]{1,0:T(8,128)(2,1)} %get-tuple-element.36), channel_id=1, source_target_pairs={{7,0},{4,1},{5,2},{6,3},{3,4},{0,5},{1,6},{2,7},{15,8},{12,9},{13,... | collective-permute-start | bytes 786440 | tf_op jit(solution)/shard_map/scatter_aggregate/ppermute | solution.py:33
  59.2 2.4 %collective-permute-done.16.r2 = bf16[1024,128]{1,0:T(8,128)(2,1)S(1)} collective-permute-done((bf16[1024,128]{1,0:T(8,128)(2,1)}, bf16[1024,128]{1,0:T(8,128)(2,1)S(1)}, u32[]{:S(2)}, u32[]{:S(2)}) %collective-permute-start.16) | collective-permute-done | bytes 262176 | tf_op jit(solution)/shard_map/scatter_aggregate/ppermute | solution.py:33
  61.6 2.2 %collective-permute-start.21 = (bf16[1024,128]{1,0:T(8,128)(2,1)}, bf16[1024,128]{1,0:T(8,128)(2,1)S(1)}, u32[]{:S(2)}, u32[]{:S(2)}) collective-permute-start(bf16[1024,128]{1,0:T(8,128)(2,1)} %get-tuple-element.38), channel_id=1, source_target_pairs={{5,0},{6,1},{7,2},{4,3},{1,4},{2,5},{3,6},{0,7},{13,8},{14,9},{15,... | collective-permute-start | bytes 786440 | tf_op jit(solution)/shard_map/scatter_aggregate/ppermute | solution.py:33
  63.8 5.9 %collective-permute-done.19.r5 = bf16[1024,128]{1,0:T(8,128)(2,1)S(1)} collective-permute-done((bf16[1024,128]{1,0:T(8,128)(2,1)}, bf16[1024,128]{1,0:T(8,128)(2,1)S(1)}, u32[]{:S(2)}, u32[]{:S(2)}) %collective-permute-start.19) | collective-permute-done | bytes 262176 | tf_op jit(solution)/shard_map/scatter_aggregate/ppermute | solution.py:33
  69.8 7.5 %collective-permute-done.20.r6 = bf16[1024,128]{1,0:T(8,128)(2,1)S(1)} collective-permute-done((bf16[1024,128]{1,0:T(8,128)(2,1)}, bf16[1024,128]{1,0:T(8,128)(2,1)S(1)}, u32[]{:S(2)}, u32[]{:S(2)}) %collective-permute-start.20) | collective-permute-done | bytes 262176 | tf_op jit(solution)/shard_map/scatter_aggregate/ppermute | solution.py:33
  77.3 5.1 %collective-permute-done.21.r7 = bf16[1024,128]{1,0:T(8,128)(2,1)S(1)} collective-permute-done((bf16[1024,128]{1,0:T(8,128)(2,1)}, bf16[1024,128]{1,0:T(8,128)(2,1)S(1)}, u32[]{:S(2)}, u32[]{:S(2)}) %collective-permute-start.21) | collective-permute-done | bytes 262176 | tf_op jit(solution)/shard_map/scatter_aggregate/ppermute | solution.py:33
  82.4 0.7 copy-done.28
  83.1 3.5 %dense.1 = (bf16[1024,256]{1,0:T(8,128)(2,1)}, bf16[1024,128]{1,0:T(8,128)(2,1)}, bf16[1024,256]{1,0:T(8,128)(2,1)}, bf16[8,128,128]{2,1,0:T(8,128)(2,1)}) custom-call(bf16[1024,128]{1,0:T(8,128)(2,1)} %get-tuple-element.31.own, bf16[1024,128]{1,0:T(8,128)(2,1)} %copy-done.22, bf16[1024,128]{1,0:T(8,128)(2,1)} %copy-done.23, bf16[1024,128]{1,0:T(8,128)(2,1)} %copy-done.24, ...), custom_call_target="tpu_custom_call" | custom-call | tf_op jit(solution)/shard_map/dense/dense/pallas_call | solution.py:336
  86.6 1.5 collective-permute-start.22
  88.0 2.5 %weight_gradients.1 = (f32[4,40,256]{2,1,0:T(8,128)}, f32[4,40,256]{2,1,0:T(8,128)}, f32[1024,128]{1,0:T(8,128)}) custom-call(s32[4]{0:T(128)} %pad_add_fusion.1.meta.refs_0_, bf16[1024,128]{1,0:T(8,128)(2,1)} %refs_1_.1, bf16[1024,128]{1,0:T(8,128)(2,1)} %get-tuple-element.41.refs_2_, bf16[1024,256]{1,0:T(8,128)(2,1)} %get-tuple-element.42.refs_3_, ...), custom_call_target="tpu_custom_call" | custom-call | flops 201326592 | bytes 2097152 | tf_op jit(solution)/shard_map/weight_gradients/weight_gradients/pallas_call | solution.py:365
  90.7 3.4 %collective-permute-start.25 = (bf16[8,128,128]{2,1,0:T(8,128)(2,1)}, bf16[8,128,128]{2,1,0:T(8,128)(2,1)S(1)}, u32[]{:S(2)}, u32[]{:S(2)}) collective-permute-start(bf16[8,128,128]{2,1,0:T(8,128)(2,1)} %get-tuple-element.40.refs_0_), channel_id=1, source_target_pairs={{4,0},{5,1},{6,2},{7,3},{0,4},{1,5},{2,6},{3,7},{12,8},{13,9},{14,... | collective-permute-start | bytes 786440 | tf_op jit(solution)/shard_map/gather_gradients/ppermute | solution.py:33
  94.1 5.3 %collective-permute-done.29 = f32[4,40,256]{2,1,0:T(8,128)S(1)} collective-permute-done((f32[4,40,256]{2,1,0:T(8,128)}, f32[4,40,256]{2,1,0:T(8,128)S(1)}, u32[]{:S(2)}, u32[]{:S(2)}) %collective-permute-start.29) | collective-permute-done | bytes 163872 | tf_op jit(solution)/shard_map/weight_gradients/ppermute | solution.py:33
  99.3 0.9 add.58
  100.4 1.8 collective-permute-start.32
  102.5 2.7 %collective-permute-start.31 = (f32[40,256]{1,0:T(8,128)S(1)}, f32[40,256]{1,0:T(8,128)S(1)}, u32[]{:S(2)}, u32[]{:S(2)}) collective-permute-start(f32[40,256]{1,0:T(8,128)S(1)} %get-tuple-element.60), channel_id=1, source_target_pairs={{2,0},{3,1},{0,2},{1,3},{6,4},{7,5},{4,6},{5,7},{10,8},{11,9},{8,1... | collective-permute-start | bytes 122888 | tf_op jit(solution)/shard_map/weight_gradients/ppermute | solution.py:33
  105.2 1.0 collective-permute-start.28
  106.3 3.4 %collective-permute-done.32 = f32[40,256]{1,0:T(8,128)S(1)} collective-permute-done((f32[40,256]{1,0:T(8,128)S(1)}, f32[40,256]{1,0:T(8,128)S(1)}, u32[]{:S(2)}, u32[]{:S(2)}) %collective-permute-start.32) | collective-permute-done | bytes 40992 | tf_op jit(solution)/shard_map/weight_gradients/ppermute | solution.py:33
  109.7 3.2 %collective-permute-start.26 = (bf16[8,128,128]{2,1,0:T(8,128)(2,1)S(1)}, bf16[8,128,128]{2,1,0:T(8,128)(2,1)S(1)}, u32[]{:S(2)}, u32[]{:S(2)}) collective-permute-start(bf16[8,128,128]{2,1,0:T(8,128)(2,1)S(1)} %collective-permute-done.25.refs_4_), channel_id=1, source_target_pairs={{1,0},{2,1},{3,2},{0,3},{5,4},{6,5},{7,6},{4,7},{9,8},{10,9},{11,1... | collective-permute-start | bytes 786440 | tf_op jit(solution)/shard_map/gather_gradients/ppermute | solution.py:33
  113.3 2.4 %collective-permute-done.28.refs_7_ = bf16[8,128,128]{2,1,0:T(8,128)(2,1)S(1)} collective-permute-done((bf16[8,128,128]{2,1,0:T(8,128)(2,1)S(1)}, bf16[8,128,128]{2,1,0:T(8,128)(2,1)S(1)}, u32[]{:S(2)}, u32[]{:S(2)}) %collective-permute-start.28) | collective-permute-done | bytes 262176 | tf_op jit(solution)/shard_map/gather_gradients/ppermute | solution.py:33
  115.7 4.1 %collective-permute-done.24.refs_3_ = bf16[8,128,128]{2,1,0:T(8,128)(2,1)S(1)} collective-permute-done((bf16[8,128,128]{2,1,0:T(8,128)(2,1)}, bf16[8,128,128]{2,1,0:T(8,128)(2,1)S(1)}, u32[]{:S(2)}, u32[]{:S(2)}) %collective-permute-start.24) | collective-permute-done | bytes 262176 | tf_op jit(solution)/shard_map/gather_gradients/ppermute | solution.py:33
  119.8 1.0 collective-permute-done.27.refs_6_
  120.9 0.7 copy-done.21
  121.5 8.4 %column_gradients.1 = (bf16[8,8,128,128]{3,2,1,0:T(8,128)(2,1)}, bf16[8,8,128,128]{3,2,1,0:T(8,128)(2,1)}) custom-call(s32[4]{0:T(128)} %pad_add_fusion.1.meta.refs_0_, s32[513]{0:T(1024)} %pad_add_fusion.cols, s32[3,320]{1,0:T(4,128)} %get-tuple-element.29.pairs, s32[1]{0:T(128)} %get-tuple-element.30.total, bf16[512,128,128]{2,1,0:T(8,128)(2,1)} %tiles_hbm.3, ...), custom_call_target="tpu_custom_call" | custom-call | flops 2147483648 | bytes 23068672 | tf_op jit(solution)/shard_map/column_gradients/column_gradients/pallas_call | solution.py:386
  130.1 1.0 collective-permute-start.43
  131.1 1.1 collective-permute-start.42
  132.3 1.3 collective-permute-done.43
  133.6 0.7 collective-permute-done.41
  134.3 0.9 collective-permute-done.42
  135.2 11.1 %collective-permute-start.44 = (f32[40,256]{1,0:T(8,128)S(1)}, f32[40,256]{1,0:T(8,128)S(1)}, u32[]{:S(2)}, u32[]{:S(2)}) collective-permute-start(f32[40,256]{1,0:T(8,128)S(1)} %add_add_fusion.1), channel_id=1, source_target_pairs={{16,0},{24,8},{32,16},{40,24},{48,32},{56,40},{0,48},{8,56},{80,64... | collective-permute-start | bytes 122888 | tf_op jit(solution)/shard_map/weight_gradients/ppermute | solution.py:29
  146.3 2.2 %collective-permute-start.45 = (f32[40,256]{1,0:T(8,128)S(1)}, f32[40,256]{1,0:T(8,128)S(1)}, u32[]{:S(2)}, u32[]{:S(2)}) collective-permute-start(f32[40,256]{1,0:T(8,128)S(1)} %add_add_fusion.1), channel_id=1, source_target_pairs={{32,0},{40,8},{48,16},{56,24},{0,32},{8,40},{16,48},{24,56},{96,64... | collective-permute-start | bytes 122888 | tf_op jit(solution)/shard_map/weight_gradients/ppermute | solution.py:29
  148.5 3.3 %collective-permute-done.45 = f32[40,256]{1,0:T(8,128)S(1)} collective-permute-done((f32[40,256]{1,0:T(8,128)S(1)}, f32[40,256]{1,0:T(8,128)S(1)}, u32[]{:S(2)}, u32[]{:S(2)}) %collective-permute-start.45) | collective-permute-done | bytes 40992 | tf_op jit(solution)/shard_map/weight_gradients/ppermute | solution.py:29
  152.4 1.9 collective-permute-start.48
  154.3 1.3 collective-permute-start.49
  155.6 2.8 %fusion.6 = (bf16[8,128,128]{2,1,0:T(8,128)(2,1)S(1)}, bf16[8,128,128]{2,1,0:T(8,128)(2,1)S(1)}, bf16[8,128,128]{2,1,0:T(8,128)(2,1)S(1)}, bf16[8,128,128]{2,1,0...) fusion(bf16[8,8,128,128]{3,2,1,0:T(8,128)(2,1)S(1)} %collective, ...), kind=kLoop, calls=%fused_computation.13 | loop fusion | flops 3670016 | bytes 5505024 | tf_op jit(solution)/shard_map/scatter_gradients/convert_element_type | solution.py:408
  158.5 3.4 %collective-permute-start.35 = (bf16[8,128,128]{2,1,0:T(8,128)(2,1)S(1)}, bf16[8,128,128]{2,1,0:T(8,128)(2,1)S(1)}, u32[]{:S(2)}, u32[]{:S(2)}) collective-permute-start(bf16[8,128,128]{2,1,0:T(8,128)(2,1)S(1)} %get-tuple-element.58), channel_id=1, source_target_pairs={{32,0},{40,8},{48,16},{56,24},{0,32},{8,40},{16,48},{24,56},{96,64... | collective-permute-start | bytes 786440 | tf_op jit(solution)/shard_map/scatter_gradients/ppermute | solution.py:29
  162.0 5.6 %collective-permute-start.50 = (f32[4,40,256]{2,1,0:T(8,128)S(1)}, f32[4,40,256]{2,1,0:T(8,128)S(1)}, u32[]{:S(2)}, u32[]{:S(2)}) collective-permute-start(f32[4,40,256]{2,1,0:T(8,128)S(1)} %pad_maximum_fusion), channel_id=1, source_target_pairs={{4,0},{5,1},{6,2},{7,3},{0,4},{1,5},{2,6},{3,7},{12,8},{13,9},{14,... | collective-permute-start | bytes 491528 | tf_op jit(solution)/shard_map/spread_weight_gradients/ppermute | solution.py:33
  167.6 0.8 collective-permute-start.36
  168.4 0.8 collective-permute-start.37
  169.2 3.1 %collective-permute-done.50.other = f32[4,40,256]{2,1,0:T(8,128)S(1)} collective-permute-done((f32[4,40,256]{2,1,0:T(8,128)S(1)}, f32[4,40,256]{2,1,0:T(8,128)S(1)}, u32[]{:S(2)}, u32[]{:S(2)}) %collective-permute-start.50) | collective-permute-done | bytes 163872 | tf_op jit(solution)/shard_map/spread_weight_gradients/ppermute | solution.py:33
  172.3 1.0 collective-permute-start.38
  173.3 1.6 collective-permute-start.39
  174.9 1.8 collective-permute-start.40
  176.7 1.8 assemble.1
  178.5 0.6 collective-permute-done.37.r4
  179.1 4.8 %collective-permute-done.38.r5 = bf16[8,128,128]{2,1,0:T(8,128)(2,1)S(1)} collective-permute-done((bf16[8,128,128]{2,1,0:T(8,128)(2,1)S(1)}, bf16[8,128,128]{2,1,0:T(8,128)(2,1)S(1)}, u32[]{:S(2)}, u32[]{:S(2)}) %collective-permute-start.38) | collective-permute-done | bytes 262176 | tf_op jit(solution)/shard_map/scatter_gradients/ppermute | solution.py:29
  183.9 6.3 %collective-permute-done.39.r6 = bf16[8,128,128]{2,1,0:T(8,128)(2,1)S(1)} collective-permute-done((bf16[8,128,128]{2,1,0:T(8,128)(2,1)S(1)}, bf16[8,128,128]{2,1,0:T(8,128)(2,1)S(1)}, u32[]{:S(2)}, u32[]{:S(2)}) %collective-permute-start.39) | collective-permute-done | bytes 262176 | tf_op jit(solution)/shard_map/scatter_gradients/ppermute | solution.py:29
  190.2 1.8 collective-permute-done.40.r7
  192.1 0.7 copy-done.35
  192.8 2.7 %grad_input.1 = bf16[1024,128]{1,0:T(8,128)(2,1)} custom-call(bf16[8,8,128,128]{3,2,1,0:T(8,128)(2,1)} %get-tuple-element.46.keep, bf16[8,8,128,128]{3,2,1,0:T(8,128)(2,1)} %copy-done, bf16[8,128,128]{2,1,0:T(8,128)(2,1)} %copy-done.29, bf16[8,128,128]{2,1,0:T(8,128)(2,1)} %copy-done.30, bf16[8,128,128]{2,1,0:T(8,128)(2,1)} %copy-done.31, ...), custom_call_target="tpu_custom_call" | custom-call | tf_op jit(solution)/shard_map/grad_input/grad_input/pallas_call | solution.py:428
  (134 shorter events, 4.5 us)
Async XLA Ops:
  0.6 9.0 %collective-permute-start = (bf16[1024,128]{1,0:T(8,128)(2,1)}, bf16[1024,128]{1,0:T(8,128)(2,1)S(1)}, u32[]{:S(2)}, u32[]{:S(2)}) collective-permute-start(bf16[1024,128]{1,0:T(8,128)(2,1)} %refs_1_.1), channel_id=1, source_target_pairs={{16,0},{24,8},{32,16},{40,24},{48,32},{56,40},{0,48},{8,56},{80,64... | collective-permute-start | bytes 786440 | tf_op jit(solution)/shard_map/gather_features/ppermute | solution.py:29
  3.8 9.5 %collective-permute-start.3 = (bf16[1024,128]{1,0:T(8,128)(2,1)}, bf16[1024,128]{1,0:T(8,128)(2,1)S(1)}, u32[]{:S(2)}, u32[]{:S(2)}) collective-permute-start(bf16[1024,128]{1,0:T(8,128)(2,1)} %refs_1_.1), channel_id=1, source_target_pairs={{64,0},{72,8},{80,16},{88,24},{96,32},{104,40},{112,48},{120,56},{... | collective-permute-start | bytes 786440 | tf_op jit(solution)/shard_map/gather_features/ppermute | solution.py:29
  5.3 10.0 %collective-permute-start.2 = (bf16[1024,128]{1,0:T(8,128)(2,1)}, bf16[1024,128]{1,0:T(8,128)(2,1)S(1)}, u32[]{:S(2)}, u32[]{:S(2)}) collective-permute-start(bf16[1024,128]{1,0:T(8,128)(2,1)} %refs_1_.1), channel_id=1, source_target_pairs={{48,0},{56,8},{0,16},{8,24},{16,32},{24,40},{32,48},{40,56},{112,6... | collective-permute-start | bytes 786440 | tf_op jit(solution)/shard_map/gather_features/ppermute | solution.py:29
  5.3 10.0 %collective-permute-start.7 = (bf16[1024,128]{1,0:T(8,128)(2,1)}, bf16[1024,128]{1,0:T(8,128)(2,1)S(1)}, u32[]{:S(2)}, u32[]{:S(2)}) collective-permute-start(bf16[1024,128]{1,0:T(8,128)(2,1)} %refs_1_.1), channel_id=1, source_target_pairs={{8,0},{0,8},{24,16},{16,24},{40,32},{32,40},{56,48},{48,56},{72,64... | collective-permute-start | bytes 786440 | tf_op jit(solution)/shard_map/gather_features/ppermute | solution.py:29
  9.7 21.5 %copy-start.2 = (bf16[1024,128]{1,0:T(8,128)(2,1)}, bf16[1024,128]{1,0:T(8,128)(2,1)S(1)}, u32[]{:S(2)}) copy-start(bf16[1024,128]{1,0:T(8,128)(2,1)S(1)} %collective-permute-done.refs_1_) | copy-start | bytes 786436
  9.7 10.3 %collective-permute-start.1 = (bf16[1024,128]{1,0:T(8,128)(2,1)S(1)}, bf16[1024,128]{1,0:T(8,128)(2,1)S(1)}, u32[]{:S(2)}, u32[]{:S(2)}) collective-permute-start(bf16[1024,128]{1,0:T(8,128)(2,1)S(1)} %collective-permute-done.refs_1_), channel_id=1, source_target_pairs={{16,0},{24,8},{32,16},{40,24},{48,32},{56,40},{0,48},{8,56},{80,64... | collective-permute-start | bytes 786440 | tf_op jit(solution)/shard_map/gather_features/ppermute | solution.py:29
  13.3 17.9 %copy-start.3 = (bf16[1024,128]{1,0:T(8,128)(2,1)}, bf16[1024,128]{1,0:T(8,128)(2,1)S(1)}, u32[]{:S(2)}) copy-start(bf16[1024,128]{1,0:T(8,128)(2,1)S(1)} %collective-permute-done.3.refs_4_) | copy-start | bytes 786436
  13.3 10.3 %collective-permute-start.4 = (bf16[1024,128]{1,0:T(8,128)(2,1)S(1)}, bf16[1024,128]{1,0:T(8,128)(2,1)S(1)}, u32[]{:S(2)}, u32[]{:S(2)}) collective-permute-start(bf16[1024,128]{1,0:T(8,128)(2,1)S(1)} %collective-permute-done.3.refs_4_), channel_id=1, source_target_pairs={{16,0},{24,8},{32,16},{40,24},{48,32},{56,40},{0,48},{8,56},{80,64... | collective-permute-start | bytes 786440 | tf_op jit(solution)/shard_map/gather_features/ppermute | solution.py:29
  13.4 10.2 %collective-permute-start.6 = (bf16[1024,128]{1,0:T(8,128)(2,1)S(1)}, bf16[1024,128]{1,0:T(8,128)(2,1)S(1)}, u32[]{:S(2)}, u32[]{:S(2)}) collective-permute-start(bf16[1024,128]{1,0:T(8,128)(2,1)S(1)} %collective-permute-done.3.refs_4_), channel_id=1, source_target_pairs={{48,0},{56,8},{0,16},{8,24},{16,32},{24,40},{32,48},{40,56},{112,6... | collective-permute-start | bytes 786440 | tf_op jit(solution)/shard_map/gather_features/ppermute | solution.py:29
  15.3 15.9 %copy-start.4 = (bf16[1024,128]{1,0:T(8,128)(2,1)}, bf16[1024,128]{1,0:T(8,128)(2,1)S(1)}, u32[]{:S(2)}) copy-start(bf16[1024,128]{1,0:T(8,128)(2,1)S(1)} %collective-permute-done.2.refs_3_) | copy-start | bytes 786436
  15.3 8.8 %collective-permute-start.8 = (bf16[1024,128]{1,0:T(8,128)(2,1)S(1)}, bf16[1024,128]{1,0:T(8,128)(2,1)S(1)}, u32[]{:S(2)}, u32[]{:S(2)}) collective-permute-start(bf16[1024,128]{1,0:T(8,128)(2,1)S(1)} %collective-permute-done.refs_1_), channel_id=1, source_target_pairs={{8,0},{0,8},{24,16},{16,24},{40,32},{32,40},{56,48},{48,56},{72,64... | collective-permute-start | bytes 786440 | tf_op jit(solution)/shard_map/gather_features/ppermute | solution.py:29
  15.3 15.9 %copy-start.5 = (bf16[1024,128]{1,0:T(8,128)(2,1)}, bf16[1024,128]{1,0:T(8,128)(2,1)S(1)}, u32[]{:S(2)}) copy-start(bf16[1024,128]{1,0:T(8,128)(2,1)S(1)} %collective-permute-done.7.refs_8_) | copy-start | bytes 786436
  15.3 8.9 %collective-permute-start.10 = (bf16[1024,128]{1,0:T(8,128)(2,1)S(1)}, bf16[1024,128]{1,0:T(8,128)(2,1)S(1)}, u32[]{:S(2)}, u32[]{:S(2)}) collective-permute-start(bf16[1024,128]{1,0:T(8,128)(2,1)S(1)} %collective-permute-done.2.refs_3_), channel_id=1, source_target_pairs={{8,0},{0,8},{24,16},{16,24},{40,32},{32,40},{56,48},{48,56},{72,64... | collective-permute-start | bytes 786440 | tf_op jit(solution)/shard_map/gather_features/ppermute | solution.py:29
  20.0 6.4 %collective-permute-start.5 = (bf16[1024,128]{1,0:T(8,128)(2,1)S(1)}, bf16[1024,128]{1,0:T(8,128)(2,1)S(1)}, u32[]{:S(2)}, u32[]{:S(2)}) collective-permute-start(bf16[1024,128]{1,0:T(8,128)(2,1)S(1)} %collective-permute-done.1.refs_2_), channel_id=1, source_target_pairs={{64,0},{72,8},{80,16},{88,24},{96,32},{104,40},{112,48},{120,56},{... | collective-permute-start | bytes 786440 | tf_op jit(solution)/shard_map/gather_features/ppermute | solution.py:29
  23.6 7.5 %collective-permute-start.11 = (bf16[1024,128]{1,0:T(8,128)(2,1)S(1)}, bf16[1024,128]{1,0:T(8,128)(2,1)S(1)}, u32[]{:S(2)}, u32[]{:S(2)}) collective-permute-start(bf16[1024,128]{1,0:T(8,128)(2,1)S(1)} %collective-permute-done.3.refs_4_), channel_id=1, source_target_pairs={{8,0},{0,8},{24,16},{16,24},{40,32},{32,40},{56,48},{48,56},{72,64... | collective-permute-start | bytes 786440 | tf_op jit(solution)/shard_map/gather_features/ppermute | solution.py:29
  23.6 7.5 %collective-permute-start.9 = (bf16[1024,128]{1,0:T(8,128)(2,1)S(1)}, bf16[1024,128]{1,0:T(8,128)(2,1)S(1)}, u32[]{:S(2)}, u32[]{:S(2)}) collective-permute-start(bf16[1024,128]{1,0:T(8,128)(2,1)S(1)} %collective-permute-done.1.refs_2_), channel_id=1, source_target_pairs={{8,0},{0,8},{24,16},{16,24},{40,32},{32,40},{56,48},{48,56},{72,64... | collective-permute-start | bytes 786440 | tf_op jit(solution)/shard_map/gather_features/ppermute | solution.py:29
  24.1 7.0 %collective-permute-start.12 = (bf16[1024,128]{1,0:T(8,128)(2,1)S(1)}, bf16[1024,128]{1,0:T(8,128)(2,1)S(1)}, u32[]{:S(2)}, u32[]{:S(2)}) collective-permute-start(bf16[1024,128]{1,0:T(8,128)(2,1)S(1)} %collective-permute-done.4.refs_5_), channel_id=1, source_target_pairs={{8,0},{0,8},{24,16},{16,24},{40,32},{32,40},{56,48},{48,56},{72,64... | collective-permute-start | bytes 786440 | tf_op jit(solution)/shard_map/gather_features/ppermute | solution.py:29
  24.2 7.0 %collective-permute-start.14 = (bf16[1024,128]{1,0:T(8,128)(2,1)S(1)}, bf16[1024,128]{1,0:T(8,128)(2,1)}, u32[]{:S(2)}, u32[]{:S(2)}) collective-permute-start(bf16[1024,128]{1,0:T(8,128)(2,1)S(1)} %collective-permute-done.6.refs_7_), channel_id=1, source_target_pairs={{8,0},{0,8},{24,16},{16,24},{40,32},{32,40},{56,48},{48,56},{72,64... | collective-permute-start | bytes 786440 | tf_op jit(solution)/shard_map/gather_features/ppermute | solution.py:29
  26.4 4.8 %collective-permute-start.13 = (bf16[1024,128]{1,0:T(8,128)(2,1)S(1)}, bf16[1024,128]{1,0:T(8,128)(2,1)}, u32[]{:S(2)}, u32[]{:S(2)}) collective-permute-start(bf16[1024,128]{1,0:T(8,128)(2,1)S(1)} %collective-permute-done.5.refs_6_), channel_id=1, source_target_pairs={{8,0},{0,8},{24,16},{16,24},{40,32},{32,40},{56,48},{48,56},{72,64... | collective-permute-start | bytes 786440 | tf_op jit(solution)/shard_map/gather_features/ppermute | solution.py:29
  40.2 19.0 %collective-permute-start.15 = (bf16[1024,128]{1,0:T(8,128)(2,1)}, bf16[1024,128]{1,0:T(8,128)(2,1)S(1)}, u32[]{:S(2)}, u32[]{:S(2)}) collective-permute-start(bf16[1024,128]{1,0:T(8,128)(2,1)} %get-tuple-element.32), channel_id=1, source_target_pairs={{3,0},{0,1},{1,2},{2,3},{7,4},{4,5},{5,6},{6,7},{11,8},{8,9},{9,10... | collective-permute-start | bytes 786440 | tf_op jit(solution)/shard_map/scatter_aggregate/ppermute | solution.py:33
  45.6 16.0 %collective-permute-start.16 = (bf16[1024,128]{1,0:T(8,128)(2,1)}, bf16[1024,128]{1,0:T(8,128)(2,1)S(1)}, u32[]{:S(2)}, u32[]{:S(2)}) collective-permute-start(bf16[1024,128]{1,0:T(8,128)(2,1)} %get-tuple-element.33), channel_id=1, source_target_pairs={{2,0},{3,1},{0,2},{1,3},{6,4},{7,5},{4,6},{5,7},{10,8},{11,9},{8,1... | collective-permute-start | bytes 786440 | tf_op jit(solution)/shard_map/scatter_aggregate/ppermute | solution.py:33
  54.2 9.6 %collective-permute-start.17 = (bf16[1024,128]{1,0:T(8,128)(2,1)}, bf16[1024,128]{1,0:T(8,128)(2,1)S(1)}, u32[]{:S(2)}, u32[]{:S(2)}) collective-permute-start(bf16[1024,128]{1,0:T(8,128)(2,1)} %get-tuple-element.34), channel_id=1, source_target_pairs={{1,0},{2,1},{3,2},{0,3},{5,4},{6,5},{7,6},{4,7},{9,8},{10,9},{11,1... | collective-permute-start | bytes 786440 | tf_op jit(solution)/shard_map/scatter_aggregate/ppermute | solution.py:33
  54.2 9.6 %collective-permute-start.18 = (bf16[1024,128]{1,0:T(8,128)(2,1)}, bf16[1024,128]{1,0:T(8,128)(2,1)S(1)}, u32[]{:S(2)}, u32[]{:S(2)}) collective-permute-start(bf16[1024,128]{1,0:T(8,128)(2,1)} %get-tuple-element.35), channel_id=1, source_target_pairs={{4,0},{5,1},{6,2},{7,3},{0,4},{1,5},{2,6},{3,7},{12,8},{13,9},{14,... | collective-permute-start | bytes 786440 | tf_op jit(solution)/shard_map/scatter_aggregate/ppermute | solution.py:33
  54.2 15.6 %collective-permute-start.19 = (bf16[1024,128]{1,0:T(8,128)(2,1)}, bf16[1024,128]{1,0:T(8,128)(2,1)S(1)}, u32[]{:S(2)}, u32[]{:S(2)}) collective-permute-start(bf16[1024,128]{1,0:T(8,128)(2,1)} %get-tuple-element.36), channel_id=1, source_target_pairs={{7,0},{4,1},{5,2},{6,3},{3,4},{0,5},{1,6},{2,7},{15,8},{12,9},{13,... | collective-permute-start | bytes 786440 | tf_op jit(solution)/shard_map/scatter_aggregate/ppermute | solution.py:33
  59.2 23.2 %copy-start.22 = (bf16[1024,128]{1,0:T(8,128)(2,1)}, bf16[1024,128]{1,0:T(8,128)(2,1)S(1)}, u32[]{:S(2)}) copy-start(bf16[1024,128]{1,0:T(8,128)(2,1)S(1)} %collective-permute-done.15.r1) | copy-start | bytes 786436
  59.2 18.1 %collective-permute-start.20 = (bf16[1024,128]{1,0:T(8,128)(2,1)}, bf16[1024,128]{1,0:T(8,128)(2,1)S(1)}, u32[]{:S(2)}, u32[]{:S(2)}) collective-permute-start(bf16[1024,128]{1,0:T(8,128)(2,1)} %get-tuple-element.37), channel_id=1, source_target_pairs={{6,0},{7,1},{4,2},{5,3},{2,4},{3,5},{0,6},{1,7},{14,8},{15,9},{12,... | collective-permute-start | bytes 786440 | tf_op jit(solution)/shard_map/scatter_aggregate/ppermute | solution.py:33
  61.6 20.8 %copy-start.23 = (bf16[1024,128]{1,0:T(8,128)(2,1)}, bf16[1024,128]{1,0:T(8,128)(2,1)S(1)}, u32[]{:S(2)}) copy-start(bf16[1024,128]{1,0:T(8,128)(2,1)S(1)} %collective-permute-done.16.r2) | copy-start | bytes 786436
  61.6 20.8 %collective-permute-start.21 = (bf16[1024,128]{1,0:T(8,128)(2,1)}, bf16[1024,128]{1,0:T(8,128)(2,1)S(1)}, u32[]{:S(2)}, u32[]{:S(2)}) collective-permute-start(bf16[1024,128]{1,0:T(8,128)(2,1)} %get-tuple-element.38), channel_id=1, source_target_pairs={{5,0},{6,1},{7,2},{4,3},{1,4},{2,5},{3,6},{0,7},{13,8},{14,9},{15,... | collective-permute-start | bytes 786440 | tf_op jit(solution)/shard_map/scatter_aggregate/ppermute | solution.py:33
  63.8 18.6 %copy-start.24 = (bf16[1024,128]{1,0:T(8,128)(2,1)}, bf16[1024,128]{1,0:T(8,128)(2,1)S(1)}, u32[]{:S(2)}) copy-start(bf16[1024,128]{1,0:T(8,128)(2,1)S(1)} %collective-permute-done.17.r3) | copy-start | bytes 786436
  63.8 18.6 %copy-start.25 = (bf16[1024,128]{1,0:T(8,128)(2,1)}, bf16[1024,128]{1,0:T(8,128)(2,1)S(1)}, u32[]{:S(2)}) copy-start(bf16[1024,128]{1,0:T(8,128)(2,1)S(1)} %collective-permute-done.18.r4) | copy-start | bytes 786436
  86.6 13.7 %collective-permute-start.22 = (bf16[8,128,128]{2,1,0:T(8,128)(2,1)}, bf16[8,128,128]{2,1,0:T(8,128)(2,1)S(1)}, u32[]{:S(2)}, u32[]{:S(2)}) collective-permute-start(bf16[8,128,128]{2,1,0:T(8,128)(2,1)} %get-tuple-element.40.refs_0_), channel_id=1, source_target_pairs={{1,0},{2,1},{3,2},{0,3},{5,4},{6,5},{7,6},{4,7},{9,8},{10,9},{11,1... | collective-permute-start | bytes 786440 | tf_op jit(solution)/shard_map/gather_gradients/ppermute | solution.py:33
  90.5 8.8 %collective-permute-start.29 = (f32[4,40,256]{2,1,0:T(8,128)}, f32[4,40,256]{2,1,0:T(8,128)S(1)}, u32[]{:S(2)}, u32[]{:S(2)}) collective-permute-start(f32[4,40,256]{2,1,0:T(8,128)} %get-tuple-element.44), channel_id=1, source_target_pairs={{4,0},{5,1},{6,2},{7,3},{0,4},{1,5},{2,6},{3,7},{12,8},{13,9},{14,... | collective-permute-start | bytes 491528 | tf_op jit(solution)/shard_map/weight_gradients/ppermute | solution.py:33
  90.7 14.6 %collective-permute-start.25 = (bf16[8,128,128]{2,1,0:T(8,128)(2,1)}, bf16[8,128,128]{2,1,0:T(8,128)(2,1)S(1)}, u32[]{:S(2)}, u32[]{:S(2)}) collective-permute-start(bf16[8,128,128]{2,1,0:T(8,128)(2,1)} %get-tuple-element.40.refs_0_), channel_id=1, source_target_pairs={{4,0},{5,1},{6,2},{7,3},{0,4},{1,5},{2,6},{3,7},{12,8},{13,9},{14,... | collective-permute-start | bytes 786440 | tf_op jit(solution)/shard_map/gather_gradients/ppermute | solution.py:33
  100.3 20.5 %copy-start.10 = (bf16[8,128,128]{2,1,0:T(8,128)(2,1)}, bf16[8,128,128]{2,1,0:T(8,128)(2,1)S(1)}, u32[]{:S(2)}) copy-start(bf16[8,128,128]{2,1,0:T(8,128)(2,1)S(1)} %collective-permute-done.22.refs_1_) | copy-start | bytes 786436
  100.3 12.6 %collective-permute-start.23 = (bf16[8,128,128]{2,1,0:T(8,128)(2,1)S(1)}, bf16[8,128,128]{2,1,0:T(8,128)(2,1)S(1)}, u32[]{:S(2)}, u32[]{:S(2)}) collective-permute-start(bf16[8,128,128]{2,1,0:T(8,128)(2,1)S(1)} %collective-permute-done.22.refs_1_), channel_id=1, source_target_pairs={{1,0},{2,1},{3,2},{0,3},{5,4},{6,5},{7,6},{4,7},{9,8},{10,9},{11,1... | collective-permute-start | bytes 786440 | tf_op jit(solution)/shard_map/gather_gradients/ppermute | solution.py:33
  100.4 9.3 %collective-permute-start.32 = (f32[40,256]{1,0:T(8,128)S(1)}, f32[40,256]{1,0:T(8,128)S(1)}, u32[]{:S(2)}, u32[]{:S(2)}) collective-permute-start(f32[40,256]{1,0:T(8,128)S(1)} %get-tuple-element.61), channel_id=1, source_target_pairs={{1,0},{2,1},{3,2},{0,3},{5,4},{6,5},{7,6},{4,7},{9,8},{10,9},{11,1... | collective-permute-start | bytes 122888 | tf_op jit(solution)/shard_map/weight_gradients/ppermute | solution.py:33
  102.2 7.5 %collective-permute-start.30 = (f32[40,256]{1,0:T(8,128)S(1)}, f32[40,256]{1,0:T(8,128)S(1)}, u32[]{:S(2)}, u32[]{:S(2)}) collective-permute-start(f32[40,256]{1,0:T(8,128)S(1)} %get-tuple-element.62), channel_id=1, source_target_pairs={{3,0},{0,1},{1,2},{2,3},{7,4},{4,5},{5,6},{6,7},{11,8},{8,9},{9,10... | collective-permute-start | bytes 122888 | tf_op jit(solution)/shard_map/weight_gradients/ppermute | solution.py:33
  102.5 10.8 %collective-permute-start.31 = (f32[40,256]{1,0:T(8,128)S(1)}, f32[40,256]{1,0:T(8,128)S(1)}, u32[]{:S(2)}, u32[]{:S(2)}) collective-permute-start(f32[40,256]{1,0:T(8,128)S(1)} %get-tuple-element.60), channel_id=1, source_target_pairs={{2,0},{3,1},{0,2},{1,3},{6,4},{7,5},{4,6},{5,7},{10,8},{11,9},{8,1... | collective-permute-start | bytes 122888 | tf_op jit(solution)/shard_map/weight_gradients/ppermute | solution.py:33
  105.2 15.6 %copy-start.13 = (bf16[8,128,128]{2,1,0:T(8,128)(2,1)}, bf16[8,128,128]{2,1,0:T(8,128)(2,1)S(1)}, u32[]{:S(2)}) copy-start(bf16[8,128,128]{2,1,0:T(8,128)(2,1)S(1)} %collective-permute-done.25.refs_4_) | copy-start | bytes 786436
  105.2 10.5 %collective-permute-start.28 = (bf16[8,128,128]{2,1,0:T(8,128)(2,1)S(1)}, bf16[8,128,128]{2,1,0:T(8,128)(2,1)S(1)}, u32[]{:S(2)}, u32[]{:S(2)}) collective-permute-start(bf16[8,128,128]{2,1,0:T(8,128)(2,1)S(1)} %collective-permute-done.25.refs_4_), channel_id=1, source_target_pairs={{3,0},{0,1},{1,2},{2,3},{7,4},{4,5},{5,6},{6,7},{11,8},{8,9},{9,10... | collective-permute-start | bytes 786440 | tf_op jit(solution)/shard_map/gather_gradients/ppermute | solution.py:33
  109.7 10.1 %collective-permute-start.24 = (bf16[8,128,128]{2,1,0:T(8,128)(2,1)}, bf16[8,128,128]{2,1,0:T(8,128)(2,1)S(1)}, u32[]{:S(2)}, u32[]{:S(2)}) collective-permute-start(bf16[8,128,128]{2,1,0:T(8,128)(2,1)} %get-tuple-element.40.refs_0_), channel_id=1, source_target_pairs={{3,0},{0,1},{1,2},{2,3},{7,4},{4,5},{5,6},{6,7},{11,8},{8,9},{9,10... | collective-permute-start | bytes 786440 | tf_op jit(solution)/shard_map/gather_gradients/ppermute | solution.py:33
  109.7 10.1 %collective-permute-start.26 = (bf16[8,128,128]{2,1,0:T(8,128)(2,1)S(1)}, bf16[8,128,128]{2,1,0:T(8,128)(2,1)S(1)}, u32[]{:S(2)}, u32[]{:S(2)}) collective-permute-start(bf16[8,128,128]{2,1,0:T(8,128)(2,1)S(1)} %collective-permute-done.25.refs_4_), channel_id=1, source_target_pairs={{1,0},{2,1},{3,2},{0,3},{5,4},{6,5},{7,6},{4,7},{9,8},{10,9},{11,1... | collective-permute-start | bytes 786440 | tf_op jit(solution)/shard_map/gather_gradients/ppermute | solution.py:33
  112.9 7.9 %collective-permute-start.27 = (bf16[8,128,128]{2,1,0:T(8,128)(2,1)S(1)}, bf16[8,128,128]{2,1,0:T(8,128)(2,1)S(1)}, u32[]{:S(2)}, u32[]{:S(2)}) collective-permute-start(bf16[8,128,128]{2,1,0:T(8,128)(2,1)S(1)} %collective-permute-done.23.refs_2_), channel_id=1, source_target_pairs={{4,0},{5,1},{6,2},{7,3},{0,4},{1,5},{2,6},{3,7},{12,8},{13,9},{14,... | collective-permute-start | bytes 786440 | tf_op jit(solution)/shard_map/gather_gradients/ppermute | solution.py:33
  130.0 25.6 %collective-permute-start.33 = (bf16[8,8,128,128]{3,2,1,0:T(8,128)(2,1)}, bf16[8,8,128,128]{3,2,1,0:T(8,128)(2,1)S(1)}, u32[]{:S(2)}, u32[]{:S(2)}) collective-permute-start(bf16[8,8,128,128]{3,2,1,0:T(8,128)(2,1)} %get-tuple-element.47), channel_id=1, source_target_pairs={{8,0},{0,8},{24,16},{16,24},{40,32},{32,40},{56,48},{48,56},{72,64... | collective-permute-start | bytes 6291464 | tf_op jit(solution)/shard_map/scatter_gradients/ppermute | solution.py:29
  130.1 3.5 %collective-permute-start.43 = (f32[40,256]{1,0:T(8,128)S(1)}, f32[40,256]{1,0:T(8,128)S(1)}, u32[]{:S(2)}, u32[]{:S(2)}) collective-permute-start(f32[40,256]{1,0:T(8,128)S(1)} %fusion.7), channel_id=1, source_target_pairs={{72,0},{64,8},{88,16},{80,24},{104,32},{96,40},{120,48},{112,56},{... | collective-permute-start | bytes 122888 | tf_op jit(solution)/shard_map/weight_gradients/ppermute | solution.py:29
  131.1 3.2 %collective-permute-start.41 = (f32[40,256]{1,0:T(8,128)S(1)}, f32[40,256]{1,0:T(8,128)S(1)}, u32[]{:S(2)}, u32[]{:S(2)}) collective-permute-start(f32[40,256]{1,0:T(8,128)S(1)} %fusion.7), channel_id=1, source_target_pairs={{8,0},{0,8},{24,16},{16,24},{40,32},{32,40},{56,48},{48,56},{72,64... | collective-permute-start | bytes 122888 | tf_op jit(solution)/shard_map/weight_gradients/ppermute | solution.py:29
  131.1 4.0 %collective-permute-start.42 = (f32[40,256]{1,0:T(8,128)S(1)}, f32[40,256]{1,0:T(8,128)S(1)}, u32[]{:S(2)}, u32[]{:S(2)}) collective-permute-start(f32[40,256]{1,0:T(8,128)S(1)} %fusion.7), channel_id=1, source_target_pairs={{64,0},{72,8},{80,16},{88,24},{96,32},{104,40},{112,48},{120,56},{... | collective-permute-start | bytes 122888 | tf_op jit(solution)/shard_map/weight_gradients/ppermute | solution.py:29
  135.2 13.3 %collective-permute-start.46 = (f32[40,256]{1,0:T(8,128)S(1)}, f32[40,256]{1,0:T(8,128)S(1)}, u32[]{:S(2)}, u32[]{:S(2)}) collective-permute-start(f32[40,256]{1,0:T(8,128)S(1)} %add_add_fusion.1), channel_id=1, source_target_pairs={{48,0},{56,8},{0,16},{8,24},{16,32},{24,40},{32,48},{40,56},{112,6... | collective-permute-start | bytes 122888 | tf_op jit(solution)/shard_map/weight_gradients/ppermute | solution.py:29
  135.2 13.2 %collective-permute-start.44 = (f32[40,256]{1,0:T(8,128)S(1)}, f32[40,256]{1,0:T(8,128)S(1)}, u32[]{:S(2)}, u32[]{:S(2)}) collective-permute-start(f32[40,256]{1,0:T(8,128)S(1)} %add_add_fusion.1), channel_id=1, source_target_pairs={{16,0},{24,8},{32,16},{40,24},{48,32},{56,40},{0,48},{8,56},{80,64... | collective-permute-start | bytes 122888 | tf_op jit(solution)/shard_map/weight_gradients/ppermute | solution.py:29
  146.3 5.5 %collective-permute-start.45 = (f32[40,256]{1,0:T(8,128)S(1)}, f32[40,256]{1,0:T(8,128)S(1)}, u32[]{:S(2)}, u32[]{:S(2)}) collective-permute-start(f32[40,256]{1,0:T(8,128)S(1)} %add_add_fusion.1), channel_id=1, source_target_pairs={{32,0},{40,8},{48,16},{56,24},{0,32},{8,40},{16,48},{24,56},{96,64... | collective-permute-start | bytes 122888 | tf_op jit(solution)/shard_map/weight_gradients/ppermute | solution.py:29
  151.8 10.1 %collective-permute-start.47 = (f32[40,256]{1,0:T(8,128)S(1)}, f32[40,256]{1,0:T(8,128)S(1)}, u32[]{:S(2)}, u32[]{:S(2)}) collective-permute-start(f32[40,256]{1,0:T(8,128)S(1)} %add_add_fusion.s0), channel_id=1, source_target_pairs={{1,0},{2,1},{3,2},{0,3},{5,4},{6,5},{7,6},{4,7},{9,8},{10,9},{11,1... | collective-permute-start | bytes 122888 | tf_op jit(solution)/shard_map/spread_weight_gradients/ppermute | solution.py:33
  152.4 9.6 %collective-permute-start.48 = (f32[40,256]{1,0:T(8,128)S(1)}, f32[40,256]{1,0:T(8,128)S(1)}, u32[]{:S(2)}, u32[]{:S(2)}) collective-permute-start(f32[40,256]{1,0:T(8,128)S(1)} %add_add_fusion.s0), channel_id=1, source_target_pairs={{2,0},{3,1},{0,2},{1,3},{6,4},{7,5},{4,6},{5,7},{10,8},{11,9},{8,1... | collective-permute-start | bytes 122888 | tf_op jit(solution)/shard_map/spread_weight_gradients/ppermute | solution.py:33
  154.3 7.7 %collective-permute-start.49 = (f32[40,256]{1,0:T(8,128)S(1)}, f32[40,256]{1,0:T(8,128)S(1)}, u32[]{:S(2)}, u32[]{:S(2)}) collective-permute-start(f32[40,256]{1,0:T(8,128)S(1)} %add_add_fusion.s0), channel_id=1, source_target_pairs={{3,0},{0,1},{1,2},{2,3},{7,4},{4,5},{5,6},{6,7},{11,8},{8,9},{9,10... | collective-permute-start | bytes 122888 | tf_op jit(solution)/shard_map/spread_weight_gradients/ppermute | solution.py:33
  158.5 14.8 %collective-permute-start.34 = (bf16[8,128,128]{2,1,0:T(8,128)(2,1)S(1)}, bf16[8,128,128]{2,1,0:T(8,128)(2,1)S(1)}, u32[]{:S(2)}, u32[]{:S(2)}) collective-permute-start(bf16[8,128,128]{2,1,0:T(8,128)(2,1)S(1)} %get-tuple-element.59), channel_id=1, source_target_pairs={{48,0},{56,8},{0,16},{8,24},{16,32},{24,40},{32,48},{40,56},{112,6... | collective-permute-start | bytes 786440 | tf_op jit(solution)/shard_map/scatter_gradients/ppermute | solution.py:29
  158.5 16.3 %collective-permute-start.35 = (bf16[8,128,128]{2,1,0:T(8,128)(2,1)S(1)}, bf16[8,128,128]{2,1,0:T(8,128)(2,1)S(1)}, u32[]{:S(2)}, u32[]{:S(2)}) collective-permute-start(bf16[8,128,128]{2,1,0:T(8,128)(2,1)S(1)} %get-tuple-element.58), channel_id=1, source_target_pairs={{32,0},{40,8},{48,16},{56,24},{0,32},{8,40},{16,48},{24,56},{96,64... | collective-permute-start | bytes 786440 | tf_op jit(solution)/shard_map/scatter_gradients/ppermute | solution.py:29
  161.9 14.8 %copy-start.36 = (f32[40,256]{1,0:T(8,128)}, f32[40,256]{1,0:T(8,128)S(1)}, u32[]{:S(2)}) copy-start(f32[40,256]{1,0:T(8,128)S(1)} %collective-permute-done.47.s1) | copy-start | bytes 122884
  162.0 10.3 %collective-permute-start.50 = (f32[4,40,256]{2,1,0:T(8,128)S(1)}, f32[4,40,256]{2,1,0:T(8,128)S(1)}, u32[]{:S(2)}, u32[]{:S(2)}) collective-permute-start(f32[4,40,256]{2,1,0:T(8,128)S(1)} %pad_maximum_fusion), channel_id=1, source_target_pairs={{4,0},{5,1},{6,2},{7,3},{0,4},{1,5},{2,6},{3,7},{12,8},{13,9},{14,... | collective-permute-start | bytes 491528 | tf_op jit(solution)/shard_map/spread_weight_gradients/ppermute | solution.py:33
  167.6 10.9 %collective-permute-start.36 = (bf16[8,128,128]{2,1,0:T(8,128)(2,1)S(1)}, bf16[8,128,128]{2,1,0:T(8,128)(2,1)S(1)}, u32[]{:S(2)}, u32[]{:S(2)}) collective-permute-start(bf16[8,128,128]{2,1,0:T(8,128)(2,1)S(1)} %get-tuple-element.57), channel_id=1, source_target_pairs={{16,0},{24,8},{32,16},{40,24},{48,32},{56,40},{0,48},{8,56},{80,64... | collective-permute-start | bytes 786440 | tf_op jit(solution)/shard_map/scatter_gradients/ppermute | solution.py:29
  168.4 10.8 %collective-permute-start.37 = (bf16[8,128,128]{2,1,0:T(8,128)(2,1)S(1)}, bf16[8,128,128]{2,1,0:T(8,128)(2,1)S(1)}, u32[]{:S(2)}, u32[]{:S(2)}) collective-permute-start(bf16[8,128,128]{2,1,0:T(8,128)(2,1)S(1)} %get-tuple-element.56), channel_id=1, source_target_pairs={{64,0},{72,8},{80,16},{88,24},{96,32},{104,40},{112,48},{120,56},{... | collective-permute-start | bytes 786440 | tf_op jit(solution)/shard_map/scatter_gradients/ppermute | solution.py:29
  172.3 11.7 %collective-permute-start.38 = (bf16[8,128,128]{2,1,0:T(8,128)(2,1)S(1)}, bf16[8,128,128]{2,1,0:T(8,128)(2,1)S(1)}, u32[]{:S(2)}, u32[]{:S(2)}) collective-permute-start(bf16[8,128,128]{2,1,0:T(8,128)(2,1)S(1)} %get-tuple-element.55), channel_id=1, source_target_pairs={{112,0},{120,8},{64,16},{72,24},{80,32},{88,40},{96,48},{104,56},{... | collective-permute-start | bytes 786440 | tf_op jit(solution)/shard_map/scatter_gradients/ppermute | solution.py:29
  173.3 18.8 %copy-start.29 = (bf16[8,128,128]{2,1,0:T(8,128)(2,1)}, bf16[8,128,128]{2,1,0:T(8,128)(2,1)S(1)}, u32[]{:S(2)}) copy-start(bf16[8,128,128]{2,1,0:T(8,128)(2,1)S(1)} %collective-permute-done.34.r1) | copy-start | bytes 786436
  173.3 17.0 %collective-permute-start.39 = (bf16[8,128,128]{2,1,0:T(8,128)(2,1)S(1)}, bf16[8,128,128]{2,1,0:T(8,128)(2,1)S(1)}, u32[]{:S(2)}, u32[]{:S(2)}) collective-permute-start(bf16[8,128,128]{2,1,0:T(8,128)(2,1)S(1)} %get-tuple-element.54), channel_id=1, source_target_pairs={{96,0},{104,8},{112,16},{120,24},{64,32},{72,40},{80,48},{88,56},{... | collective-permute-start | bytes 786440 | tf_op jit(solution)/shard_map/scatter_gradients/ppermute | solution.py:29
  174.9 17.2 %copy-start.30 = (bf16[8,128,128]{2,1,0:T(8,128)(2,1)}, bf16[8,128,128]{2,1,0:T(8,128)(2,1)S(1)}, u32[]{:S(2)}) copy-start(bf16[8,128,128]{2,1,0:T(8,128)(2,1)S(1)} %collective-permute-done.35.r2) | copy-start | bytes 786436
  174.9 17.2 %collective-permute-start.40 = (bf16[8,128,128]{2,1,0:T(8,128)(2,1)S(1)}, bf16[8,128,128]{2,1,0:T(8,128)(2,1)S(1)}, u32[]{:S(2)}, u32[]{:S(2)}) collective-permute-start(bf16[8,128,128]{2,1,0:T(8,128)(2,1)S(1)} %get-tuple-element.53), channel_id=1, source_target_pairs={{80,0},{88,8},{96,16},{104,24},{112,32},{120,40},{64,48},{72,56},{... | collective-permute-start | bytes 786440 | tf_op jit(solution)/shard_map/scatter_gradients/ppermute | solution.py:29
  (27 other events, 164.8 us)

commit v2 on v1

--- a/solution.py
+++ b/solution.py
@@ -12,7 +12,8 @@
 CHUNK = 32
 UNROLL = 32
 BATCH = 4
-SLICE = 32
+SLICE = 64
+STEPS = ((), (4, 6, 2), (1, 3, 5, 7))
 VMEM_BYTES = 56 * 1024 * 1024
 RELATIVE = [(dx, dy) for dx in (0, 1) for dy in range(4)]
 
@@ -33,12 +34,10 @@
     return lax.ppermute(x, "narrow", [(narrow_index(n, dx, dz), n) for n in range(8)])
 
 
-def gather_ring(x, fetch):
-    got = {(0, 0): x}
-    got[0, 1] = fetch(x, 0, 1)
-    got[0, 3] = fetch(x, 0, 3)
-    got[1, 0] = fetch(x, 1, 0)
-    got[0, 2] = fetch(got[0, 1], 0, 1)
+def gather_ring(x, fetch, together):
+    first = [(1, 0), (0, 2), (0, 1), (0, 3)]
+    got = dict(zip(first, together([fetch(x, *key) for key in first])))
+    got[0, 0] = x
     got[1, 1] = fetch(got[1, 0], 0, 1)
     got[1, 3] = fetch(got[1, 0], 0, 3)
     got[1, 2] = fetch(got[0, 2], 1, 0)
@@ -106,7 +105,7 @@
 
 def forward_kernel(meta, cols, pairs, total, tiles_hbm, *refs):
     panels_hbm, outs = refs[:16], refs[16:24]
-    panels, tiles, acc, panel_sems, tile_sems = refs[24:]
+    panels, tiles, acc, staged, panel_sems, tile_sems, out_sems = refs[24:]
     count, w, n = meta[0], meta[1], meta[2]
     copies = []
     for k in range(16):
@@ -122,13 +121,11 @@
     load_tiles(tiles_hbm, tiles, tile_sems, count)
     acc[...] = jnp.zeros_like(acc)
     tiles[tiles.shape[0] - 1] = jnp.zeros(tiles.shape[1:], tiles.dtype)
-    spare = pl.ds(panels.shape[0] - TILE, TILE)
-    panels[spare, :] = jnp.zeros((TILE, panels.shape[1]), panels.dtype)
     for copy in copies:
         copy.wait()
 
     def panel(s):
-        column = pl.multiple_of(cols[s] * TILE, TILE)
+        column = pl.multiple_of(cols[jnp.minimum(s, cols.shape[0] - 1)] * TILE, TILE)
         return panels[pl.ds(column, TILE), :]
 
     def visit(group):
@@ -145,7 +142,10 @@
     for k, (dx, dz) in enumerate(RELATIVE):
         owner = narrow_index(n, dx, dz)
         block = acc[pl.ds(owner * PANEL, PANEL)]
-        outs[k][...] = block.reshape(PANEL * TILE, -1).astype(jnp.bfloat16)
+        staged[k] = block.reshape(PANEL * TILE, -1).astype(jnp.bfloat16)
+        pltpu.make_async_copy(staged.at[k], outs[k], out_sems.at[k]).start()
+    for k in range(8):
+        pltpu.make_async_copy(staged.at[k], outs[k], out_sems.at[k]).wait()
 
 
 def dense_kernel(
@@ -171,44 +171,26 @@
         back_out[k] = back[:, k * TILE : (k + 1) * TILE]
 
 
-def weight_kernel(scale, meta, x, agg, pre, ws, far, near, self_term):
+def weight_kernel(scale, meta, x, agg, pre, ws, slices, self_term):
     rows = (((0,), (0,)), ((), ()))
     n = meta[2]
     block = pre[...]
-    half = [
-        scale * lax.dot_general(v[...], block, rows, preferred_element_type=jnp.float32)
-        for v in (x, agg)
-    ]
-    mine = (n >> 2) == 0
     total = scale * jnp.sum(block.astype(jnp.float32), axis=0, keepdims=True)
     total = jnp.broadcast_to(total, (8, total.shape[1]))
-    for out, grads in (
-        (near, jnp.where(mine, half[0], half[1])),
-        (far, jnp.where(mine, half[1], half[0])),
-    ):
-        for z in range(Z):
-            place = (z - n) & 3
-            out[place, :SLICE] = grads[z * SLICE : (z + 1) * SLICE]
-            out[place, SLICE:] = total
+    for j, left in enumerate((x, agg)):
+        grads = scale * lax.dot_general(left[...], block, rows, preferred_element_type=jnp.float32)
+        for k in range(2):
+            place = (2 * j + k - n) & 3
+            slices[place, :SLICE] = grads[k * SLICE : (k + 1) * SLICE]
+            slices[place, SLICE:] = total
     self_term[...] = lax.dot_general(
         block, ws[...], (((1,), (1,)), ((), ())), preferred_element_type=jnp.float32
     )
 
 
-def assemble_kernel(meta, s0, s1, s2, s3, other, grad_self, grad_neigh, grad_bias):
-    n = meta[2]
-    mine = (n >> 2) == 0
-    grad_bias[...] = s0[SLICE : SLICE + 1, :]
-    for dz, s in enumerate((s0, s1, s2, s3)):
-        place = pl.ds(pl.multiple_of(((n + dz) & 3) * SLICE, SLICE), SLICE)
-        here, there = s[:SLICE, :], other[dz, :SLICE, :]
-        grad_self[place, :] = jnp.where(mine, here, there)
-        grad_neigh[place, :] = jnp.where(mine, there, here)
-
-
 def backward_kernel(meta, cols, pairs, total, tiles_hbm, *refs):
     grads_hbm, (swap, keep) = refs[:8], refs[8:10]
-    grads, tiles, acc, grad_sems, tile_sems = refs[10:]
+    grads, tiles, acc, staged, grad_sems, tile_sems, out_sems = refs[10:]
     count, w, n = meta[0], meta[1], meta[2]
     copies = []
     for k, (dx, dz) in enumerate(RELATIVE):
@@ -234,23 +216,47 @@
                 right = jnp.concatenate([tiles[first], tiles[second]], axis=1)
                 products.append(jnp.dot(grads[row], right, preferred_element_type=jnp.float32))
             for (_, first, second), product in zip(group[part : part + BATCH], products):
-                acc[cols[first]] += product[:, :TILE]
-                acc[cols[second]] += product[:, TILE:]
+                last = cols.shape[0] - 1
+                acc[cols[jnp.minimum(first, last)]] += product[:, :TILE]
+                acc[cols[jnp.minimum(second, last)]] += product[:, TILE:]
 
     visit_pairs(count, total, pairs, visit, tiles_hbm, tiles, tile_sems)
-    for k, (dx, dy) in enumerate(RELATIVE):
-        for dc, out in ((0, keep), (1, swap)):
+    outs = ((1, swap), (0, keep))
+    for dc, out in outs:
+        for k, (dx, dy) in enumerate(RELATIVE):
             owner = wide_index(w, dx, dy, dc)
-            out[k] = acc[pl.ds(owner * PANEL, PANEL)].astype(jnp.bfloat16)
-
-
-def final_kernel(keep, swapped, r1, r2, r3, r4, r5, r6, r7, self_term, out):
+            staged[dc, k] = acc[pl.ds(owner * PANEL, PANEL)].astype(jnp.bfloat16)
+            pltpu.make_async_copy(staged.at[dc, k], out.at[k], out_sems.at[dc, k]).start()
+    for dc, out in outs:
+        for k in range(8):
+            pltpu.make_async_copy(staged.at[dc, k], out.at[k], out_sems.at[dc, k]).wait()
+
+
+def final_kernel(
+    meta, keep, swapped, r1, r2, r3, r4, r5, r6, r7, self_term, s0, s1, s2, s3, *outs
+):
+    out, grad_self, grad_neigh, grad_bias = outs
     for j in range(r1.shape[0]):
         total = keep[0, j].astype(jnp.float32) + swapped[0, j].astype(jnp.float32)
         for r in (r1, r2, r3, r4, r5, r6, r7):
             total = total + r[j].astype(jnp.float32)
         rows = pl.ds(j * TILE, TILE)
         out[rows, :] = (self_term[rows, :] + total.T).astype(jnp.bfloat16)
+
+    @pl.when(pl.program_id(0) == 0)
+    def _():
+        grad_bias[...] = s0[SLICE : SLICE + 1, :]
+        for dz, s in enumerate((s0, s1, s2, s3)):
+            place = (meta[2] + dz) & 3
+            rows = pl.ds(pl.multiple_of((place & 1) * SLICE, SLICE), SLICE)
+
+            @pl.when(place < 2)
+            def _():
+                grad_self[rows, :] = s[:SLICE, :]
+
+            @pl.when(place >= 2)
+            def _():
+                grad_neigh[rows, :] = s[:SLICE, :]
 
 
 def local(
@@ -273,8 +279,6 @@
     col_tiles = wide_count * PANEL
     w, n = lax.axis_index("wide"), lax.axis_index("narrow")
     meta = jnp.stack([tile_count[0], w.astype(jnp.int32), n.astype(jnp.int32), row_tiles])
-    dead = jnp.full((1,), col_tiles, jnp.int32)
-    cols = jnp.concatenate([tile_cols, dead])
     smem = pl.BlockSpec(memory_space=pltpu.SMEM)
     hbm = pl.BlockSpec(memory_space=pl.ANY)
     vmem = pl.BlockSpec(memory_space=pltpu.VMEM)
@@ -286,10 +290,6 @@
         transcendentals=0,
     )
 
-    with jax.named_scope("gather_features"):
-        same_core = gather_ring(node_features, lambda v, dx, dy: from_wide(v, dx, dy, 0))
-        other_core = [from_wide(v, 0, 0, 1) for v in same_core]
-
     with jax.named_scope("plan"):
         pairs, total = pl.pallas_call(
             plan_kernel,
@@ -302,30 +302,37 @@
             name="plan",
         )(meta, tile_rows)
 
+    def after_plan(blocks):
+        return lax.optimization_barrier((*blocks, total))[:-1]
+
+    with jax.named_scope("gather_features"):
+        same_core = gather_ring(
+            node_features, lambda v, dx, dy: from_wide(v, dx, dy, 0), after_plan
+        )
+        other_core = [from_wide(v, 0, 0, 1) for v in same_core]
+
     with jax.named_scope("aggregate"):
         partial = pl.pallas_call(
             forward_kernel,
             out_shape=[jax.ShapeDtypeStruct((own_nodes, features), bf16)] * 8,
             in_specs=[smem] * 4 + [hbm] * 17,
-            out_specs=[vmem] * 8,
+            out_specs=[hbm] * 8,
             scratch_shapes=[
-                pltpu.VMEM(((col_tiles + 1) * TILE, features), bf16),
+                pltpu.VMEM((col_tiles * TILE, features), bf16),
                 pltpu.VMEM((slots + 1, TILE, TILE), bf16),
                 pltpu.VMEM((row_tiles + 1, TILE, features), f32),
+                pltpu.VMEM((8, own_nodes, features), bf16),
                 pltpu.SemaphoreType.DMA((16,)),
                 pltpu.SemaphoreType.DMA((slots // CHUNK,)),
+                pltpu.SemaphoreType.DMA((8,)),
             ],
             compiler_params=pltpu.CompilerParams(vmem_limit_bytes=VMEM_BYTES),
             cost_estimate=tile_dots,
             name="aggregate",
-        )(meta, cols, pairs, total, tile_values, *same_core, *other_core)
+        )(meta, tile_cols, pairs, total, tile_values, *same_core, *other_core)
 
     with jax.named_scope("scatter_aggregate"):
-        received = [
-            from_narrow(partial[k], dx, -dz & 3)
-            for k, (dx, dz) in enumerate(RELATIVE)
-            if k > 0
-        ]
+        received = [from_narrow(partial[k], RELATIVE[k][0], -k & 3) for k in (6, 4, 2, 5, 7, 1, 3)]
 
     block = own_nodes // 2
     node_spec = pl.BlockSpec((block, features), lambda i: (i, 0))
@@ -357,16 +364,15 @@
             grad_output,
         )
 
-    with jax.named_scope("gather_gradients"):
-        grads = gather_ring(back, from_narrow)
-
     with jax.named_scope("weight_gradients"):
-        slices = jax.ShapeDtypeStruct((Z, SLICE + 8, hidden), f32)
-        far, near, self_term = pl.pallas_call(
+        slices, self_term = pl.pallas_call(
             lambda *refs: weight_kernel(scale, *refs),
-            out_shape=[slices, slices, jax.ShapeDtypeStruct((own_nodes, features), f32)],
+            out_shape=[
+                jax.ShapeDtypeStruct((Z, SLICE + 8, hidden), f32),
+                jax.ShapeDtypeStruct((own_nodes, features), f32),
+            ],
             in_specs=[smem] + [vmem] * 4,
-            out_specs=[vmem] * 3,
+            out_specs=[vmem] * 2,
             compiler_params=pltpu.CompilerParams(vmem_limit_bytes=VMEM_BYTES),
             cost_estimate=pl.CostEstimate(
                 flops=6 * own_nodes * features * hidden,
@@ -375,11 +381,12 @@
             ),
             name="weight_gradients",
         )(meta, node_features, own_agg, grad_pre, weight_self)
-        near = near + from_narrow(far, 1, 0)
-        part = near[0] + sum(from_narrow(near[dz], 0, -dz & 3) for dz in (1, 2, 3))
-        grads[-1], part = lax.optimization_barrier((grads[-1], part))
-        part = part + sum(from_wide(part, dx, 0, dc) for dx, dc in ((0, 1), (1, 0), (1, 1)))
-        part = part + sum(from_wide(part, 0, dy, 0) for dy in (1, 2, 3))
+
+        part = slices[0] + sum(from_narrow(slices[dz], 0, -dz & 3) for dz in (1, 2, 3))
+
+    with jax.named_scope("gather_gradients"):
+        grads = gather_ring(back, from_narrow, lax.optimization_barrier)
+        *grads, part = lax.optimization_barrier((*grads, part))
 
     with jax.named_scope("column_gradients"):
         pieces = jax.ShapeDtypeStruct((8, PANEL, features, TILE), bf16)
@@ -387,53 +394,74 @@
             backward_kernel,
             out_shape=[pieces, pieces],
             in_specs=[smem] * 4 + [hbm] * 9,
-            out_specs=[vmem] * 2,
+            out_specs=[hbm] * 2,
             scratch_shapes=[
                 pltpu.VMEM((row_tiles + 1, features, TILE), bf16),
                 pltpu.VMEM((slots + 1, TILE, TILE), bf16),
-                pltpu.VMEM((col_tiles + 1, features, TILE), f32),
+                pltpu.VMEM((col_tiles, features, TILE), f32),
+                pltpu.VMEM((CORES, 8, PANEL, features, TILE), bf16),
                 pltpu.SemaphoreType.DMA((8,)),
                 pltpu.SemaphoreType.DMA((slots // CHUNK,)),
+                pltpu.SemaphoreType.DMA((CORES, 8)),
             ],
             compiler_params=pltpu.CompilerParams(vmem_limit_bytes=VMEM_BYTES),
             cost_estimate=tile_dots,
             name="column_gradients",
-        )(meta, cols, pairs, total, tile_values, *grads)
+        )(meta, tile_cols, pairs, total, tile_values, *grads)
+
+    def send(k):
+        dx, dy = RELATIVE[k]
+        return from_wide(pairs_sum[k], dx, -dy & 3, 0)
+
+    def together(values, part):
+        *values, part = lax.optimization_barrier((*values, part))
+        return values, part
 
     with jax.named_scope("scatter_gradients"):
+        part = part + from_narrow(part, 1, 0)
+        swap, keep, part = lax.optimization_barrier((swap, keep, part))
         swapped = from_wide(swap, 0, 0, 1)
-        column = []
-        for k, (dx, dy) in enumerate(RELATIVE):
-            if k > 0:
-                pair = (keep[k].astype(f32) + swapped[k].astype(f32)).astype(bf16)
-                column.append(from_wide(pair, dx, -dy & 3, 0))
-
-    with jax.named_scope("spread_weight_gradients"):
+        part = part + sum(from_wide(part, dx, 0, dc) for dx, dc in ((0, 1), (1, 0), (1, 1)))
+        pairs_sum = [
+            (keep[k].astype(f32) + swapped[k].astype(f32)).astype(bf16) for k in range(8)
+        ]
+        pairs_sum, part = together(pairs_sum, part)
+        column = {k: send(k) for k in STEPS[0]}
+        part = part + sum(from_wide(part, 0, dy, 0) for dy in (1, 2, 3))
+        sent, part = together([column[k] for k in STEPS[0]], part)
+        column.update(zip(STEPS[0], sent))
+        column.update((k, send(k)) for k in STEPS[1])
         quarters = [part] + [from_narrow(part, 0, dz) for dz in (1, 2, 3)]
-        other = from_narrow(jnp.stack(quarters), 1, 0)
-        grad_self, grad_neigh, grad_bias = pl.pallas_call(
-            assemble_kernel,
+        sent = lax.optimization_barrier([column[k] for k in STEPS[1]] + quarters)
+        column.update(zip(STEPS[1], sent))
+        quarters = sent[len(STEPS[1]) :]
+        column.update((k, send(k)) for k in STEPS[2])
+
+    with jax.named_scope("grad_input"):
+        slice_spec = pl.BlockSpec((SLICE + 8, hidden), lambda i: (0, 0))
+        first_spec = pl.BlockSpec((1, block // TILE, features, TILE), lambda i: (0, i, 0, 0))
+        grad_input, grad_self, grad_neigh, grad_bias = pl.pallas_call(
+            final_kernel,
+            grid=(own_nodes // block,),
             out_shape=[
+                jax.ShapeDtypeStruct((own_nodes, features), bf16),
                 jax.ShapeDtypeStruct((features, hidden), f32),
                 jax.ShapeDtypeStruct((features, hidden), f32),
                 jax.ShapeDtypeStruct((1, hidden), f32),
             ],
-            in_specs=[smem] + [vmem] * 5,
-            out_specs=[vmem] * 3,
-            name="assemble",
-        )(meta, *quarters, other)
-
-    with jax.named_scope("grad_input"):
-        first_spec = pl.BlockSpec((1, block // TILE, features, TILE), lambda i: (0, i, 0, 0))
-        grad_input = pl.pallas_call(
-            final_kernel,
-            grid=(own_nodes // block,),
-            out_shape=jax.ShapeDtypeStruct((own_nodes, features), bf16),
-            in_specs=[first_spec] * 2 + [piece_spec] * 7 + [node_spec],
-            out_specs=node_spec,
+            in_specs=[smem, first_spec, first_spec]
+            + [piece_spec] * 7
+            + [node_spec]
+            + [slice_spec] * Z,
+            out_specs=[
+                node_spec,
+                weight_spec,
+                weight_spec,
+                pl.BlockSpec((1, hidden), lambda i: (0, 0)),
+            ],
             compiler_params=pltpu.CompilerParams(vmem_limit_bytes=VMEM_BYTES),
             name="grad_input",
-        )(keep, swapped, *column, self_term)
+        )(meta, keep, swapped, *[column[k] for k in range(1, 8)], self_term, *quarters)
     return (output, grad_input, grad_self, grad_neigh, grad_bias[0])
 
 

time: 196 us -> 176 us (0.90); the launches traced: 196 us -> 172 us
  waiting for transfers between devices: 72.5 us -> 57.6 us
  starting transfers between devices: 83.4 us -> 78.5 us
  Pallas kernels: 29.2 us -> 26.5 us
    ppermute x22 -> x21, waiting for transfers between devices: 40.2 us -> 28.5 us  [from_narrow(): lax.ppermute(x, 'narrow', [(narrow_index(n, dx, dz), n) for n in range(8)])]
    ppermute x29, starting transfers between devices: 38.3 us -> 34 us  [from_wide(): lax.ppermute(x, 'wide', [(wide_index(w, dx, dy, dc), w) for w in range(16)])]
    ppermute x29, waiting for transfers between devices: 32.3 us -> 29.1 us  [from_wide(): lax.ppermute(x, 'wide', [(wide_index(w, dx, dy, dc), w) for w in range(16)])]
    pallas_call x3 -> x2, Pallas kernels: 6.99 us -> 5.52 us  [the longest x1 3.01 us: local(): pl.pallas_call(final_kernel, grid=(own_nodes // block,), out_shape=[jax.S...]
    ppermute x22 -> x21, starting transfers between devices: 45.1 us -> 44.4 us  [from_narrow(): lax.ppermute(x, 'narrow', [(narrow_index(n, dx, dz), n) for n in range(8)])]
  transfers between devices with their start and end apart: 51 -> 50, of which waited for: 23 -> 19; matrix products, arithmetic and copies ran while one was open for 3% -> 1% of each run, Pallas kernels for 3% -> 7%
where the time goes in v2:
time: 176 us; the launch traced here: 172 us
  starting transfers between devices  78.5 us (45%)
  waiting for transfers between devices  57.6 us (33%)
  Pallas kernels  26.5 us (15%)
  other arithmetic  4.42 us (3%)
  local copies, waits for them, and re-layouts  3.36 us (2%)
  between operations  1.92 us (1%)
    ppermute x21, starting transfers between devices, from_narrow(): lax.ppermute(x, 'narrow', [(narrow_index(n, dx, dz), n) for n in range(8)])  44.4 us
    ppermute x29, starting transfers between devices, from_wide(): lax.ppermute(x, 'wide', [(wide_index(w, dx, dy, dc), w) for w in range(16)])  34 us
    ppermute x29, waiting for transfers between devices, from_wide(): lax.ppermute(x, 'wide', [(wide_index(w, dx, dy, dc), w) for w in range(16)])  29.1 us
    ppermute x21, waiting for transfers between devices, from_narrow(): lax.ppermute(x, 'narrow', [(narrow_index(n, dx, dz), n) for n in range(8)])  28.5 us
    pallas_call x1, Pallas kernels, local(): pl.pallas_call(backward_kernel, out_shape=[pieces, pieces], in_specs=[sme...  7.84 us
    pallas_call x1, Pallas kernels, local(): pl.pallas_call(forward_kernel, out_shape=[jax.ShapeDtypeStruct((own_nodes...  7.72 us
  transfers between devices with their start and end apart: 50, of which 19 were waited for; matrix products, arithmetic and copies ran while one was open for 1% of the time, Pallas kernels for 7%

profile of v2, /device:TPU:0, one launch (start us, length us, event | category | flops | bytes accessed | tf_op | source)
XLA Modules:
  0.0 172.2 jit_solution(4556705272254580070)
XLA Ops:
  0.6 1.7 %collective-permute-start.3 = (bf16[1024,128]{1,0:T(8,128)(2,1)}, bf16[1024,128]{1,0:T(8,128)(2,1)S(1)}, u32[]{:S(2)}, u32[]{:S(2)}) collective-permute-start(bf16[1024,128]{1,0:T(8,128)(2,1)} %refs_1_.1), channel_id=1, source_target_pairs={{48,0},{56,8},{0,16},{8,24},{16,32},{24,40},{32,48},{40,56},{112,6... | collective-permute-start | bytes 786440 | tf_op jit(solution)/shard_map/gather_features/ppermute | solution.py:30
  2.4 1.6 collective-permute-start.2
  3.9 2.1 %collective-permute-start.1 = (bf16[1024,128]{1,0:T(8,128)(2,1)}, bf16[1024,128]{1,0:T(8,128)(2,1)S(1)}, u32[]{:S(2)}, u32[]{:S(2)}) collective-permute-start(bf16[1024,128]{1,0:T(8,128)(2,1)} %refs_1_.1), channel_id=1, source_target_pairs={{32,0},{40,8},{48,16},{56,24},{0,32},{8,40},{16,48},{24,56},{96,64... | collective-permute-start | bytes 786440 | tf_op jit(solution)/shard_map/gather_features/ppermute | solution.py:30
  6.0 1.5 collective-permute-start
  8.2 0.6 pad_add_fusion.meta.refs_0_
  8.8 1.9 %plan.1 = (s32[3,320]{1,0:T(4,128)}, s32[1]{0:T(128)}) custom-call(s32[4]{0:T(128)} %pad_add_fusion.meta.refs_0_, s32[512]{0:T(512)} %rows.1), custom_call_target="tpu_custom_call" | custom-call | tf_op jit(solution)/shard_map/plan/plan/pallas_call | solution.py:294
  10.7 4.7 %collective-permute-done.2.refs_1_ = bf16[1024,128]{1,0:T(8,128)(2,1)S(1)} collective-permute-done((bf16[1024,128]{1,0:T(8,128)(2,1)}, bf16[1024,128]{1,0:T(8,128)(2,1)S(1)}, u32[]{:S(2)}, u32[]{:S(2)}) %collective-permute-start.2) | collective-permute-done | bytes 262176 | tf_op jit(solution)/shard_map/gather_features/ppermute | solution.py:30
  15.4 1.7 collective-permute-done.1.refs_2_
  17.2 0.5 collective-permute-start.10
  17.7 1.5 collective-permute-start.5
  19.2 1.1 collective-permute-start.6
  20.3 2.1 %collective-permute-start.4 = (bf16[1024,128]{1,0:T(8,128)(2,1)S(1)}, bf16[1024,128]{1,0:T(8,128)(2,1)S(1)}, u32[]{:S(2)}, u32[]{:S(2)}) collective-permute-start(bf16[1024,128]{1,0:T(8,128)(2,1)S(1)} %collective-permute-done.refs_4_), channel_id=1, source_target_pairs={{16,0},{24,8},{32,16},{40,24},{48,32},{56,40},{0,48},{8,56},{80,64... | collective-permute-start | bytes 786440 | tf_op jit(solution)/shard_map/gather_features/ppermute | solution.py:30
  22.5 0.5 collective-permute-start.11
  23.0 3.0 %collective-permute-done.5.refs_6_ = bf16[1024,128]{1,0:T(8,128)(2,1)S(1)} collective-permute-done((bf16[1024,128]{1,0:T(8,128)(2,1)S(1)}, bf16[1024,128]{1,0:T(8,128)(2,1)S(1)}, u32[]{:S(2)}, u32[]{:S(2)}) %collective-permute-start.5) | collective-permute-done | bytes 262176 | tf_op jit(solution)/shard_map/gather_features/ppermute | solution.py:30
  26.0 2.4 %collective-permute-done.6.refs_7_ = bf16[1024,128]{1,0:T(8,128)(2,1)S(1)} collective-permute-done((bf16[1024,128]{1,0:T(8,128)(2,1)S(1)}, bf16[1024,128]{1,0:T(8,128)(2,1)S(1)}, u32[]{:S(2)}, u32[]{:S(2)}) %collective-permute-start.6) | collective-permute-done | bytes 262176 | tf_op jit(solution)/shard_map/gather_features/ppermute | solution.py:30
  28.4 0.5 collective-permute-start.12
  29.0 1.0 collective-permute-done.14.refs_15_
  30.7 0.4 copy-done.22
  31.1 7.7 %aggregate.1 = (bf16[1024,128]{1,0:T(8,128)(2,1)}, bf16[1024,128]{1,0:T(8,128)(2,1)}, bf16[1024,128]{1,0:T(8,128)(2,1)}, bf16[1024,128]{1,0:T(8,128)(2,1)}, bf16...) custom-call(s32[4]{0:T(128)} %pad_add_fusion.meta.refs_0_, ...), custom_call_target="tpu_custom_call" | custom-call | flops 2147483648 | bytes 23068672 | tf_op jit(solution)/shard_map/aggregate/aggregate/pallas_call | solution.py:315
  38.8 6.1 %collective-permute-start.15 = (bf16[1024,128]{1,0:T(8,128)(2,1)}, bf16[1024,128]{1,0:T(8,128)(2,1)S(1)}, u32[]{:S(2)}, u32[]{:S(2)}) collective-permute-start(bf16[1024,128]{1,0:T(8,128)(2,1)} %get-tuple-element.69), channel_id=1, source_target_pairs={{6,0},{7,1},{4,2},{5,3},{2,4},{3,5},{0,6},{1,7},{14,8},{15,9},{12,... | collective-permute-start | bytes 786440 | tf_op jit(solution)/shard_map/scatter_aggregate/ppermute | solution.py:34
  44.9 3.3 %collective-permute-start.16 = (bf16[1024,128]{1,0:T(8,128)(2,1)}, bf16[1024,128]{1,0:T(8,128)(2,1)S(1)}, u32[]{:S(2)}, u32[]{:S(2)}) collective-permute-start(bf16[1024,128]{1,0:T(8,128)(2,1)} %get-tuple-element.70), channel_id=1, source_target_pairs={{4,0},{5,1},{6,2},{7,3},{0,4},{1,5},{2,6},{3,7},{12,8},{13,9},{14,... | collective-permute-start | bytes 786440 | tf_op jit(solution)/shard_map/scatter_aggregate/ppermute | solution.py:34
  48.2 2.3 %collective-permute-start.18 = (bf16[1024,128]{1,0:T(8,128)(2,1)}, bf16[1024,128]{1,0:T(8,128)(2,1)S(1)}, u32[]{:S(2)}, u32[]{:S(2)}) collective-permute-start(bf16[1024,128]{1,0:T(8,128)(2,1)} %get-tuple-element.72), channel_id=1, source_target_pairs={{7,0},{4,1},{5,2},{6,3},{3,4},{0,5},{1,6},{2,7},{15,8},{12,9},{13,... | collective-permute-start | bytes 786440 | tf_op jit(solution)/shard_map/scatter_aggregate/ppermute | solution.py:34
  50.5 3.3 %collective-permute-start.19 = (bf16[1024,128]{1,0:T(8,128)(2,1)}, bf16[1024,128]{1,0:T(8,128)(2,1)S(1)}, u32[]{:S(2)}, u32[]{:S(2)}) collective-permute-start(bf16[1024,128]{1,0:T(8,128)(2,1)} %get-tuple-element.73), channel_id=1, source_target_pairs={{5,0},{6,1},{7,2},{4,3},{1,4},{2,5},{3,6},{0,7},{13,8},{14,9},{15,... | collective-permute-start | bytes 786440 | tf_op jit(solution)/shard_map/scatter_aggregate/ppermute | solution.py:34
  53.8 0.8 collective-permute-start.20
  54.6 0.9 collective-permute-done.16.r2
  55.5 3.9 %collective-permute-start.21 = (bf16[1024,128]{1,0:T(8,128)(2,1)}, bf16[1024,128]{1,0:T(8,128)(2,1)S(1)}, u32[]{:S(2)}, u32[]{:S(2)}) collective-permute-start(bf16[1024,128]{1,0:T(8,128)(2,1)} %get-tuple-element.75), channel_id=1, source_target_pairs={{1,0},{2,1},{3,2},{0,3},{5,4},{6,5},{7,6},{4,7},{9,8},{10,9},{11,1... | collective-permute-start | bytes 786440 | tf_op jit(solution)/shard_map/scatter_aggregate/ppermute | solution.py:34
  59.4 9.0 %collective-permute-done.17.r3 = bf16[1024,128]{1,0:T(8,128)(2,1)S(1)} collective-permute-done((bf16[1024,128]{1,0:T(8,128)(2,1)}, bf16[1024,128]{1,0:T(8,128)(2,1)S(1)}, u32[]{:S(2)}, u32[]{:S(2)}) %collective-permute-start.17) | collective-permute-done | bytes 262176 | tf_op jit(solution)/shard_map/scatter_aggregate/ppermute | solution.py:34
  68.5 6.0 %collective-permute-done.20.r6 = bf16[1024,128]{1,0:T(8,128)(2,1)S(1)} collective-permute-done((bf16[1024,128]{1,0:T(8,128)(2,1)}, bf16[1024,128]{1,0:T(8,128)(2,1)S(1)}, u32[]{:S(2)}, u32[]{:S(2)}) %collective-permute-start.20) | collective-permute-done | bytes 262176 | tf_op jit(solution)/shard_map/scatter_aggregate/ppermute | solution.py:34
  74.6 0.6 copy-done.36
  75.3 3.5 %dense.1 = (bf16[1024,256]{1,0:T(8,128)(2,1)}, bf16[1024,128]{1,0:T(8,128)(2,1)}, bf16[1024,256]{1,0:T(8,128)(2,1)}, bf16[8,128,128]{2,1,0:T(8,128)(2,1)}) custom-call(bf16[1024,128]{1,0:T(8,128)(2,1)} %get-tuple-element.68.own, bf16[1024,128]{1,0:T(8,128)(2,1)} %copy-done.31, bf16[1024,128]{1,0:T(8,128)(2,1)} %copy-done.32, bf16[1024,128]{1,0:T(8,128)(2,1)} %copy-done.33, ...), custom_call_target="tpu_custom_call" | custom-call | tf_op jit(solution)/shard_map/dense/dense/pallas_call | solution.py:343
  78.9 3.2 %collective-permute-start.24 = (bf16[8,128,128]{2,1,0:T(8,128)(2,1)}, bf16[8,128,128]{2,1,0:T(8,128)(2,1)S(1)}, u32[]{:S(2)}, u32[]{:S(2)}) collective-permute-start(bf16[8,128,128]{2,1,0:T(8,128)(2,1)} %get-tuple-element.85.refs_0_), channel_id=1, source_target_pairs={{1,0},{2,1},{3,2},{0,3},{5,4},{6,5},{7,6},{4,7},{9,8},{10,9},{11,1... | collective-permute-start | bytes 786440 | tf_op jit(solution)/shard_map/gather_gradients/ppermute | solution.py:34
  82.1 2.3 %collective-permute-start.22 = (bf16[8,128,128]{2,1,0:T(8,128)(2,1)}, bf16[8,128,128]{2,1,0:T(8,128)(2,1)S(1)}, u32[]{:S(2)}, u32[]{:S(2)}) collective-permute-start(bf16[8,128,128]{2,1,0:T(8,128)(2,1)} %get-tuple-element.85.refs_0_), channel_id=1, source_target_pairs={{4,0},{5,1},{6,2},{7,3},{0,4},{1,5},{2,6},{3,7},{12,8},{13,9},{14,... | collective-permute-start | bytes 786440 | tf_op jit(solution)/shard_map/gather_gradients/ppermute | solution.py:34
  84.4 2.5 %weight_gradients.1 = (f32[4,72,256]{2,1,0:T(8,128)}, f32[1024,128]{1,0:T(8,128)}) custom-call(s32[4]{0:T(128)} %pad_add_fusion.meta.refs_0_, bf16[1024,128]{1,0:T(8,128)(2,1)} %refs_1_.1, bf16[1024,128]{1,0:T(8,128)(2,1)} %get-tuple-element.82.refs_2_, bf16[1024,256]{1,0:T(8,128)(2,1)} %get-tuple-element.83.refs_3_, bf16[128,256]{1,0:T(8,128)(2,1)} %refs_4_.1), custom_call_target="tpu_custom_call" | custom-call | flops 201326592 | bytes 2097152 | tf_op jit(solution)/shard_map/weight_gradients/weight_gradients/pallas_call | solution.py:368
  86.9 1.0 slice_bitcast_fusion.1
  87.9 3.6 %collective-permute-start.30 = (f32[72,256]{1,0:T(8,128)S(1)}, f32[72,256]{1,0:T(8,128)S(1)}, u32[]{:S(2)}, u32[]{:S(2)}) collective-permute-start(f32[72,256]{1,0:T(8,128)S(1)} %get-tuple-element.126), channel_id=1, source_target_pairs={{2,0},{3,1},{0,2},{1,3},{6,4},{7,5},{4,6},{5,7},{10,8},{11,9},{8,1... | collective-permute-start | bytes 221192 | tf_op jit(solution)/shard_map/weight_gradients/ppermute | solution.py:34
  91.5 4.3 %collective-permute-done.25.refs_3_ = bf16[8,128,128]{2,1,0:T(8,128)(2,1)S(1)} collective-permute-done((bf16[8,128,128]{2,1,0:T(8,128)(2,1)}, bf16[8,128,128]{2,1,0:T(8,128)(2,1)S(1)}, u32[]{:S(2)}, u32[]{:S(2)}) %collective-permute-start.25) | collective-permute-done | bytes 262176 | tf_op jit(solution)/shard_map/gather_gradients/ppermute | solution.py:34
  96.0 1.9 %collective-permute-start.29 = (f32[72,256]{1,0:T(8,128)S(1)}, f32[72,256]{1,0:T(8,128)S(1)}, u32[]{:S(2)}, u32[]{:S(2)}) collective-permute-start(f32[72,256]{1,0:T(8,128)S(1)} %get-tuple-element.128), channel_id=1, source_target_pairs={{3,0},{0,1},{1,2},{2,3},{7,4},{4,5},{5,6},{6,7},{11,8},{8,9},{9,10... | collective-permute-start | bytes 221192 | tf_op jit(solution)/shard_map/weight_gradients/ppermute | solution.py:34
  97.8 2.5 %collective-permute-start.27 = (bf16[8,128,128]{2,1,0:T(8,128)(2,1)S(1)}, bf16[8,128,128]{2,1,0:T(8,128)(2,1)S(1)}, u32[]{:S(2)}, u32[]{:S(2)}) collective-permute-start(bf16[8,128,128]{2,1,0:T(8,128)(2,1)S(1)} %collective-permute-done.23.refs_2_), channel_id=1, source_target_pairs={{4,0},{5,1},{6,2},{7,3},{0,4},{1,5},{2,6},{3,7},{12,8},{13,9},{14,... | collective-permute-start | bytes 786440 | tf_op jit(solution)/shard_map/gather_gradients/ppermute | solution.py:34
  100.4 3.2 %collective-permute-start.26 = (bf16[8,128,128]{2,1,0:T(8,128)(2,1)S(1)}, bf16[8,128,128]{2,1,0:T(8,128)(2,1)S(1)}, u32[]{:S(2)}, u32[]{:S(2)}) collective-permute-start(bf16[8,128,128]{2,1,0:T(8,128)(2,1)S(1)} %collective-permute-done.22.refs_4_), channel_id=1, source_target_pairs={{1,0},{2,1},{3,2},{0,3},{5,4},{6,5},{7,6},{4,7},{9,8},{10,9},{11,1... | collective-permute-start | bytes 786440 | tf_op jit(solution)/shard_map/gather_gradients/ppermute | solution.py:34
  103.6 0.9 bitcast_add_fusion
  104.5 2.3 %collective-permute-done.27.refs_6_ = bf16[8,128,128]{2,1,0:T(8,128)(2,1)S(1)} collective-permute-done((bf16[8,128,128]{2,1,0:T(8,128)(2,1)S(1)}, bf16[8,128,128]{2,1,0:T(8,128)(2,1)S(1)}, u32[]{:S(2)}, u32[]{:S(2)}) %collective-permute-start.27) | collective-permute-done | bytes 262176 | tf_op jit(solution)/shard_map/gather_gradients/ppermute | solution.py:34
  106.8 2.7 %collective-permute-done.28.refs_7_ = bf16[8,128,128]{2,1,0:T(8,128)(2,1)S(1)} collective-permute-done((bf16[8,128,128]{2,1,0:T(8,128)(2,1)S(1)}, bf16[8,128,128]{2,1,0:T(8,128)(2,1)S(1)}, u32[]{:S(2)}, u32[]{:S(2)}) %collective-permute-start.28) | collective-permute-done | bytes 262176 | tf_op jit(solution)/shard_map/gather_gradients/ppermute | solution.py:34
  109.5 0.7 collective-permute-start.32
  110.3 7.8 %column_gradients.1 = (bf16[8,8,128,128]{3,2,1,0:T(8,128)(2,1)}, bf16[8,8,128,128]{3,2,1,0:T(8,128)(2,1)}) custom-call(s32[4]{0:T(128)} %pad_add_fusion.meta.refs_0_, s32[512]{0:T(512)} %cols.3, s32[3,320]{1,0:T(4,128)} %get-tuple-element.62.pairs, s32[1]{0:T(128)} %get-tuple-element.63.total, bf16[512,128,128]{2,1,0:T(8,128)(2,1)} %tiles_hbm.3, ...), custom_call_target="tpu_custom_call" | custom-call | flops 2147483648 | bytes 23068672 | tf_op jit(solution)/shard_map/column_gradients/column_gradients/pallas_call | solution.py:393
  118.2 3.0 %collective-permute-start.33 = (bf16[8,8,128,128]{3,2,1,0:T(8,128)(2,1)}, bf16[8,8,128,128]{3,2,1,0:T(8,128)(2,1)S(1)}, u32[]{:S(2)}, u32[]{:S(2)}) collective-permute-start(bf16[8,8,128,128]{3,2,1,0:T(8,128)(2,1)} %get-tuple-element.97), channel_id=1, source_target_pairs={{8,0},{0,8},{24,16},{16,24},{40,32},{32,40},{56,48},{48,56},{72,64... | collective-permute-start | bytes 6291464 | tf_op jit(solution)/shard_map/scatter_gradients/ppermute | solution.py:30
  121.2 1.6 collective-permute-start.36
  123.1 2.4 %collective-permute-done.36 = f32[72,256]{1,0:T(8,128)S(1)} collective-permute-done((f32[72,256]{1,0:T(8,128)S(1)}, f32[72,256]{1,0:T(8,128)S(1)}, u32[]{:S(2)}, u32[]{:S(2)}) %collective-permute-start.36) | collective-permute-done | bytes 73760 | tf_op jit(solution)/shard_map/scatter_gradients/ppermute | solution.py:30
  125.5 1.9 %collective-permute-done.35 = f32[72,256]{1,0:T(8,128)S(1)} collective-permute-done((f32[72,256]{1,0:T(8,128)S(1)}, f32[72,256]{1,0:T(8,128)S(1)}, u32[]{:S(2)}, u32[]{:S(2)}) %collective-permute-start.35) | collective-permute-done | bytes 73760 | tf_op jit(solution)/shard_map/scatter_gradients/ppermute | solution.py:30
  127.4 2.8 %fusion.6 = (bf16[8,128,128]{2,1,0:T(8,128)(2,1)S(1)}, bf16[8,128,128]{2,1,0:T(8,128)(2,1)S(1)}, bf16[8,128,128]{2,1,0:T(8,128)(2,1)S(1)}, bf16[8,128,128]{2,1,0...) fusion(bf16[8,8,128,128]{3,2,1,0:T(8,128)(2,1)S(1)} %collective, ...), kind=kLoop, calls=%fused_computation.13 | loop fusion | flops 3670016 | bytes 5505024 | tf_op jit(solution)/shard_map/scatter_gradients/convert_element_type | solution.py:426
  130.3 5.1 %collective-permute-start.42 = (f32[72,256]{1,0:T(8,128)S(1)}, f32[72,256]{1,0:T(8,128)S(1)}, u32[]{:S(2)}, u32[]{:S(2)}) collective-permute-start(f32[72,256]{1,0:T(8,128)S(1)} %add_add_fusion.1), channel_id=1, source_target_pairs={{32,0},{40,8},{48,16},{56,24},{0,32},{8,40},{16,48},{24,56},{96,64... | collective-permute-start | bytes 221192 | tf_op jit(solution)/shard_map/scatter_gradients/ppermute | solution.py:30
  135.5 2.5 %collective-permute-start.41 = (f32[72,256]{1,0:T(8,128)S(1)}, f32[72,256]{1,0:T(8,128)S(1)}, u32[]{:S(2)}, u32[]{:S(2)}) collective-permute-start(f32[72,256]{1,0:T(8,128)S(1)} %add_add_fusion.1), channel_id=1, source_target_pairs={{16,0},{24,8},{32,16},{40,24},{48,32},{56,40},{0,48},{8,56},{80,64... | collective-permute-start | bytes 221192 | tf_op jit(solution)/shard_map/scatter_gradients/ppermute | solution.py:30
  138.0 1.7 collective-permute-start.38
  140.0 4.4 %collective-permute-start.46 = (f32[72,256]{1,0:T(8,128)S(1)}, f32[72,256]{1,0:T(8,128)S(1)}, u32[]{:S(2)}, u32[]{:S(2)}) collective-permute-start(f32[72,256]{1,0:T(8,128)S(1)} %add_add_fusion.s0), channel_id=1, source_target_pairs={{3,0},{0,1},{1,2},{2,3},{7,4},{4,5},{5,6},{6,7},{11,8},{8,9},{9,10... | collective-permute-start | bytes 221192 | tf_op jit(solution)/shard_map/scatter_gradients/ppermute | solution.py:34
  144.5 1.3 collective-permute-start.45
  145.8 1.5 collective-permute-start.44
  147.2 3.1 %collective-permute-done.45.s2 = f32[72,256]{1,0:T(8,128)S(1)} collective-permute-done((f32[72,256]{1,0:T(8,128)S(1)}, f32[72,256]{1,0:T(8,128)S(1)}, u32[]{:S(2)}, u32[]{:S(2)}) %collective-permute-start.45) | collective-permute-done | bytes 73760 | tf_op jit(solution)/shard_map/scatter_gradients/ppermute | solution.py:34
  150.3 1.5 collective-permute-start.40
  151.8 0.8 collective-permute-start.47
  152.7 1.3 collective-permute-start.48
  153.9 2.9 %collective-permute-start.49 = (bf16[8,128,128]{2,1,0:T(8,128)(2,1)S(1)}, bf16[8,128,128]{2,1,0:T(8,128)(2,1)S(1)}, u32[]{:S(2)}, u32[]{:S(2)}) collective-permute-start(bf16[8,128,128]{2,1,0:T(8,128)(2,1)S(1)} %get-tuple-element.109), channel_id=1, source_target_pairs={{80,0},{88,8},{96,16},{104,24},{112,32},{120,40},{64,48},{72,56},{... | collective-permute-start | bytes 786440 | tf_op jit(solution)/shard_map/scatter_gradients/ppermute | solution.py:30
  156.8 9.7 %collective-permute-done.40.r2 = bf16[8,128,128]{2,1,0:T(8,128)(2,1)S(1)} collective-permute-done((bf16[8,128,128]{2,1,0:T(8,128)(2,1)S(1)}, bf16[8,128,128]{2,1,0:T(8,128)(2,1)S(1)}, u32[]{:S(2)}, u32[]{:S(2)}) %collective-permute-start.40) | collective-permute-done | bytes 262176 | tf_op jit(solution)/shard_map/scatter_gradients/ppermute | solution.py:30
  166.5 1.6 collective-permute-done.47.r3
  168.2 0.6 copy-done.28
  169.0 3.0 %grad_input.1 = (bf16[1024,128]{1,0:T(8,128)(2,1)}, f32[128,256]{1,0:T(8,128)}, f32[128,256]{1,0:T(8,128)}, f32[1,256]{1,0:T(1,128)}) custom-call(s32[4]{0:T(128)} %pad_add_fusion.meta.refs_0_, bf16[8,8,128,128]{3,2,1,0:T(8,128)(2,1)} %get-tuple-element.96.keep, bf16[8,8,128,128]{3,2,1,0:T(8,128)(2,1)} %copy-done, bf16[8,128,128]{2,1,0:T(8,128)(2,1)} %copy-done.26, ...), custom_call_target="tpu_custom_call" | custom-call | tf_op jit(solution)/shard_map/grad_input/grad_input/pallas_call | solution.py:443
  (131 shorter events, 2.2 us)
Async XLA Ops:
  0.6 10.1 %collective-permute-start.3 = (bf16[1024,128]{1,0:T(8,128)(2,1)}, bf16[1024,128]{1,0:T(8,128)(2,1)S(1)}, u32[]{:S(2)}, u32[]{:S(2)}) collective-permute-start(bf16[1024,128]{1,0:T(8,128)(2,1)} %refs_1_.1), channel_id=1, source_target_pairs={{48,0},{56,8},{0,16},{8,24},{16,32},{24,40},{32,48},{40,56},{112,6... | collective-permute-start | bytes 786440 | tf_op jit(solution)/shard_map/gather_features/ppermute | solution.py:30
  2.4 13.1 %collective-permute-start.2 = (bf16[1024,128]{1,0:T(8,128)(2,1)}, bf16[1024,128]{1,0:T(8,128)(2,1)S(1)}, u32[]{:S(2)}, u32[]{:S(2)}) collective-permute-start(bf16[1024,128]{1,0:T(8,128)(2,1)} %refs_1_.1), channel_id=1, source_target_pairs={{16,0},{24,8},{32,16},{40,24},{48,32},{56,40},{0,48},{8,56},{80,64... | collective-permute-start | bytes 786440 | tf_op jit(solution)/shard_map/gather_features/ppermute | solution.py:30
  3.9 13.2 %collective-permute-start.1 = (bf16[1024,128]{1,0:T(8,128)(2,1)}, bf16[1024,128]{1,0:T(8,128)(2,1)S(1)}, u32[]{:S(2)}, u32[]{:S(2)}) collective-permute-start(bf16[1024,128]{1,0:T(8,128)(2,1)} %refs_1_.1), channel_id=1, source_target_pairs={{32,0},{40,8},{48,16},{56,24},{0,32},{8,40},{16,48},{24,56},{96,64... | collective-permute-start | bytes 786440 | tf_op jit(solution)/shard_map/gather_features/ppermute | solution.py:30
  6.0 11.1 %collective-permute-start = (bf16[1024,128]{1,0:T(8,128)(2,1)}, bf16[1024,128]{1,0:T(8,128)(2,1)S(1)}, u32[]{:S(2)}, u32[]{:S(2)}) collective-permute-start(bf16[1024,128]{1,0:T(8,128)(2,1)} %refs_1_.1), channel_id=1, source_target_pairs={{64,0},{72,8},{80,16},{88,24},{96,32},{104,40},{112,48},{120,56},{... | collective-permute-start | bytes 786440 | tf_op jit(solution)/shard_map/gather_features/ppermute | solution.py:30
  7.5 12.8 %collective-permute-start.7 = (bf16[1024,128]{1,0:T(8,128)(2,1)}, bf16[1024,128]{1,0:T(8,128)(2,1)S(1)}, u32[]{:S(2)}, u32[]{:S(2)}) collective-permute-start(bf16[1024,128]{1,0:T(8,128)(2,1)} %refs_1_.1), channel_id=1, source_target_pairs={{8,0},{0,8},{24,16},{16,24},{40,32},{32,40},{56,48},{48,56},{72,64... | collective-permute-start | bytes 786440 | tf_op jit(solution)/shard_map/gather_features/ppermute | solution.py:30
  10.7 19.6 %copy-start.2 = (bf16[1024,128]{1,0:T(8,128)(2,1)}, bf16[1024,128]{1,0:T(8,128)(2,1)S(1)}, u32[]{:S(2)}) copy-start(bf16[1024,128]{1,0:T(8,128)(2,1)S(1)} %collective-permute-done.3.refs_3_) | copy-start | bytes 786436
  15.4 14.9 %copy-start.3 = (bf16[1024,128]{1,0:T(8,128)(2,1)}, bf16[1024,128]{1,0:T(8,128)(2,1)S(1)}, u32[]{:S(2)}) copy-start(bf16[1024,128]{1,0:T(8,128)(2,1)S(1)} %collective-permute-done.2.refs_1_) | copy-start | bytes 786436
  17.1 13.2 %copy-start.4 = (bf16[1024,128]{1,0:T(8,128)(2,1)}, bf16[1024,128]{1,0:T(8,128)(2,1)S(1)}, u32[]{:S(2)}) copy-start(bf16[1024,128]{1,0:T(8,128)(2,1)S(1)} %collective-permute-done.1.refs_2_) | copy-start | bytes 786436
  17.1 13.2 %copy-start.5 = (bf16[1024,128]{1,0:T(8,128)(2,1)}, bf16[1024,128]{1,0:T(8,128)(2,1)S(1)}, u32[]{:S(2)}) copy-start(bf16[1024,128]{1,0:T(8,128)(2,1)S(1)} %collective-permute-done.refs_4_) | copy-start | bytes 786436
  17.1 5.3 %collective-permute-start.8 = (bf16[1024,128]{1,0:T(8,128)(2,1)S(1)}, bf16[1024,128]{1,0:T(8,128)(2,1)S(1)}, u32[]{:S(2)}, u32[]{:S(2)}) collective-permute-start(bf16[1024,128]{1,0:T(8,128)(2,1)S(1)} %collective-permute-done.2.refs_1_), channel_id=1, source_target_pairs={{8,0},{0,8},{24,16},{16,24},{40,32},{32,40},{56,48},{48,56},{72,64... | collective-permute-start | bytes 786440 | tf_op jit(solution)/shard_map/gather_features/ppermute | solution.py:30
  17.2 5.2 %collective-permute-start.10 = (bf16[1024,128]{1,0:T(8,128)(2,1)S(1)}, bf16[1024,128]{1,0:T(8,128)(2,1)S(1)}, u32[]{:S(2)}, u32[]{:S(2)}) collective-permute-start(bf16[1024,128]{1,0:T(8,128)(2,1)S(1)} %collective-permute-done.3.refs_3_), channel_id=1, source_target_pairs={{8,0},{0,8},{24,16},{16,24},{40,32},{32,40},{56,48},{48,56},{72,64... | collective-permute-start | bytes 786440 | tf_op jit(solution)/shard_map/gather_features/ppermute | solution.py:30
  17.7 8.3 %collective-permute-start.5 = (bf16[1024,128]{1,0:T(8,128)(2,1)S(1)}, bf16[1024,128]{1,0:T(8,128)(2,1)S(1)}, u32[]{:S(2)}, u32[]{:S(2)}) collective-permute-start(bf16[1024,128]{1,0:T(8,128)(2,1)S(1)} %collective-permute-done.1.refs_2_), channel_id=1, source_target_pairs={{64,0},{72,8},{80,16},{88,24},{96,32},{104,40},{112,48},{120,56},{... | collective-permute-start | bytes 786440 | tf_op jit(solution)/shard_map/gather_features/ppermute | solution.py:30
  19.2 9.2 %collective-permute-start.6 = (bf16[1024,128]{1,0:T(8,128)(2,1)S(1)}, bf16[1024,128]{1,0:T(8,128)(2,1)S(1)}, u32[]{:S(2)}, u32[]{:S(2)}) collective-permute-start(bf16[1024,128]{1,0:T(8,128)(2,1)S(1)} %collective-permute-done.refs_4_), channel_id=1, source_target_pairs={{48,0},{56,8},{0,16},{8,24},{16,32},{24,40},{32,48},{40,56},{112,6... | collective-permute-start | bytes 786440 | tf_op jit(solution)/shard_map/gather_features/ppermute | solution.py:30
  20.3 8.1 %collective-permute-start.4 = (bf16[1024,128]{1,0:T(8,128)(2,1)S(1)}, bf16[1024,128]{1,0:T(8,128)(2,1)S(1)}, u32[]{:S(2)}, u32[]{:S(2)}) collective-permute-start(bf16[1024,128]{1,0:T(8,128)(2,1)S(1)} %collective-permute-done.refs_4_), channel_id=1, source_target_pairs={{16,0},{24,8},{32,16},{40,24},{48,32},{56,40},{0,48},{8,56},{80,64... | collective-permute-start | bytes 786440 | tf_op jit(solution)/shard_map/gather_features/ppermute | solution.py:30
  22.4 6.5 %collective-permute-start.9 = (bf16[1024,128]{1,0:T(8,128)(2,1)S(1)}, bf16[1024,128]{1,0:T(8,128)(2,1)S(1)}, u32[]{:S(2)}, u32[]{:S(2)}) collective-permute-start(bf16[1024,128]{1,0:T(8,128)(2,1)S(1)} %collective-permute-done.1.refs_2_), channel_id=1, source_target_pairs={{8,0},{0,8},{24,16},{16,24},{40,32},{32,40},{56,48},{48,56},{72,64... | collective-permute-start | bytes 786440 | tf_op jit(solution)/shard_map/gather_features/ppermute | solution.py:30
  22.5 6.5 %collective-permute-start.11 = (bf16[1024,128]{1,0:T(8,128)(2,1)S(1)}, bf16[1024,128]{1,0:T(8,128)(2,1)S(1)}, u32[]{:S(2)}, u32[]{:S(2)}) collective-permute-start(bf16[1024,128]{1,0:T(8,128)(2,1)S(1)} %collective-permute-done.refs_4_), channel_id=1, source_target_pairs={{8,0},{0,8},{24,16},{16,24},{40,32},{32,40},{56,48},{48,56},{72,64... | collective-permute-start | bytes 786440 | tf_op jit(solution)/shard_map/gather_features/ppermute | solution.py:30
  26.0 3.0 %collective-permute-start.13 = (bf16[1024,128]{1,0:T(8,128)(2,1)S(1)}, bf16[1024,128]{1,0:T(8,128)(2,1)S(1)}, u32[]{:S(2)}, u32[]{:S(2)}) collective-permute-start(bf16[1024,128]{1,0:T(8,128)(2,1)S(1)} %collective-permute-done.5.refs_6_), channel_id=1, source_target_pairs={{8,0},{0,8},{24,16},{16,24},{40,32},{32,40},{56,48},{48,56},{72,64... | collective-permute-start | bytes 786440 | tf_op jit(solution)/shard_map/gather_features/ppermute | solution.py:30
  28.4 1.5 collective-permute-start.14
  28.4 1.9 %collective-permute-start.12 = (bf16[1024,128]{1,0:T(8,128)(2,1)S(1)}, bf16[1024,128]{1,0:T(8,128)(2,1)S(1)}, u32[]{:S(2)}, u32[]{:S(2)}) collective-permute-start(bf16[1024,128]{1,0:T(8,128)(2,1)S(1)} %collective-permute-done.4.refs_5_), channel_id=1, source_target_pairs={{8,0},{0,8},{24,16},{16,24},{40,32},{32,40},{56,48},{48,56},{72,64... | collective-permute-start | bytes 786440 | tf_op jit(solution)/shard_map/gather_features/ppermute | solution.py:30
  38.8 15.0 %collective-permute-start.15 = (bf16[1024,128]{1,0:T(8,128)(2,1)}, bf16[1024,128]{1,0:T(8,128)(2,1)S(1)}, u32[]{:S(2)}, u32[]{:S(2)}) collective-permute-start(bf16[1024,128]{1,0:T(8,128)(2,1)} %get-tuple-element.69), channel_id=1, source_target_pairs={{6,0},{7,1},{4,2},{5,3},{2,4},{3,5},{0,6},{1,7},{14,8},{15,9},{12,... | collective-permute-start | bytes 786440 | tf_op jit(solution)/shard_map/scatter_aggregate/ppermute | solution.py:34
  44.9 10.6 %collective-permute-start.16 = (bf16[1024,128]{1,0:T(8,128)(2,1)}, bf16[1024,128]{1,0:T(8,128)(2,1)S(1)}, u32[]{:S(2)}, u32[]{:S(2)}) collective-permute-start(bf16[1024,128]{1,0:T(8,128)(2,1)} %get-tuple-element.70), channel_id=1, source_target_pairs={{4,0},{5,1},{6,2},{7,3},{0,4},{1,5},{2,6},{3,7},{12,8},{13,9},{14,... | collective-permute-start | bytes 786440 | tf_op jit(solution)/shard_map/scatter_aggregate/ppermute | solution.py:34
  48.2 20.3 %collective-permute-start.17 = (bf16[1024,128]{1,0:T(8,128)(2,1)}, bf16[1024,128]{1,0:T(8,128)(2,1)S(1)}, u32[]{:S(2)}, u32[]{:S(2)}) collective-permute-start(bf16[1024,128]{1,0:T(8,128)(2,1)} %get-tuple-element.71), channel_id=1, source_target_pairs={{2,0},{3,1},{0,2},{1,3},{6,4},{7,5},{4,6},{5,7},{10,8},{11,9},{8,1... | collective-permute-start | bytes 786440 | tf_op jit(solution)/shard_map/scatter_aggregate/ppermute | solution.py:34
  48.2 20.3 %collective-permute-start.18 = (bf16[1024,128]{1,0:T(8,128)(2,1)}, bf16[1024,128]{1,0:T(8,128)(2,1)S(1)}, u32[]{:S(2)}, u32[]{:S(2)}) collective-permute-start(bf16[1024,128]{1,0:T(8,128)(2,1)} %get-tuple-element.72), channel_id=1, source_target_pairs={{7,0},{4,1},{5,2},{6,3},{3,4},{0,5},{1,6},{2,7},{15,8},{12,9},{13,... | collective-permute-start | bytes 786440 | tf_op jit(solution)/shard_map/scatter_aggregate/ppermute | solution.py:34
  50.5 18.0 %collective-permute-start.19 = (bf16[1024,128]{1,0:T(8,128)(2,1)}, bf16[1024,128]{1,0:T(8,128)(2,1)S(1)}, u32[]{:S(2)}, u32[]{:S(2)}) collective-permute-start(bf16[1024,128]{1,0:T(8,128)(2,1)} %get-tuple-element.73), channel_id=1, source_target_pairs={{5,0},{6,1},{7,2},{4,3},{1,4},{2,5},{3,6},{0,7},{13,8},{14,9},{15,... | collective-permute-start | bytes 786440 | tf_op jit(solution)/shard_map/scatter_aggregate/ppermute | solution.py:34
  53.8 20.7 %copy-start.31 = (bf16[1024,128]{1,0:T(8,128)(2,1)}, bf16[1024,128]{1,0:T(8,128)(2,1)S(1)}, u32[]{:S(2)}) copy-start(bf16[1024,128]{1,0:T(8,128)(2,1)S(1)} %collective-permute-done.15.r1) | copy-start | bytes 786436
  53.8 20.7 %collective-permute-start.20 = (bf16[1024,128]{1,0:T(8,128)(2,1)}, bf16[1024,128]{1,0:T(8,128)(2,1)S(1)}, u32[]{:S(2)}, u32[]{:S(2)}) collective-permute-start(bf16[1024,128]{1,0:T(8,128)(2,1)} %get-tuple-element.74), channel_id=1, source_target_pairs={{3,0},{0,1},{1,2},{2,3},{7,4},{4,5},{5,6},{6,7},{11,8},{8,9},{9,10... | collective-permute-start | bytes 786440 | tf_op jit(solution)/shard_map/scatter_aggregate/ppermute | solution.py:34
  55.5 19.0 %copy-start.32 = (bf16[1024,128]{1,0:T(8,128)(2,1)}, bf16[1024,128]{1,0:T(8,128)(2,1)S(1)}, u32[]{:S(2)}) copy-start(bf16[1024,128]{1,0:T(8,128)(2,1)S(1)} %collective-permute-done.16.r2) | copy-start | bytes 786436
  55.5 19.0 %collective-permute-start.21 = (bf16[1024,128]{1,0:T(8,128)(2,1)}, bf16[1024,128]{1,0:T(8,128)(2,1)S(1)}, u32[]{:S(2)}, u32[]{:S(2)}) collective-permute-start(bf16[1024,128]{1,0:T(8,128)(2,1)} %get-tuple-element.75), channel_id=1, source_target_pairs={{1,0},{2,1},{3,2},{0,3},{5,4},{6,5},{7,6},{4,7},{9,8},{10,9},{11,1... | collective-permute-start | bytes 786440 | tf_op jit(solution)/shard_map/scatter_aggregate/ppermute | solution.py:34
  78.8 17.0 %collective-permute-start.25 = (bf16[8,128,128]{2,1,0:T(8,128)(2,1)}, bf16[8,128,128]{2,1,0:T(8,128)(2,1)S(1)}, u32[]{:S(2)}, u32[]{:S(2)}) collective-permute-start(bf16[8,128,128]{2,1,0:T(8,128)(2,1)} %get-tuple-element.85.refs_0_), channel_id=1, source_target_pairs={{3,0},{0,1},{1,2},{2,3},{7,4},{4,5},{5,6},{6,7},{11,8},{8,9},{9,10... | collective-permute-start | bytes 786440 | tf_op jit(solution)/shard_map/gather_gradients/ppermute | solution.py:34
  78.9 17.1 %collective-permute-start.24 = (bf16[8,128,128]{2,1,0:T(8,128)(2,1)}, bf16[8,128,128]{2,1,0:T(8,128)(2,1)S(1)}, u32[]{:S(2)}, u32[]{:S(2)}) collective-permute-start(bf16[8,128,128]{2,1,0:T(8,128)(2,1)} %get-tuple-element.85.refs_0_), channel_id=1, source_target_pairs={{1,0},{2,1},{3,2},{0,3},{5,4},{6,5},{7,6},{4,7},{9,8},{10,9},{11,1... | collective-permute-start | bytes 786440 | tf_op jit(solution)/shard_map/gather_gradients/ppermute | solution.py:34
  82.1 15.7 %collective-permute-start.23 = (bf16[8,128,128]{2,1,0:T(8,128)(2,1)}, bf16[8,128,128]{2,1,0:T(8,128)(2,1)S(1)}, u32[]{:S(2)}, u32[]{:S(2)}) collective-permute-start(bf16[8,128,128]{2,1,0:T(8,128)(2,1)} %get-tuple-element.85.refs_0_), channel_id=1, source_target_pairs={{2,0},{3,1},{0,2},{1,3},{6,4},{7,5},{4,6},{5,7},{10,8},{11,9},{8,1... | collective-permute-start | bytes 786440 | tf_op jit(solution)/shard_map/gather_gradients/ppermute | solution.py:34
  82.1 15.7 %collective-permute-start.22 = (bf16[8,128,128]{2,1,0:T(8,128)(2,1)}, bf16[8,128,128]{2,1,0:T(8,128)(2,1)S(1)}, u32[]{:S(2)}, u32[]{:S(2)}) collective-permute-start(bf16[8,128,128]{2,1,0:T(8,128)(2,1)} %get-tuple-element.85.refs_0_), channel_id=1, source_target_pairs={{4,0},{5,1},{6,2},{7,3},{0,4},{1,5},{2,6},{3,7},{12,8},{13,9},{14,... | collective-permute-start | bytes 786440 | tf_op jit(solution)/shard_map/gather_gradients/ppermute | solution.py:34
  87.9 12.5 %collective-permute-start.30 = (f32[72,256]{1,0:T(8,128)S(1)}, f32[72,256]{1,0:T(8,128)S(1)}, u32[]{:S(2)}, u32[]{:S(2)}) collective-permute-start(f32[72,256]{1,0:T(8,128)S(1)} %get-tuple-element.126), channel_id=1, source_target_pairs={{2,0},{3,1},{0,2},{1,3},{6,4},{7,5},{4,6},{5,7},{10,8},{11,9},{8,1... | collective-permute-start | bytes 221192 | tf_op jit(solution)/shard_map/weight_gradients/ppermute | solution.py:34
  95.8 14.4 %copy-start.7 = (bf16[8,128,128]{2,1,0:T(8,128)(2,1)}, bf16[8,128,128]{2,1,0:T(8,128)(2,1)S(1)}, u32[]{:S(2)}) copy-start(bf16[8,128,128]{2,1,0:T(8,128)(2,1)S(1)} %collective-permute-done.25.refs_3_) | copy-start | bytes 786436
  95.8 7.8 %collective-permute-start.31 = (f32[72,256]{1,0:T(8,128)S(1)}, f32[72,256]{1,0:T(8,128)S(1)}, u32[]{:S(2)}, u32[]{:S(2)}) collective-permute-start(f32[72,256]{1,0:T(8,128)S(1)} %get-tuple-element.127), channel_id=1, source_target_pairs={{1,0},{2,1},{3,2},{0,3},{5,4},{6,5},{7,6},{4,7},{9,8},{10,9},{11,1... | collective-permute-start | bytes 221192 | tf_op jit(solution)/shard_map/weight_gradients/ppermute | solution.py:34
  95.9 14.2 %copy-start.8 = (bf16[8,128,128]{2,1,0:T(8,128)(2,1)}, bf16[8,128,128]{2,1,0:T(8,128)(2,1)S(1)}, u32[]{:S(2)}) copy-start(bf16[8,128,128]{2,1,0:T(8,128)(2,1)S(1)} %collective-permute-done.24.refs_1_) | copy-start | bytes 786436
  96.0 7.7 %collective-permute-start.29 = (f32[72,256]{1,0:T(8,128)S(1)}, f32[72,256]{1,0:T(8,128)S(1)}, u32[]{:S(2)}, u32[]{:S(2)}) collective-permute-start(f32[72,256]{1,0:T(8,128)S(1)} %get-tuple-element.128), channel_id=1, source_target_pairs={{3,0},{0,1},{1,2},{2,3},{7,4},{4,5},{5,6},{6,7},{11,8},{8,9},{9,10... | collective-permute-start | bytes 221192 | tf_op jit(solution)/shard_map/weight_gradients/ppermute | solution.py:34
  97.8 9.0 %collective-permute-start.27 = (bf16[8,128,128]{2,1,0:T(8,128)(2,1)S(1)}, bf16[8,128,128]{2,1,0:T(8,128)(2,1)S(1)}, u32[]{:S(2)}, u32[]{:S(2)}) collective-permute-start(bf16[8,128,128]{2,1,0:T(8,128)(2,1)S(1)} %collective-permute-done.23.refs_2_), channel_id=1, source_target_pairs={{4,0},{5,1},{6,2},{7,3},{0,4},{1,5},{2,6},{3,7},{12,8},{13,9},{14,... | collective-permute-start | bytes 786440 | tf_op jit(solution)/shard_map/gather_gradients/ppermute | solution.py:34
  100.4 9.1 %collective-permute-start.28 = (bf16[8,128,128]{2,1,0:T(8,128)(2,1)S(1)}, bf16[8,128,128]{2,1,0:T(8,128)(2,1)S(1)}, u32[]{:S(2)}, u32[]{:S(2)}) collective-permute-start(bf16[8,128,128]{2,1,0:T(8,128)(2,1)S(1)} %collective-permute-done.22.refs_4_), channel_id=1, source_target_pairs={{3,0},{0,1},{1,2},{2,3},{7,4},{4,5},{5,6},{6,7},{11,8},{8,9},{9,10... | collective-permute-start | bytes 786440 | tf_op jit(solution)/shard_map/gather_gradients/ppermute | solution.py:34
  100.4 9.1 %collective-permute-start.26 = (bf16[8,128,128]{2,1,0:T(8,128)(2,1)S(1)}, bf16[8,128,128]{2,1,0:T(8,128)(2,1)S(1)}, u32[]{:S(2)}, u32[]{:S(2)}) collective-permute-start(bf16[8,128,128]{2,1,0:T(8,128)(2,1)S(1)} %collective-permute-done.22.refs_4_), channel_id=1, source_target_pairs={{1,0},{2,1},{3,2},{0,3},{5,4},{6,5},{7,6},{4,7},{9,8},{10,9},{11,1... | collective-permute-start | bytes 786440 | tf_op jit(solution)/shard_map/gather_gradients/ppermute | solution.py:34
  109.5 8.6 %collective-permute-start.32 = (f32[72,256]{1,0:T(8,128)S(1)}, f32[72,256]{1,0:T(8,128)S(1)}, u32[]{:S(2)}, u32[]{:S(2)}) collective-permute-start(f32[72,256]{1,0:T(8,128)S(1)} %bitcast_add_fusion), channel_id=1, source_target_pairs={{4,0},{5,1},{6,2},{7,3},{0,4},{1,5},{2,6},{3,7},{12,8},{13,9},{14,... | collective-permute-start | bytes 221192 | tf_op jit(solution)/shard_map/scatter_gradients/ppermute | solution.py:34
  118.2 9.2 %collective-permute-start.33 = (bf16[8,8,128,128]{3,2,1,0:T(8,128)(2,1)}, bf16[8,8,128,128]{3,2,1,0:T(8,128)(2,1)S(1)}, u32[]{:S(2)}, u32[]{:S(2)}) collective-permute-start(bf16[8,8,128,128]{3,2,1,0:T(8,128)(2,1)} %get-tuple-element.97), channel_id=1, source_target_pairs={{8,0},{0,8},{24,16},{16,24},{40,32},{32,40},{56,48},{48,56},{72,64... | collective-permute-start | bytes 6291464 | tf_op jit(solution)/shard_map/scatter_gradients/ppermute | solution.py:30
  121.2 4.3 %collective-permute-start.36 = (f32[72,256]{1,0:T(8,128)S(1)}, f32[72,256]{1,0:T(8,128)S(1)}, u32[]{:S(2)}, u32[]{:S(2)}) collective-permute-start(f32[72,256]{1,0:T(8,128)S(1)} %add.62), channel_id=1, source_target_pairs={{72,0},{64,8},{88,16},{80,24},{104,32},{96,40},{120,48},{112,56},{... | collective-permute-start | bytes 221192 | tf_op jit(solution)/shard_map/scatter_gradients/ppermute | solution.py:30
  122.8 4.5 %collective-permute-start.35 = (f32[72,256]{1,0:T(8,128)S(1)}, f32[72,256]{1,0:T(8,128)S(1)}, u32[]{:S(2)}, u32[]{:S(2)}) collective-permute-start(f32[72,256]{1,0:T(8,128)S(1)} %add.62), channel_id=1, source_target_pairs={{64,0},{72,8},{80,16},{88,24},{96,32},{104,40},{112,48},{120,56},{... | collective-permute-start | bytes 221192 | tf_op jit(solution)/shard_map/scatter_gradients/ppermute | solution.py:30
  122.9 4.4 %collective-permute-start.34 = (f32[72,256]{1,0:T(8,128)S(1)}, f32[72,256]{1,0:T(8,128)S(1)}, u32[]{:S(2)}, u32[]{:S(2)}) collective-permute-start(f32[72,256]{1,0:T(8,128)S(1)} %add.62), channel_id=1, source_target_pairs={{8,0},{0,8},{24,16},{16,24},{40,32},{32,40},{56,48},{48,56},{72,64... | collective-permute-start | bytes 221192 | tf_op jit(solution)/shard_map/scatter_gradients/ppermute | solution.py:30
  130.3 9.5 %collective-permute-start.43 = (f32[72,256]{1,0:T(8,128)S(1)}, f32[72,256]{1,0:T(8,128)S(1)}, u32[]{:S(2)}, u32[]{:S(2)}) collective-permute-start(f32[72,256]{1,0:T(8,128)S(1)} %add_add_fusion.1), channel_id=1, source_target_pairs={{48,0},{56,8},{0,16},{8,24},{16,32},{24,40},{32,48},{40,56},{112,6... | collective-permute-start | bytes 221192 | tf_op jit(solution)/shard_map/scatter_gradients/ppermute | solution.py:30
  130.3 9.4 %collective-permute-start.42 = (f32[72,256]{1,0:T(8,128)S(1)}, f32[72,256]{1,0:T(8,128)S(1)}, u32[]{:S(2)}, u32[]{:S(2)}) collective-permute-start(f32[72,256]{1,0:T(8,128)S(1)} %add_add_fusion.1), channel_id=1, source_target_pairs={{32,0},{40,8},{48,16},{56,24},{0,32},{8,40},{16,48},{24,56},{96,64... | collective-permute-start | bytes 221192 | tf_op jit(solution)/shard_map/scatter_gradients/ppermute | solution.py:30
  135.5 4.5 %collective-permute-start.41 = (f32[72,256]{1,0:T(8,128)S(1)}, f32[72,256]{1,0:T(8,128)S(1)}, u32[]{:S(2)}, u32[]{:S(2)}) collective-permute-start(f32[72,256]{1,0:T(8,128)S(1)} %add_add_fusion.1), channel_id=1, source_target_pairs={{16,0},{24,8},{32,16},{40,24},{48,32},{56,40},{0,48},{8,56},{80,64... | collective-permute-start | bytes 221192 | tf_op jit(solution)/shard_map/scatter_gradients/ppermute | solution.py:30
  138.0 14.6 %collective-permute-start.38 = (bf16[8,128,128]{2,1,0:T(8,128)(2,1)S(1)}, bf16[8,128,128]{2,1,0:T(8,128)(2,1)S(1)}, u32[]{:S(2)}, u32[]{:S(2)}) collective-permute-start(bf16[8,128,128]{2,1,0:T(8,128)(2,1)S(1)} %get-tuple-element.100), channel_id=1, source_target_pairs={{64,0},{72,8},{80,16},{88,24},{96,32},{104,40},{112,48},{120,56},{... | collective-permute-start | bytes 786440 | tf_op jit(solution)/shard_map/scatter_gradients/ppermute | solution.py:30
  139.7 14.2 %collective-permute-start.39 = (bf16[8,128,128]{2,1,0:T(8,128)(2,1)S(1)}, bf16[8,128,128]{2,1,0:T(8,128)(2,1)S(1)}, u32[]{:S(2)}, u32[]{:S(2)}) collective-permute-start(bf16[8,128,128]{2,1,0:T(8,128)(2,1)S(1)} %get-tuple-element.101), channel_id=1, source_target_pairs={{96,0},{104,8},{112,16},{120,24},{64,32},{72,40},{80,48},{88,56},{... | collective-permute-start | bytes 786440 | tf_op jit(solution)/shard_map/scatter_gradients/ppermute | solution.py:30
  140.0 28.1 %copy-start.1 = (f32[72,256]{1,0:T(8,128)}, f32[72,256]{1,0:T(8,128)S(1)}, u32[]{:S(2)}) copy-start(f32[72,256]{1,0:T(8,128)S(1)} %add_add_fusion.s0) | copy-start | bytes 221188
  140.0 7.2 %collective-permute-start.46 = (f32[72,256]{1,0:T(8,128)S(1)}, f32[72,256]{1,0:T(8,128)S(1)}, u32[]{:S(2)}, u32[]{:S(2)}) collective-permute-start(f32[72,256]{1,0:T(8,128)S(1)} %add_add_fusion.s0), channel_id=1, source_target_pairs={{3,0},{0,1},{1,2},{2,3},{7,4},{4,5},{5,6},{6,7},{11,8},{8,9},{9,10... | collective-permute-start | bytes 221192 | tf_op jit(solution)/shard_map/scatter_gradients/ppermute | solution.py:34
  144.5 5.9 %collective-permute-start.45 = (f32[72,256]{1,0:T(8,128)S(1)}, f32[72,256]{1,0:T(8,128)S(1)}, u32[]{:S(2)}, u32[]{:S(2)}) collective-permute-start(f32[72,256]{1,0:T(8,128)S(1)} %add_add_fusion.s0), channel_id=1, source_target_pairs={{2,0},{3,1},{0,2},{1,3},{6,4},{7,5},{4,6},{5,7},{10,8},{11,9},{8,1... | collective-permute-start | bytes 221192 | tf_op jit(solution)/shard_map/scatter_gradients/ppermute | solution.py:34
  145.8 6.1 %collective-permute-start.44 = (f32[72,256]{1,0:T(8,128)S(1)}, f32[72,256]{1,0:T(8,128)S(1)}, u32[]{:S(2)}, u32[]{:S(2)}) collective-permute-start(f32[72,256]{1,0:T(8,128)S(1)} %add_add_fusion.s0), channel_id=1, source_target_pairs={{1,0},{2,1},{3,2},{0,3},{5,4},{6,5},{7,6},{4,7},{9,8},{10,9},{11,1... | collective-permute-start | bytes 221192 | tf_op jit(solution)/shard_map/scatter_gradients/ppermute | solution.py:34
  147.2 20.9 %copy-start.38 = (f32[72,256]{1,0:T(8,128)}, f32[72,256]{1,0:T(8,128)S(1)}, u32[]{:S(2)}) copy-start(f32[72,256]{1,0:T(8,128)S(1)} %collective-permute-done.46.s3) | copy-start | bytes 221188
  147.2 19.3 %collective-permute-start.37 = (bf16[8,128,128]{2,1,0:T(8,128)(2,1)S(1)}, bf16[8,128,128]{2,1,0:T(8,128)(2,1)S(1)}, u32[]{:S(2)}, u32[]{:S(2)}) collective-permute-start(bf16[8,128,128]{2,1,0:T(8,128)(2,1)S(1)} %get-tuple-element.99), channel_id=1, source_target_pairs={{48,0},{56,8},{0,16},{8,24},{16,32},{24,40},{32,48},{40,56},{112,6... | collective-permute-start | bytes 786440 | tf_op jit(solution)/shard_map/scatter_gradients/ppermute | solution.py:30
  150.3 17.8 %copy-start.39 = (f32[72,256]{1,0:T(8,128)}, f32[72,256]{1,0:T(8,128)S(1)}, u32[]{:S(2)}) copy-start(f32[72,256]{1,0:T(8,128)S(1)} %collective-permute-done.45.s2) | copy-start | bytes 221188
  150.3 16.2 %collective-permute-start.40 = (bf16[8,128,128]{2,1,0:T(8,128)(2,1)S(1)}, bf16[8,128,128]{2,1,0:T(8,128)(2,1)S(1)}, u32[]{:S(2)}, u32[]{:S(2)}) collective-permute-start(bf16[8,128,128]{2,1,0:T(8,128)(2,1)S(1)} %get-tuple-element.102), channel_id=1, source_target_pairs={{32,0},{40,8},{48,16},{56,24},{0,32},{8,40},{16,48},{24,56},{96,64... | collective-permute-start | bytes 786440 | tf_op jit(solution)/shard_map/scatter_gradients/ppermute | solution.py:30
  151.8 16.3 %copy-start.40 = (f32[72,256]{1,0:T(8,128)}, f32[72,256]{1,0:T(8,128)S(1)}, u32[]{:S(2)}) copy-start(f32[72,256]{1,0:T(8,128)S(1)} %collective-permute-done.44.s1) | copy-start | bytes 221188
  151.8 16.3 %collective-permute-start.47 = (bf16[8,128,128]{2,1,0:T(8,128)(2,1)S(1)}, bf16[8,128,128]{2,1,0:T(8,128)(2,1)S(1)}, u32[]{:S(2)}, u32[]{:S(2)}) collective-permute-start(bf16[8,128,128]{2,1,0:T(8,128)(2,1)S(1)} %get-tuple-element.105), channel_id=1, source_target_pairs={{16,0},{24,8},{32,16},{40,24},{48,32},{56,40},{0,48},{8,56},{80,64... | collective-permute-start | bytes 786440 | tf_op jit(solution)/shard_map/scatter_gradients/ppermute | solution.py:30
  152.7 15.5 %copy-start.24 = (bf16[8,128,128]{2,1,0:T(8,128)(2,1)}, bf16[8,128,128]{2,1,0:T(8,128)(2,1)S(1)}, u32[]{:S(2)}) copy-start(bf16[8,128,128]{2,1,0:T(8,128)(2,1)S(1)} %collective-permute-done.38.r4) | copy-start | bytes 786436
  152.7 15.5 %collective-permute-start.48 = (bf16[8,128,128]{2,1,0:T(8,128)(2,1)S(1)}, bf16[8,128,128]{2,1,0:T(8,128)(2,1)S(1)}, u32[]{:S(2)}, u32[]{:S(2)}) collective-permute-start(bf16[8,128,128]{2,1,0:T(8,128)(2,1)S(1)} %get-tuple-element.107), channel_id=1, source_target_pairs={{112,0},{120,8},{64,16},{72,24},{80,32},{88,40},{96,48},{104,56},{... | collective-permute-start | bytes 786440 | tf_op jit(solution)/shard_map/scatter_gradients/ppermute | solution.py:30
  153.9 14.3 %copy-start.25 = (bf16[8,128,128]{2,1,0:T(8,128)(2,1)}, bf16[8,128,128]{2,1,0:T(8,128)(2,1)S(1)}, u32[]{:S(2)}) copy-start(bf16[8,128,128]{2,1,0:T(8,128)(2,1)S(1)} %collective-permute-done.39.r6) | copy-start | bytes 786436
  153.9 14.2 %collective-permute-start.49 = (bf16[8,128,128]{2,1,0:T(8,128)(2,1)S(1)}, bf16[8,128,128]{2,1,0:T(8,128)(2,1)S(1)}, u32[]{:S(2)}, u32[]{:S(2)}) collective-permute-start(bf16[8,128,128]{2,1,0:T(8,128)(2,1)S(1)} %get-tuple-element.109), channel_id=1, source_target_pairs={{80,0},{88,8},{96,16},{104,24},{112,32},{120,40},{64,48},{72,56},{... | collective-permute-start | bytes 786440 | tf_op jit(solution)/shard_map/scatter_gradients/ppermute | solution.py:30
  (27 other events, 98.1 us)

commit v3 on v2

--- a/solution.py
+++ b/solution.py
@@ -14,7 +14,8 @@
 BATCH = 4
 SLICE = 64
 STEPS = ((), (4, 6, 2), (1, 3, 5, 7))
-VMEM_BYTES = 56 * 1024 * 1024
+VMEM_BYTES = 36 * 1024 * 1024
+SMALL_BYTES = 16 * 1024 * 1024
 RELATIVE = [(dx, dy) for dx in (0, 1) for dy in range(4)]
 
 
@@ -352,7 +353,7 @@
             in_specs=[node_spec] * 9
             + [weight_spec, weight_spec, pl.BlockSpec((1, hidden), lambda i: (0, 0)), hid_spec],
             out_specs=[hid_spec, node_spec, hid_spec, piece_spec],
-            compiler_params=pltpu.CompilerParams(vmem_limit_bytes=VMEM_BYTES),
+            compiler_params=pltpu.CompilerParams(vmem_limit_bytes=SMALL_BYTES),
             name="dense",
         )(
             partial[0],
@@ -373,7 +374,7 @@
             ],
             in_specs=[smem] + [vmem] * 4,
             out_specs=[vmem] * 2,
-            compiler_params=pltpu.CompilerParams(vmem_limit_bytes=VMEM_BYTES),
+            compiler_params=pltpu.CompilerParams(vmem_limit_bytes=SMALL_BYTES),
             cost_estimate=pl.CostEstimate(
                 flops=6 * own_nodes * features * hidden,
                 bytes_accessed=2 * 1024 * 1024,
@@ -459,7 +460,7 @@
                 weight_spec,
                 pl.BlockSpec((1, hidden), lambda i: (0, 0)),
             ],
-            compiler_params=pltpu.CompilerParams(vmem_limit_bytes=VMEM_BYTES),
+            compiler_params=pltpu.CompilerParams(vmem_limit_bytes=SMALL_BYTES),
             name="grad_input",
         )(meta, keep, swapped, *[column[k] for k in range(1, 8)], self_term, *quarters)
     return (output, grad_input, grad_self, grad_neigh, grad_bias[0])

time: 176 us -> 159 us (0.903); the launches traced: 172 us -> 157 us
  starting transfers between devices: 78.5 us -> 71 us
  waiting for transfers between devices: 57.6 us -> 50.1 us
  Pallas kernels: 26.5 us -> 30.4 us
  other arithmetic: 4.42 us -> 1.32 us
    ppermute x21, waiting for transfers between devices: 28.5 us -> 23.1 us  [from_narrow(): lax.ppermute(x, 'narrow', [(narrow_index(n, dx, dz), n) for n in range(8)])]
    ppermute x21, starting transfers between devices: 44.4 us -> 39.5 us  [from_narrow(): lax.ppermute(x, 'narrow', [(narrow_index(n, dx, dz), n) for n in range(8)])]
    pallas_call x1, Pallas kernels: 1.93 us -> 5.16 us  [local(): pl.pallas_call(plan_kernel, out_shape=[jax.ShapeDtypeStruct((3, (slots +...]
    ppermute x29, starting transfers between devices: 34 us -> 31.4 us  [from_wide(): lax.ppermute(x, 'wide', [(wide_index(w, dx, dy, dc), w) for w in range(16)])]
    pallas_call x1, Pallas kernels: 7.84 us -> 10.4 us  [local(): pl.pallas_call(backward_kernel, out_shape=[pieces, pieces], in_specs=[sme...]
    pallas_call x1, Pallas kernels: 7.72 us -> 10.2 us  [local(): pl.pallas_call(forward_kernel, out_shape=[jax.ShapeDtypeStruct((own_nodes...]
    convert_element_type x1, other arithmetic: 2.84 us -> 0.65 us  [local(): (keep[k].astype(f32) + swapped[k].astype(f32)).astype(bf16)]
    ppermute x29, waiting for transfers between devices: 29.1 us -> 27.1 us  [from_wide(): lax.ppermute(x, 'wide', [(wide_index(w, dx, dy, dc), w) for w in range(16)])]
  transfers between devices with their start and end apart: 50 -> 50, of which waited for: 19 -> 20; matrix products, arithmetic and copies ran while one was open for 1% -> 0% of each run, Pallas kernels for 7% -> 11%
where the time goes in v3:
time: 159 us; the launch traced here: 157 us
  starting transfers between devices  71 us (45%)
  waiting for transfers between devices  50.1 us (32%)
  Pallas kernels  30.4 us (19%)
  local copies, waits for them, and re-layouts  3.01 us (2%)
    ppermute x21, starting transfers between devices, from_narrow(): lax.ppermute(x, 'narrow', [(narrow_index(n, dx, dz), n) for n in range(8)])  39.5 us
    ppermute x29, starting transfers between devices, from_wide(): lax.ppermute(x, 'wide', [(wide_index(w, dx, dy, dc), w) for w in range(16)])  31.4 us
    ppermute x29, waiting for transfers between devices, from_wide(): lax.ppermute(x, 'wide', [(wide_index(w, dx, dy, dc), w) for w in range(16)])  27.1 us
    ppermute x21, waiting for transfers between devices, from_narrow(): lax.ppermute(x, 'narrow', [(narrow_index(n, dx, dz), n) for n in range(8)])  23.1 us
    pallas_call x1, Pallas kernels, local(): pl.pallas_call(backward_kernel, out_shape=[pieces, pieces], in_specs=[sme...  10.4 us
    pallas_call x1, Pallas kernels, local(): pl.pallas_call(forward_kernel, out_shape=[jax.ShapeDtypeStruct((own_nodes...  10.2 us
    pallas_call x1, Pallas kernels, local(): pl.pallas_call(plan_kernel, out_shape=[jax.ShapeDtypeStruct((3, (slots +...  5.16 us
  transfers between devices with their start and end apart: 50, of which 20 were waited for; matrix products, arithmetic and copies ran while one was open for 0% of the time, Pallas kernels for 11%

profile of v3, /device:TPU:0, one launch (start us, length us, event | category | flops | bytes accessed | tf_op | source)
XLA Modules:
  0.0 157.3 jit_solution(10649164616043934366)
XLA Ops:
  0.6 1.7 %collective-permute-start.3 = (bf16[1024,128]{1,0:T(8,128)(2,1)}, bf16[1024,128]{1,0:T(8,128)(2,1)S(1)}, u32[]{:S(2)}, u32[]{:S(2)}) collective-permute-start(bf16[1024,128]{1,0:T(8,128)(2,1)} %refs_1_.1), channel_id=1, source_target_pairs={{48,0},{56,8},{0,16},{8,24},{16,32},{24,40},{32,48},{40,56},{112,6... | collective-permute-start | bytes 786440 | tf_op jit(solution)/shard_map/gather_features/ppermute | solution.py:31
  2.4 1.6 %collective-permute-start.2 = (bf16[1024,128]{1,0:T(8,128)(2,1)}, bf16[1024,128]{1,0:T(8,128)(2,1)S(1)}, u32[]{:S(2)}, u32[]{:S(2)}) collective-permute-start(bf16[1024,128]{1,0:T(8,128)(2,1)} %refs_1_.1), channel_id=1, source_target_pairs={{16,0},{24,8},{32,16},{40,24},{48,32},{56,40},{0,48},{8,56},{80,64... | collective-permute-start | bytes 786440 | tf_op jit(solution)/shard_map/gather_features/ppermute | solution.py:31
  3.9 2.1 %collective-permute-start.1 = (bf16[1024,128]{1,0:T(8,128)(2,1)}, bf16[1024,128]{1,0:T(8,128)(2,1)S(1)}, u32[]{:S(2)}, u32[]{:S(2)}) collective-permute-start(bf16[1024,128]{1,0:T(8,128)(2,1)} %refs_1_.1), channel_id=1, source_target_pairs={{32,0},{40,8},{48,16},{56,24},{0,32},{8,40},{16,48},{24,56},{96,64... | collective-permute-start | bytes 786440 | tf_op jit(solution)/shard_map/gather_features/ppermute | solution.py:31
  6.0 1.5 collective-permute-start
  8.2 0.6 pad_add_fusion.meta.refs_0_
  8.7 5.2 %plan.1 = (s32[3,320]{1,0:T(4,128)}, s32[1]{0:T(128)}) custom-call(s32[4]{0:T(128)} %pad_add_fusion.meta.refs_0_, s32[512]{0:T(512)} %rows.1), custom_call_target="tpu_custom_call" | custom-call | tf_op jit(solution)/shard_map/plan/plan/pallas_call | solution.py:295
  13.9 1.5 collective-permute-done.2.refs_1_
  15.4 1.7 %collective-permute-done.1.refs_2_ = bf16[1024,128]{1,0:T(8,128)(2,1)S(1)} collective-permute-done((bf16[1024,128]{1,0:T(8,128)(2,1)}, bf16[1024,128]{1,0:T(8,128)(2,1)S(1)}, u32[]{:S(2)}, u32[]{:S(2)}) %collective-permute-start.1) | collective-permute-done | bytes 262176 | tf_op jit(solution)/shard_map/gather_features/ppermute | solution.py:31
  17.6 1.5 collective-permute-start.5
  19.1 1.1 collective-permute-start.6
  20.3 2.1 %collective-permute-start.4 = (bf16[1024,128]{1,0:T(8,128)(2,1)S(1)}, bf16[1024,128]{1,0:T(8,128)(2,1)S(1)}, u32[]{:S(2)}, u32[]{:S(2)}) collective-permute-start(bf16[1024,128]{1,0:T(8,128)(2,1)S(1)} %collective-permute-done.refs_4_), channel_id=1, source_target_pairs={{16,0},{24,8},{32,16},{40,24},{48,32},{56,40},{0,48},{8,56},{80,64... | collective-permute-start | bytes 786440 | tf_op jit(solution)/shard_map/gather_features/ppermute | solution.py:31
  22.9 3.0 %collective-permute-done.5.refs_6_ = bf16[1024,128]{1,0:T(8,128)(2,1)S(1)} collective-permute-done((bf16[1024,128]{1,0:T(8,128)(2,1)S(1)}, bf16[1024,128]{1,0:T(8,128)(2,1)S(1)}, u32[]{:S(2)}, u32[]{:S(2)}) %collective-permute-start.5) | collective-permute-done | bytes 262176 | tf_op jit(solution)/shard_map/gather_features/ppermute | solution.py:31
  25.8 2.4 %collective-permute-done.6.refs_7_ = bf16[1024,128]{1,0:T(8,128)(2,1)S(1)} collective-permute-done((bf16[1024,128]{1,0:T(8,128)(2,1)S(1)}, bf16[1024,128]{1,0:T(8,128)(2,1)S(1)}, u32[]{:S(2)}, u32[]{:S(2)}) %collective-permute-start.6) | collective-permute-done | bytes 262176 | tf_op jit(solution)/shard_map/gather_features/ppermute | solution.py:31
  28.8 1.0 collective-permute-done.14.refs_15_
  30.2 0.9 copy-done
  31.1 0.7 copy-done.4
  31.8 0.7 copy-done.5
  32.5 0.7 copy-done.6
  33.2 10.2 %aggregate.1 = (bf16[1024,128]{1,0:T(8,128)(2,1)S(1)}, bf16[1024,128]{1,0:T(8,128)(2,1)S(1)}, bf16[1024,128]{1,0:T(8,128)(2,1)S(1)}, bf16[1024,128]{1,0:T(8,128)...) custom-call(s32[4]{0:T(128)S(1)} %copy-done.5, ...), custom_call_target="tpu_custom_call" | custom-call | flops 2147483648 | bytes 23068672 | tf_op jit(solution)/shard_map/aggregate/aggregate/pallas_call | solution.py:316
  43.4 1.5 collective-permute-start.15
  44.8 0.8 collective-permute-start.16
  45.6 4.3 %collective-permute-start.17 = (bf16[1024,128]{1,0:T(8,128)(2,1)S(1)}, bf16[1024,128]{1,0:T(8,128)(2,1)S(1)}, u32[]{:S(2)}, u32[]{:S(2)}) collective-permute-start(bf16[1024,128]{1,0:T(8,128)(2,1)S(1)} %get-tuple-element.71), channel_id=1, source_target_pairs={{2,0},{3,1},{0,2},{1,3},{6,4},{7,5},{4,6},{5,7},{10,8},{11,9},{8,1... | collective-permute-start | bytes 786440 | tf_op jit(solution)/shard_map/scatter_aggregate/ppermute | solution.py:35
  50.4 5.2 %collective-permute-start.19 = (bf16[1024,128]{1,0:T(8,128)(2,1)S(1)}, bf16[1024,128]{1,0:T(8,128)(2,1)S(1)}, u32[]{:S(2)}, u32[]{:S(2)}) collective-permute-start(bf16[1024,128]{1,0:T(8,128)(2,1)S(1)} %get-tuple-element.73), channel_id=1, source_target_pairs={{5,0},{6,1},{7,2},{4,3},{1,4},{2,5},{3,6},{0,7},{13,8},{14,9},{15,... | collective-permute-start | bytes 786440 | tf_op jit(solution)/shard_map/scatter_aggregate/ppermute | solution.py:35
  55.6 2.8 %collective-permute-done.16.r2 = bf16[1024,128]{1,0:T(8,128)(2,1)S(1)} collective-permute-done((bf16[1024,128]{1,0:T(8,128)(2,1)S(1)}, bf16[1024,128]{1,0:T(8,128)(2,1)S(1)}, u32[]{:S(2)}, u32[]{:S(2)}) %collective-permute-start.16) | collective-permute-done | bytes 262176 | tf_op jit(solution)/shard_map/scatter_aggregate/ppermute | solution.py:35
  58.4 2.2 %collective-permute-start.21 = (bf16[1024,128]{1,0:T(8,128)(2,1)S(1)}, bf16[1024,128]{1,0:T(8,128)(2,1)S(1)}, u32[]{:S(2)}, u32[]{:S(2)}) collective-permute-start(bf16[1024,128]{1,0:T(8,128)(2,1)S(1)} %get-tuple-element.75), channel_id=1, source_target_pairs={{1,0},{2,1},{3,2},{0,3},{5,4},{6,5},{7,6},{4,7},{9,8},{10,9},{11,1... | collective-permute-start | bytes 786440 | tf_op jit(solution)/shard_map/scatter_aggregate/ppermute | solution.py:35
  60.6 4.5 %collective-permute-done.17.r3 = bf16[1024,128]{1,0:T(8,128)(2,1)S(1)} collective-permute-done((bf16[1024,128]{1,0:T(8,128)(2,1)S(1)}, bf16[1024,128]{1,0:T(8,128)(2,1)S(1)}, u32[]{:S(2)}, u32[]{:S(2)}) %collective-permute-start.17) | collective-permute-done | bytes 262176 | tf_op jit(solution)/shard_map/scatter_aggregate/ppermute | solution.py:35
  65.1 1.2 collective-permute-done.18.r4
  66.3 3.3 %collective-permute-done.19.r5 = bf16[1024,128]{1,0:T(8,128)(2,1)S(1)} collective-permute-done((bf16[1024,128]{1,0:T(8,128)(2,1)S(1)}, bf16[1024,128]{1,0:T(8,128)(2,1)S(1)}, u32[]{:S(2)}, u32[]{:S(2)}) %collective-permute-start.19) | collective-permute-done | bytes 262176 | tf_op jit(solution)/shard_map/scatter_aggregate/ppermute | solution.py:35
  70.1 1.7 %collective-permute-done.21.r7 = bf16[1024,128]{1,0:T(8,128)(2,1)S(1)} collective-permute-done((bf16[1024,128]{1,0:T(8,128)(2,1)S(1)}, bf16[1024,128]{1,0:T(8,128)(2,1)S(1)}, u32[]{:S(2)}, u32[]{:S(2)}) %collective-permute-start.21) | collective-permute-done | bytes 262176 | tf_op jit(solution)/shard_map/scatter_aggregate/ppermute | solution.py:35
  71.8 1.8 %dense.1 = (bf16[1024,256]{1,0:T(8,128)(2,1)}, bf16[1024,128]{1,0:T(8,128)(2,1)S(1)}, bf16[1024,256]{1,0:T(8,128)(2,1)S(1)}, bf16[8,128,128]{2,1,0:T(8,128)(2,1)S(1)}) custom-call(bf16[1024,128]{1,0:T(8,128)(2,1)S(1)} %get-tuple-element.68.own, bf16[1024,128]{1,0:T(8,128)(2,1)S(1)} %collective-permute-done.15.r1, ...), custom_call_target="tpu_custom_call" | custom-call | tf_op jit(solution)/shard_map/dense/dense/pallas_call | solution.py:344
  73.6 0.8 collective-permute-start.25
  74.4 2.4 %collective-permute-start.24 = (bf16[8,128,128]{2,1,0:T(8,128)(2,1)S(1)}, bf16[8,128,128]{2,1,0:T(8,128)(2,1)S(1)}, u32[]{:S(2)}, u32[]{:S(2)}) collective-permute-start(bf16[8,128,128]{2,1,0:T(8,128)(2,1)S(1)} %get-tuple-element.85.refs_0_), channel_id=1, source_target_pairs={{1,0},{2,1},{3,2},{0,3},{5,4},{6,5},{7,6},{4,7},{9,8},{10,9},{11,1... | collective-permute-start | bytes 786440 | tf_op jit(solution)/shard_map/gather_gradients/ppermute | solution.py:35
  76.8 1.2 collective-permute-start.23
  78.0 2.9 %collective-permute-start.22 = (bf16[8,128,128]{2,1,0:T(8,128)(2,1)S(1)}, bf16[8,128,128]{2,1,0:T(8,128)(2,1)S(1)}, u32[]{:S(2)}, u32[]{:S(2)}) collective-permute-start(bf16[8,128,128]{2,1,0:T(8,128)(2,1)S(1)} %get-tuple-element.85.refs_0_), channel_id=1, source_target_pairs={{4,0},{5,1},{6,2},{7,3},{0,4},{1,5},{2,6},{3,7},{12,8},{13,9},{14,... | collective-permute-start | bytes 786440 | tf_op jit(solution)/shard_map/gather_gradients/ppermute | solution.py:35
  80.9 1.0 weight_gradients.1
  82.0 3.5 %collective-permute-start.30 = (f32[72,256]{1,0:T(8,128)S(1)}, f32[72,256]{1,0:T(8,128)S(1)}, u32[]{:S(2)}, u32[]{:S(2)}) collective-permute-start(f32[72,256]{1,0:T(8,128)S(1)} %get-tuple-element.126), channel_id=1, source_target_pairs={{2,0},{3,1},{0,2},{1,3},{6,4},{7,5},{4,6},{5,7},{10,8},{11,9},{8,1... | collective-permute-start | bytes 221192 | tf_op jit(solution)/shard_map/weight_gradients/ppermute | solution.py:35
  85.5 0.7 collective-permute-start.31
  86.2 1.3 collective-permute-start.29
  87.5 2.3 %collective-permute-done.23.refs_2_ = bf16[8,128,128]{2,1,0:T(8,128)(2,1)S(1)} collective-permute-done((bf16[8,128,128]{2,1,0:T(8,128)(2,1)S(1)}, bf16[8,128,128]{2,1,0:T(8,128)(2,1)S(1)}, u32[]{:S(2)}, u32[]{:S(2)}) %collective-permute-start.23) | collective-permute-done | bytes 262176 | tf_op jit(solution)/shard_map/gather_gradients/ppermute | solution.py:35
  89.8 4.0 %collective-permute-start.27 = (bf16[8,128,128]{2,1,0:T(8,128)(2,1)S(1)}, bf16[8,128,128]{2,1,0:T(8,128)(2,1)S(1)}, u32[]{:S(2)}, u32[]{:S(2)}) collective-permute-start(bf16[8,128,128]{2,1,0:T(8,128)(2,1)S(1)} %collective-permute-done.23.refs_2_), channel_id=1, source_target_pairs={{4,0},{5,1},{6,2},{7,3},{0,4},{1,5},{2,6},{3,7},{12,8},{13,9},{14,... | collective-permute-start | bytes 786440 | tf_op jit(solution)/shard_map/gather_gradients/ppermute | solution.py:35
  93.8 0.8 collective-permute-start.28
  94.6 2.8 %collective-permute-start.26 = (bf16[8,128,128]{2,1,0:T(8,128)(2,1)S(1)}, bf16[8,128,128]{2,1,0:T(8,128)(2,1)S(1)}, u32[]{:S(2)}, u32[]{:S(2)}) collective-permute-start(bf16[8,128,128]{2,1,0:T(8,128)(2,1)S(1)} %collective-permute-done.22.refs_4_), channel_id=1, source_target_pairs={{1,0},{2,1},{3,2},{0,3},{5,4},{6,5},{7,6},{4,7},{9,8},{10,9},{11,1... | collective-permute-start | bytes 786440 | tf_op jit(solution)/shard_map/gather_gradients/ppermute | solution.py:35
  97.5 0.7 collective-permute-done.27.refs_6_
  98.2 3.6 %collective-permute-done.28.refs_7_ = bf16[8,128,128]{2,1,0:T(8,128)(2,1)S(1)} collective-permute-done((bf16[8,128,128]{2,1,0:T(8,128)(2,1)S(1)}, bf16[8,128,128]{2,1,0:T(8,128)(2,1)S(1)}, u32[]{:S(2)}, u32[]{:S(2)}) %collective-permute-start.28) | collective-permute-done | bytes 262176 | tf_op jit(solution)/shard_map/gather_gradients/ppermute | solution.py:35
  101.8 1.3 collective-permute-done.26.refs_5_
  103.2 10.4 %column_gradients.1 = (bf16[8,8,128,128]{3,2,1,0:T(8,128)(2,1)S(1)}, bf16[8,8,128,128]{3,2,1,0:T(8,128)(2,1)S(1)}) custom-call(s32[4]{0:T(128)S(1)} %copy-done.5, s32[512]{0:T(512)S(1)} %copy-done.6, s32[3,320]{1,0:T(4,128)S(1)} %copy-done.4, s32[1]{0:T(128)} %get-tuple-element.63.total, bf16[512,128,128]{2,1,0:T(8,128)(2,1)} %tiles_hbm.3, ...), custom_call_target="tpu_custom_call" | custom-call | flops 2147483648 | bytes 23068672 | tf_op jit(solution)/shard_map/column_gradients/column_gradients/pallas_call | solution.py:394
  113.8 2.0 %collective-permute-start.35 = (f32[72,256]{1,0:T(8,128)S(1)}, f32[72,256]{1,0:T(8,128)S(1)}, u32[]{:S(2)}, u32[]{:S(2)}) collective-permute-start(f32[72,256]{1,0:T(8,128)S(1)} %add.62), channel_id=1, source_target_pairs={{64,0},{72,8},{80,16},{88,24},{96,32},{104,40},{112,48},{120,56},{... | collective-permute-start | bytes 221192 | tf_op jit(solution)/shard_map/scatter_gradients/ppermute | solution.py:31
  115.9 1.9 %collective-permute-done.36 = f32[72,256]{1,0:T(8,128)S(1)} collective-permute-done((f32[72,256]{1,0:T(8,128)S(1)}, f32[72,256]{1,0:T(8,128)S(1)}, u32[]{:S(2)}, u32[]{:S(2)}) %collective-permute-start.36) | collective-permute-done | bytes 73760 | tf_op jit(solution)/shard_map/scatter_gradients/ppermute | solution.py:31
  117.8 2.1 %collective-permute-done.35 = f32[72,256]{1,0:T(8,128)S(1)} collective-permute-done((f32[72,256]{1,0:T(8,128)S(1)}, f32[72,256]{1,0:T(8,128)S(1)}, u32[]{:S(2)}, u32[]{:S(2)}) %collective-permute-start.35) | collective-permute-done | bytes 73760 | tf_op jit(solution)/shard_map/scatter_gradients/ppermute | solution.py:31
  120.0 0.7 fusion.6
  120.7 1.6 %collective-permute-start.42 = (f32[72,256]{1,0:T(8,128)S(1)}, f32[72,256]{1,0:T(8,128)S(1)}, u32[]{:S(2)}, u32[]{:S(2)}) collective-permute-start(f32[72,256]{1,0:T(8,128)S(1)} %add_add_fusion.1), channel_id=1, source_target_pairs={{32,0},{40,8},{48,16},{56,24},{0,32},{8,40},{16,48},{24,56},{96,64... | collective-permute-start | bytes 221192 | tf_op jit(solution)/shard_map/scatter_gradients/ppermute | solution.py:31
  122.3 1.6 %collective-permute-start.41 = (f32[72,256]{1,0:T(8,128)S(1)}, f32[72,256]{1,0:T(8,128)S(1)}, u32[]{:S(2)}, u32[]{:S(2)}) collective-permute-start(f32[72,256]{1,0:T(8,128)S(1)} %add_add_fusion.1), channel_id=1, source_target_pairs={{16,0},{24,8},{32,16},{40,24},{48,32},{56,40},{0,48},{8,56},{80,64... | collective-permute-start | bytes 221192 | tf_op jit(solution)/shard_map/scatter_gradients/ppermute | solution.py:31
  124.0 0.7 collective-permute-start.38
  124.7 3.7 %collective-permute-start.39 = (bf16[8,128,128]{2,1,0:T(8,128)(2,1)S(1)}, bf16[8,128,128]{2,1,0:T(8,128)(2,1)S(1)}, u32[]{:S(2)}, u32[]{:S(2)}) collective-permute-start(bf16[8,128,128]{2,1,0:T(8,128)(2,1)S(1)} %get-tuple-element.101), channel_id=1, source_target_pairs={{96,0},{104,8},{112,16},{120,24},{64,32},{72,40},{80,48},{88,56},{... | collective-permute-start | bytes 786440 | tf_op jit(solution)/shard_map/scatter_gradients/ppermute | solution.py:31
  128.5 3.2 %collective-permute-start.45 = (f32[72,256]{1,0:T(8,128)S(1)}, f32[72,256]{1,0:T(8,128)S(1)}, u32[]{:S(2)}, u32[]{:S(2)}) collective-permute-start(f32[72,256]{1,0:T(8,128)S(1)} %add_add_fusion.s0), channel_id=1, source_target_pairs={{2,0},{3,1},{0,2},{1,3},{6,4},{7,5},{4,6},{5,7},{10,8},{11,9},{8,1... | collective-permute-start | bytes 221192 | tf_op jit(solution)/shard_map/scatter_gradients/ppermute | solution.py:35
  131.7 1.3 collective-permute-start.44
  133.0 1.1 collective-permute-done.46.s3
  134.0 1.6 %collective-permute-start.37 = (bf16[8,128,128]{2,1,0:T(8,128)(2,1)S(1)}, bf16[8,128,128]{2,1,0:T(8,128)(2,1)S(1)}, u32[]{:S(2)}, u32[]{:S(2)}) collective-permute-start(bf16[8,128,128]{2,1,0:T(8,128)(2,1)S(1)} %get-tuple-element.99), channel_id=1, source_target_pairs={{48,0},{56,8},{0,16},{8,24},{16,32},{24,40},{32,48},{40,56},{112,6... | collective-permute-start | bytes 786440 | tf_op jit(solution)/shard_map/scatter_gradients/ppermute | solution.py:31
  135.6 1.8 %collective-permute-start.40 = (bf16[8,128,128]{2,1,0:T(8,128)(2,1)S(1)}, bf16[8,128,128]{2,1,0:T(8,128)(2,1)S(1)}, u32[]{:S(2)}, u32[]{:S(2)}) collective-permute-start(bf16[8,128,128]{2,1,0:T(8,128)(2,1)S(1)} %get-tuple-element.102), channel_id=1, source_target_pairs={{32,0},{40,8},{48,16},{56,24},{0,32},{8,40},{16,48},{24,56},{96,64... | collective-permute-start | bytes 786440 | tf_op jit(solution)/shard_map/scatter_gradients/ppermute | solution.py:31
  137.5 0.9 collective-permute-start.47
  138.3 1.3 collective-permute-start.48
  139.6 2.9 %collective-permute-start.49 = (bf16[8,128,128]{2,1,0:T(8,128)(2,1)S(1)}, bf16[8,128,128]{2,1,0:T(8,128)(2,1)S(1)}, u32[]{:S(2)}, u32[]{:S(2)}) collective-permute-start(bf16[8,128,128]{2,1,0:T(8,128)(2,1)S(1)} %get-tuple-element.109), channel_id=1, source_target_pairs={{80,0},{88,8},{96,16},{104,24},{112,32},{120,40},{64,48},{72,56},{... | collective-permute-start | bytes 786440 | tf_op jit(solution)/shard_map/scatter_gradients/ppermute | solution.py:31
  142.5 13.0 %collective-permute-done.40.r2 = bf16[8,128,128]{2,1,0:T(8,128)(2,1)S(1)} collective-permute-done((bf16[8,128,128]{2,1,0:T(8,128)(2,1)S(1)}, bf16[8,128,128]{2,1,0:T(8,128)(2,1)S(1)}, u32[]{:S(2)}, u32[]{:S(2)}) %collective-permute-start.40) | collective-permute-done | bytes 262176 | tf_op jit(solution)/shard_map/scatter_gradients/ppermute | solution.py:31
  155.5 1.9 %grad_input.1 = (bf16[1024,128]{1,0:T(8,128)(2,1)}, f32[128,256]{1,0:T(8,128)}, f32[128,256]{1,0:T(8,128)}, f32[1,256]{1,0:T(1,128)}) custom-call(s32[4]{0:T(128)S(1)} %copy-done.5, bf16[8,8,128,128]{3,2,1,0:T(8,128)(2,1)S(1)} %get-tuple-element.96.keep, bf16[8,8,128,128]{3,2,1,0:T(8,128)(2,1)S(1)} %collective-permute-done.33.swapped, ...), custom_call_target="tpu_custom_call" | custom-call | tf_op jit(solution)/shard_map/grad_input/grad_input/pallas_call | solution.py:444
  (65 shorter events, 3.4 us)
Async XLA Ops:
  0.6 13.3 %collective-permute-start.3 = (bf16[1024,128]{1,0:T(8,128)(2,1)}, bf16[1024,128]{1,0:T(8,128)(2,1)S(1)}, u32[]{:S(2)}, u32[]{:S(2)}) collective-permute-start(bf16[1024,128]{1,0:T(8,128)(2,1)} %refs_1_.1), channel_id=1, source_target_pairs={{48,0},{56,8},{0,16},{8,24},{16,32},{24,40},{32,48},{40,56},{112,6... | collective-permute-start | bytes 786440 | tf_op jit(solution)/shard_map/gather_features/ppermute | solution.py:31
  2.4 13.1 %collective-permute-start.2 = (bf16[1024,128]{1,0:T(8,128)(2,1)}, bf16[1024,128]{1,0:T(8,128)(2,1)S(1)}, u32[]{:S(2)}, u32[]{:S(2)}) collective-permute-start(bf16[1024,128]{1,0:T(8,128)(2,1)} %refs_1_.1), channel_id=1, source_target_pairs={{16,0},{24,8},{32,16},{40,24},{48,32},{56,40},{0,48},{8,56},{80,64... | collective-permute-start | bytes 786440 | tf_op jit(solution)/shard_map/gather_features/ppermute | solution.py:31
  3.9 13.2 %collective-permute-start.1 = (bf16[1024,128]{1,0:T(8,128)(2,1)}, bf16[1024,128]{1,0:T(8,128)(2,1)S(1)}, u32[]{:S(2)}, u32[]{:S(2)}) collective-permute-start(bf16[1024,128]{1,0:T(8,128)(2,1)} %refs_1_.1), channel_id=1, source_target_pairs={{32,0},{40,8},{48,16},{56,24},{0,32},{8,40},{16,48},{24,56},{96,64... | collective-permute-start | bytes 786440 | tf_op jit(solution)/shard_map/gather_features/ppermute | solution.py:31
  6.0 11.1 %collective-permute-start = (bf16[1024,128]{1,0:T(8,128)(2,1)}, bf16[1024,128]{1,0:T(8,128)(2,1)S(1)}, u32[]{:S(2)}, u32[]{:S(2)}) collective-permute-start(bf16[1024,128]{1,0:T(8,128)(2,1)} %refs_1_.1), channel_id=1, source_target_pairs={{64,0},{72,8},{80,16},{88,24},{96,32},{104,40},{112,48},{120,56},{... | collective-permute-start | bytes 786440 | tf_op jit(solution)/shard_map/gather_features/ppermute | solution.py:31
  7.5 12.8 %collective-permute-start.7 = (bf16[1024,128]{1,0:T(8,128)(2,1)}, bf16[1024,128]{1,0:T(8,128)(2,1)S(1)}, u32[]{:S(2)}, u32[]{:S(2)}) collective-permute-start(bf16[1024,128]{1,0:T(8,128)(2,1)} %refs_1_.1), channel_id=1, source_target_pairs={{8,0},{0,8},{24,16},{16,24},{40,32},{32,40},{56,48},{48,56},{72,64... | collective-permute-start | bytes 786440 | tf_op jit(solution)/shard_map/gather_features/ppermute | solution.py:31
  17.1 5.2 %collective-permute-start.8 = (bf16[1024,128]{1,0:T(8,128)(2,1)S(1)}, bf16[1024,128]{1,0:T(8,128)(2,1)S(1)}, u32[]{:S(2)}, u32[]{:S(2)}) collective-permute-start(bf16[1024,128]{1,0:T(8,128)(2,1)S(1)} %collective-permute-done.2.refs_1_), channel_id=1, source_target_pairs={{8,0},{0,8},{24,16},{16,24},{40,32},{32,40},{56,48},{48,56},{72,64... | collective-permute-start | bytes 786440 | tf_op jit(solution)/shard_map/gather_features/ppermute | solution.py:31
  17.1 5.3 %collective-permute-start.10 = (bf16[1024,128]{1,0:T(8,128)(2,1)S(1)}, bf16[1024,128]{1,0:T(8,128)(2,1)S(1)}, u32[]{:S(2)}, u32[]{:S(2)}) collective-permute-start(bf16[1024,128]{1,0:T(8,128)(2,1)S(1)} %collective-permute-done.3.refs_3_), channel_id=1, source_target_pairs={{8,0},{0,8},{24,16},{16,24},{40,32},{32,40},{56,48},{48,56},{72,64... | collective-permute-start | bytes 786440 | tf_op jit(solution)/shard_map/gather_features/ppermute | solution.py:31
  17.6 8.2 %collective-permute-start.5 = (bf16[1024,128]{1,0:T(8,128)(2,1)S(1)}, bf16[1024,128]{1,0:T(8,128)(2,1)S(1)}, u32[]{:S(2)}, u32[]{:S(2)}) collective-permute-start(bf16[1024,128]{1,0:T(8,128)(2,1)S(1)} %collective-permute-done.1.refs_2_), channel_id=1, source_target_pairs={{64,0},{72,8},{80,16},{88,24},{96,32},{104,40},{112,48},{120,56},{... | collective-permute-start | bytes 786440 | tf_op jit(solution)/shard_map/gather_features/ppermute | solution.py:31
  19.1 9.1 %collective-permute-start.6 = (bf16[1024,128]{1,0:T(8,128)(2,1)S(1)}, bf16[1024,128]{1,0:T(8,128)(2,1)S(1)}, u32[]{:S(2)}, u32[]{:S(2)}) collective-permute-start(bf16[1024,128]{1,0:T(8,128)(2,1)S(1)} %collective-permute-done.refs_4_), channel_id=1, source_target_pairs={{48,0},{56,8},{0,16},{8,24},{16,32},{24,40},{32,48},{40,56},{112,6... | collective-permute-start | bytes 786440 | tf_op jit(solution)/shard_map/gather_features/ppermute | solution.py:31
  20.3 8.0 %collective-permute-start.4 = (bf16[1024,128]{1,0:T(8,128)(2,1)S(1)}, bf16[1024,128]{1,0:T(8,128)(2,1)S(1)}, u32[]{:S(2)}, u32[]{:S(2)}) collective-permute-start(bf16[1024,128]{1,0:T(8,128)(2,1)S(1)} %collective-permute-done.refs_4_), channel_id=1, source_target_pairs={{16,0},{24,8},{32,16},{40,24},{48,32},{56,40},{0,48},{8,56},{80,64... | collective-permute-start | bytes 786440 | tf_op jit(solution)/shard_map/gather_features/ppermute | solution.py:31
  22.4 6.4 %collective-permute-start.9 = (bf16[1024,128]{1,0:T(8,128)(2,1)S(1)}, bf16[1024,128]{1,0:T(8,128)(2,1)S(1)}, u32[]{:S(2)}, u32[]{:S(2)}) collective-permute-start(bf16[1024,128]{1,0:T(8,128)(2,1)S(1)} %collective-permute-done.1.refs_2_), channel_id=1, source_target_pairs={{8,0},{0,8},{24,16},{16,24},{40,32},{32,40},{56,48},{48,56},{72,64... | collective-permute-start | bytes 786440 | tf_op jit(solution)/shard_map/gather_features/ppermute | solution.py:31
  22.4 6.4 %collective-permute-start.11 = (bf16[1024,128]{1,0:T(8,128)(2,1)S(1)}, bf16[1024,128]{1,0:T(8,128)(2,1)S(1)}, u32[]{:S(2)}, u32[]{:S(2)}) collective-permute-start(bf16[1024,128]{1,0:T(8,128)(2,1)S(1)} %collective-permute-done.refs_4_), channel_id=1, source_target_pairs={{8,0},{0,8},{24,16},{16,24},{40,32},{32,40},{56,48},{48,56},{72,64... | collective-permute-start | bytes 786440 | tf_op jit(solution)/shard_map/gather_features/ppermute | solution.py:31
  25.8 2.9 %collective-permute-start.13 = (bf16[1024,128]{1,0:T(8,128)(2,1)S(1)}, bf16[1024,128]{1,0:T(8,128)(2,1)S(1)}, u32[]{:S(2)}, u32[]{:S(2)}) collective-permute-start(bf16[1024,128]{1,0:T(8,128)(2,1)S(1)} %collective-permute-done.5.refs_6_), channel_id=1, source_target_pairs={{8,0},{0,8},{24,16},{16,24},{40,32},{32,40},{56,48},{48,56},{72,64... | collective-permute-start | bytes 786440 | tf_op jit(solution)/shard_map/gather_features/ppermute | solution.py:31
  28.3 1.5 collective-permute-start.14
  28.3 1.9 %collective-permute-start.12 = (bf16[1024,128]{1,0:T(8,128)(2,1)S(1)}, bf16[1024,128]{1,0:T(8,128)(2,1)S(1)}, u32[]{:S(2)}, u32[]{:S(2)}) collective-permute-start(bf16[1024,128]{1,0:T(8,128)(2,1)S(1)} %collective-permute-done.4.refs_5_), channel_id=1, source_target_pairs={{8,0},{0,8},{24,16},{16,24},{40,32},{32,40},{56,48},{48,56},{72,64... | collective-permute-start | bytes 786440 | tf_op jit(solution)/shard_map/gather_features/ppermute | solution.py:31
  30.2 1.0 copy-start
  31.1 0.7 copy-start.4
  31.8 0.7 copy-start.5
  32.5 0.7 copy-start.6
  33.2 38.7 %copy-start.1 = (bf16[1024,256]{1,0:T(8,128)(2,1)S(1)}, bf16[1024,256]{1,0:T(8,128)(2,1)}, u32[]{:S(2)}) copy-start(bf16[1024,256]{1,0:T(8,128)(2,1)} %grad.1) | copy-start | bytes 1572868
  33.2 38.7 %copy-start.2 = (bf16[128,256]{1,0:T(8,128)(2,1)S(1)}, bf16[128,256]{1,0:T(8,128)(2,1)}, u32[]{:S(2)}) copy-start(bf16[128,256]{1,0:T(8,128)(2,1)} %refs_4_.1) | copy-start | bytes 196612
  33.2 38.7 %copy-start.3 = (bf16[128,256]{1,0:T(8,128)(2,1)S(1)}, bf16[128,256]{1,0:T(8,128)(2,1)}, u32[]{:S(2)}) copy-start(bf16[128,256]{1,0:T(8,128)(2,1)} %wn.1) | copy-start | bytes 196612
  33.2 38.7 %copy-start.7 = (f32[256]{0:T(256)S(1)}, f32[256]{0:T(256)}, u32[]{:S(2)}) copy-start(f32[256]{0:T(256)} %param.16) | copy-start | bytes 3076
  43.4 12.2 %collective-permute-start.15 = (bf16[1024,128]{1,0:T(8,128)(2,1)S(1)}, bf16[1024,128]{1,0:T(8,128)(2,1)S(1)}, u32[]{:S(2)}, u32[]{:S(2)}) collective-permute-start(bf16[1024,128]{1,0:T(8,128)(2,1)S(1)} %get-tuple-element.69), channel_id=1, source_target_pairs={{6,0},{7,1},{4,2},{5,3},{2,4},{3,5},{0,6},{1,7},{14,8},{15,9},{12,... | collective-permute-start | bytes 786440 | tf_op jit(solution)/shard_map/scatter_aggregate/ppermute | solution.py:35
  44.8 13.6 %collective-permute-start.16 = (bf16[1024,128]{1,0:T(8,128)(2,1)S(1)}, bf16[1024,128]{1,0:T(8,128)(2,1)S(1)}, u32[]{:S(2)}, u32[]{:S(2)}) collective-permute-start(bf16[1024,128]{1,0:T(8,128)(2,1)S(1)} %get-tuple-element.70), channel_id=1, source_target_pairs={{4,0},{5,1},{6,2},{7,3},{0,4},{1,5},{2,6},{3,7},{12,8},{13,9},{14,... | collective-permute-start | bytes 786440 | tf_op jit(solution)/shard_map/scatter_aggregate/ppermute | solution.py:35
  45.6 19.5 %collective-permute-start.17 = (bf16[1024,128]{1,0:T(8,128)(2,1)S(1)}, bf16[1024,128]{1,0:T(8,128)(2,1)S(1)}, u32[]{:S(2)}, u32[]{:S(2)}) collective-permute-start(bf16[1024,128]{1,0:T(8,128)(2,1)S(1)} %get-tuple-element.71), channel_id=1, source_target_pairs={{2,0},{3,1},{0,2},{1,3},{6,4},{7,5},{4,6},{5,7},{10,8},{11,9},{8,1... | collective-permute-start | bytes 786440 | tf_op jit(solution)/shard_map/scatter_aggregate/ppermute | solution.py:35
  49.9 16.4 %collective-permute-start.18 = (bf16[1024,128]{1,0:T(8,128)(2,1)S(1)}, bf16[1024,128]{1,0:T(8,128)(2,1)S(1)}, u32[]{:S(2)}, u32[]{:S(2)}) collective-permute-start(bf16[1024,128]{1,0:T(8,128)(2,1)S(1)} %get-tuple-element.72), channel_id=1, source_target_pairs={{7,0},{4,1},{5,2},{6,3},{3,4},{0,5},{1,6},{2,7},{15,8},{12,9},{13,... | collective-permute-start | bytes 786440 | tf_op jit(solution)/shard_map/scatter_aggregate/ppermute | solution.py:35
  50.4 19.3 %collective-permute-start.19 = (bf16[1024,128]{1,0:T(8,128)(2,1)S(1)}, bf16[1024,128]{1,0:T(8,128)(2,1)S(1)}, u32[]{:S(2)}, u32[]{:S(2)}) collective-permute-start(bf16[1024,128]{1,0:T(8,128)(2,1)S(1)} %get-tuple-element.73), channel_id=1, source_target_pairs={{5,0},{6,1},{7,2},{4,3},{1,4},{2,5},{3,6},{0,7},{13,8},{14,9},{15,... | collective-permute-start | bytes 786440 | tf_op jit(solution)/shard_map/scatter_aggregate/ppermute | solution.py:35
  55.6 14.5 %collective-permute-start.20 = (bf16[1024,128]{1,0:T(8,128)(2,1)S(1)}, bf16[1024,128]{1,0:T(8,128)(2,1)S(1)}, u32[]{:S(2)}, u32[]{:S(2)}) collective-permute-start(bf16[1024,128]{1,0:T(8,128)(2,1)S(1)} %get-tuple-element.74), channel_id=1, source_target_pairs={{3,0},{0,1},{1,2},{2,3},{7,4},{4,5},{5,6},{6,7},{11,8},{8,9},{9,10... | collective-permute-start | bytes 786440 | tf_op jit(solution)/shard_map/scatter_aggregate/ppermute | solution.py:35
  58.4 13.4 %collective-permute-start.21 = (bf16[1024,128]{1,0:T(8,128)(2,1)S(1)}, bf16[1024,128]{1,0:T(8,128)(2,1)S(1)}, u32[]{:S(2)}, u32[]{:S(2)}) collective-permute-start(bf16[1024,128]{1,0:T(8,128)(2,1)S(1)} %get-tuple-element.75), channel_id=1, source_target_pairs={{1,0},{2,1},{3,2},{0,3},{5,4},{6,5},{7,6},{4,7},{9,8},{10,9},{11,1... | collective-permute-start | bytes 786440 | tf_op jit(solution)/shard_map/scatter_aggregate/ppermute | solution.py:35
  73.6 11.9 %collective-permute-start.25 = (bf16[8,128,128]{2,1,0:T(8,128)(2,1)S(1)}, bf16[8,128,128]{2,1,0:T(8,128)(2,1)S(1)}, u32[]{:S(2)}, u32[]{:S(2)}) collective-permute-start(bf16[8,128,128]{2,1,0:T(8,128)(2,1)S(1)} %get-tuple-element.85.refs_0_), channel_id=1, source_target_pairs={{3,0},{0,1},{1,2},{2,3},{7,4},{4,5},{5,6},{6,7},{11,8},{8,9},{9,10... | collective-permute-start | bytes 786440 | tf_op jit(solution)/shard_map/gather_gradients/ppermute | solution.py:35
  74.4 11.7 %collective-permute-start.24 = (bf16[8,128,128]{2,1,0:T(8,128)(2,1)S(1)}, bf16[8,128,128]{2,1,0:T(8,128)(2,1)S(1)}, u32[]{:S(2)}, u32[]{:S(2)}) collective-permute-start(bf16[8,128,128]{2,1,0:T(8,128)(2,1)S(1)} %get-tuple-element.85.refs_0_), channel_id=1, source_target_pairs={{1,0},{2,1},{3,2},{0,3},{5,4},{6,5},{7,6},{4,7},{9,8},{10,9},{11,1... | collective-permute-start | bytes 786440 | tf_op jit(solution)/shard_map/gather_gradients/ppermute | solution.py:35
  76.8 13.0 %collective-permute-start.23 = (bf16[8,128,128]{2,1,0:T(8,128)(2,1)S(1)}, bf16[8,128,128]{2,1,0:T(8,128)(2,1)S(1)}, u32[]{:S(2)}, u32[]{:S(2)}) collective-permute-start(bf16[8,128,128]{2,1,0:T(8,128)(2,1)S(1)} %get-tuple-element.85.refs_0_), channel_id=1, source_target_pairs={{2,0},{3,1},{0,2},{1,3},{6,4},{7,5},{4,6},{5,7},{10,8},{11,9},{8,1... | collective-permute-start | bytes 786440 | tf_op jit(solution)/shard_map/gather_gradients/ppermute | solution.py:35
  78.0 11.8 %collective-permute-start.22 = (bf16[8,128,128]{2,1,0:T(8,128)(2,1)S(1)}, bf16[8,128,128]{2,1,0:T(8,128)(2,1)S(1)}, u32[]{:S(2)}, u32[]{:S(2)}) collective-permute-start(bf16[8,128,128]{2,1,0:T(8,128)(2,1)S(1)} %get-tuple-element.85.refs_0_), channel_id=1, source_target_pairs={{4,0},{5,1},{6,2},{7,3},{0,4},{1,5},{2,6},{3,7},{12,8},{13,9},{14,... | collective-permute-start | bytes 786440 | tf_op jit(solution)/shard_map/gather_gradients/ppermute | solution.py:35
  82.0 12.7 %collective-permute-start.30 = (f32[72,256]{1,0:T(8,128)S(1)}, f32[72,256]{1,0:T(8,128)S(1)}, u32[]{:S(2)}, u32[]{:S(2)}) collective-permute-start(f32[72,256]{1,0:T(8,128)S(1)} %get-tuple-element.126), channel_id=1, source_target_pairs={{2,0},{3,1},{0,2},{1,3},{6,4},{7,5},{4,6},{5,7},{10,8},{11,9},{8,1... | collective-permute-start | bytes 221192 | tf_op jit(solution)/shard_map/weight_gradients/ppermute | solution.py:35
  85.5 12.0 %collective-permute-start.31 = (f32[72,256]{1,0:T(8,128)S(1)}, f32[72,256]{1,0:T(8,128)S(1)}, u32[]{:S(2)}, u32[]{:S(2)}) collective-permute-start(f32[72,256]{1,0:T(8,128)S(1)} %get-tuple-element.127), channel_id=1, source_target_pairs={{1,0},{2,1},{3,2},{0,3},{5,4},{6,5},{7,6},{4,7},{9,8},{10,9},{11,1... | collective-permute-start | bytes 221192 | tf_op jit(solution)/shard_map/weight_gradients/ppermute | solution.py:35
  86.2 11.3 %collective-permute-start.29 = (f32[72,256]{1,0:T(8,128)S(1)}, f32[72,256]{1,0:T(8,128)S(1)}, u32[]{:S(2)}, u32[]{:S(2)}) collective-permute-start(f32[72,256]{1,0:T(8,128)S(1)} %get-tuple-element.128), channel_id=1, source_target_pairs={{3,0},{0,1},{1,2},{2,3},{7,4},{4,5},{5,6},{6,7},{11,8},{8,9},{9,10... | collective-permute-start | bytes 221192 | tf_op jit(solution)/shard_map/weight_gradients/ppermute | solution.py:35
  89.8 8.4 %collective-permute-start.27 = (bf16[8,128,128]{2,1,0:T(8,128)(2,1)S(1)}, bf16[8,128,128]{2,1,0:T(8,128)(2,1)S(1)}, u32[]{:S(2)}, u32[]{:S(2)}) collective-permute-start(bf16[8,128,128]{2,1,0:T(8,128)(2,1)S(1)} %collective-permute-done.23.refs_2_), channel_id=1, source_target_pairs={{4,0},{5,1},{6,2},{7,3},{0,4},{1,5},{2,6},{3,7},{12,8},{13,9},{14,... | collective-permute-start | bytes 786440 | tf_op jit(solution)/shard_map/gather_gradients/ppermute | solution.py:35
  93.8 7.9 %collective-permute-start.28 = (bf16[8,128,128]{2,1,0:T(8,128)(2,1)S(1)}, bf16[8,128,128]{2,1,0:T(8,128)(2,1)S(1)}, u32[]{:S(2)}, u32[]{:S(2)}) collective-permute-start(bf16[8,128,128]{2,1,0:T(8,128)(2,1)S(1)} %collective-permute-done.22.refs_4_), channel_id=1, source_target_pairs={{3,0},{0,1},{1,2},{2,3},{7,4},{4,5},{5,6},{6,7},{11,8},{8,9},{9,10... | collective-permute-start | bytes 786440 | tf_op jit(solution)/shard_map/gather_gradients/ppermute | solution.py:35
  94.6 8.5 %collective-permute-start.26 = (bf16[8,128,128]{2,1,0:T(8,128)(2,1)S(1)}, bf16[8,128,128]{2,1,0:T(8,128)(2,1)S(1)}, u32[]{:S(2)}, u32[]{:S(2)}) collective-permute-start(bf16[8,128,128]{2,1,0:T(8,128)(2,1)S(1)} %collective-permute-done.22.refs_4_), channel_id=1, source_target_pairs={{1,0},{2,1},{3,2},{0,3},{5,4},{6,5},{7,6},{4,7},{9,8},{10,9},{11,1... | collective-permute-start | bytes 786440 | tf_op jit(solution)/shard_map/gather_gradients/ppermute | solution.py:35
  103.1 10.5 %collective-permute-start.32 = (f32[72,256]{1,0:T(8,128)S(1)}, f32[72,256]{1,0:T(8,128)S(1)}, u32[]{:S(2)}, u32[]{:S(2)}) collective-permute-start(f32[72,256]{1,0:T(8,128)S(1)} %bitcast_add_fusion), channel_id=1, source_target_pairs={{4,0},{5,1},{6,2},{7,3},{0,4},{1,5},{2,6},{3,7},{12,8},{13,9},{14,... | collective-permute-start | bytes 221192 | tf_op jit(solution)/shard_map/scatter_gradients/ppermute | solution.py:35
  113.7 6.3 %collective-permute-start.33 = (bf16[8,8,128,128]{3,2,1,0:T(8,128)(2,1)S(1)}, bf16[8,8,128,128]{3,2,1,0:T(8,128)(2,1)S(1)}, u32[]{:S(2)}, u32[]{:S(2)}) collective-permute-start(bf16[8,8,128,128]{3,2,1,0:T(8,128)(2,1)S(1)} %get-tuple-element.97), channel_id=1, source_target_pairs={{8,0},{0,8},{24,16},{16,24},{40,32},{32,40},{56,48},{48,56},{72,64... | collective-permute-start | bytes 6291464 | tf_op jit(solution)/shard_map/scatter_gradients/ppermute | solution.py:31
  113.7 4.1 %collective-permute-start.36 = (f32[72,256]{1,0:T(8,128)S(1)}, f32[72,256]{1,0:T(8,128)S(1)}, u32[]{:S(2)}, u32[]{:S(2)}) collective-permute-start(f32[72,256]{1,0:T(8,128)S(1)} %add.62), channel_id=1, source_target_pairs={{72,0},{64,8},{88,16},{80,24},{104,32},{96,40},{120,48},{112,56},{... | collective-permute-start | bytes 221192 | tf_op jit(solution)/shard_map/scatter_gradients/ppermute | solution.py:31
  113.8 6.1 %collective-permute-start.35 = (f32[72,256]{1,0:T(8,128)S(1)}, f32[72,256]{1,0:T(8,128)S(1)}, u32[]{:S(2)}, u32[]{:S(2)}) collective-permute-start(f32[72,256]{1,0:T(8,128)S(1)} %add.62), channel_id=1, source_target_pairs={{64,0},{72,8},{80,16},{88,24},{96,32},{104,40},{112,48},{120,56},{... | collective-permute-start | bytes 221192 | tf_op jit(solution)/shard_map/scatter_gradients/ppermute | solution.py:31
  115.9 4.1 %collective-permute-start.34 = (f32[72,256]{1,0:T(8,128)S(1)}, f32[72,256]{1,0:T(8,128)S(1)}, u32[]{:S(2)}, u32[]{:S(2)}) collective-permute-start(f32[72,256]{1,0:T(8,128)S(1)} %add.62), channel_id=1, source_target_pairs={{8,0},{0,8},{24,16},{16,24},{40,32},{32,40},{56,48},{48,56},{72,64... | collective-permute-start | bytes 221192 | tf_op jit(solution)/shard_map/scatter_gradients/ppermute | solution.py:31
  120.7 7.7 %collective-permute-start.43 = (f32[72,256]{1,0:T(8,128)S(1)}, f32[72,256]{1,0:T(8,128)S(1)}, u32[]{:S(2)}, u32[]{:S(2)}) collective-permute-start(f32[72,256]{1,0:T(8,128)S(1)} %add_add_fusion.1), channel_id=1, source_target_pairs={{48,0},{56,8},{0,16},{8,24},{16,32},{24,40},{32,48},{40,56},{112,6... | collective-permute-start | bytes 221192 | tf_op jit(solution)/shard_map/scatter_gradients/ppermute | solution.py:31
  120.7 7.6 %collective-permute-start.42 = (f32[72,256]{1,0:T(8,128)S(1)}, f32[72,256]{1,0:T(8,128)S(1)}, u32[]{:S(2)}, u32[]{:S(2)}) collective-permute-start(f32[72,256]{1,0:T(8,128)S(1)} %add_add_fusion.1), channel_id=1, source_target_pairs={{32,0},{40,8},{48,16},{56,24},{0,32},{8,40},{16,48},{24,56},{96,64... | collective-permute-start | bytes 221192 | tf_op jit(solution)/shard_map/scatter_gradients/ppermute | solution.py:31
  122.3 6.0 %collective-permute-start.41 = (f32[72,256]{1,0:T(8,128)S(1)}, f32[72,256]{1,0:T(8,128)S(1)}, u32[]{:S(2)}, u32[]{:S(2)}) collective-permute-start(f32[72,256]{1,0:T(8,128)S(1)} %add_add_fusion.1), channel_id=1, source_target_pairs={{16,0},{24,8},{32,16},{40,24},{48,32},{56,40},{0,48},{8,56},{80,64... | collective-permute-start | bytes 221192 | tf_op jit(solution)/shard_map/scatter_gradients/ppermute | solution.py:31
  124.0 14.3 %collective-permute-start.38 = (bf16[8,128,128]{2,1,0:T(8,128)(2,1)S(1)}, bf16[8,128,128]{2,1,0:T(8,128)(2,1)S(1)}, u32[]{:S(2)}, u32[]{:S(2)}) collective-permute-start(bf16[8,128,128]{2,1,0:T(8,128)(2,1)S(1)} %get-tuple-element.100), channel_id=1, source_target_pairs={{64,0},{72,8},{80,16},{88,24},{96,32},{104,40},{112,48},{120,56},{... | collective-permute-start | bytes 786440 | tf_op jit(solution)/shard_map/scatter_gradients/ppermute | solution.py:31
  124.7 14.9 %collective-permute-start.39 = (bf16[8,128,128]{2,1,0:T(8,128)(2,1)S(1)}, bf16[8,128,128]{2,1,0:T(8,128)(2,1)S(1)}, u32[]{:S(2)}, u32[]{:S(2)}) collective-permute-start(bf16[8,128,128]{2,1,0:T(8,128)(2,1)S(1)} %get-tuple-element.101), channel_id=1, source_target_pairs={{96,0},{104,8},{112,16},{120,24},{64,32},{72,40},{80,48},{88,56},{... | collective-permute-start | bytes 786440 | tf_op jit(solution)/shard_map/scatter_gradients/ppermute | solution.py:31
  128.4 5.6 %collective-permute-start.46 = (f32[72,256]{1,0:T(8,128)S(1)}, f32[72,256]{1,0:T(8,128)S(1)}, u32[]{:S(2)}, u32[]{:S(2)}) collective-permute-start(f32[72,256]{1,0:T(8,128)S(1)} %add_add_fusion.s0), channel_id=1, source_target_pairs={{3,0},{0,1},{1,2},{2,3},{7,4},{4,5},{5,6},{6,7},{11,8},{8,9},{9,10... | collective-permute-start | bytes 221192 | tf_op jit(solution)/shard_map/scatter_gradients/ppermute | solution.py:35
  128.5 7.1 %collective-permute-start.45 = (f32[72,256]{1,0:T(8,128)S(1)}, f32[72,256]{1,0:T(8,128)S(1)}, u32[]{:S(2)}, u32[]{:S(2)}) collective-permute-start(f32[72,256]{1,0:T(8,128)S(1)} %add_add_fusion.s0), channel_id=1, source_target_pairs={{2,0},{3,1},{0,2},{1,3},{6,4},{7,5},{4,6},{5,7},{10,8},{11,9},{8,1... | collective-permute-start | bytes 221192 | tf_op jit(solution)/shard_map/scatter_gradients/ppermute | solution.py:35
  131.7 5.7 %collective-permute-start.44 = (f32[72,256]{1,0:T(8,128)S(1)}, f32[72,256]{1,0:T(8,128)S(1)}, u32[]{:S(2)}, u32[]{:S(2)}) collective-permute-start(f32[72,256]{1,0:T(8,128)S(1)} %add_add_fusion.s0), channel_id=1, source_target_pairs={{1,0},{2,1},{3,2},{0,3},{5,4},{6,5},{7,6},{4,7},{9,8},{10,9},{11,1... | collective-permute-start | bytes 221192 | tf_op jit(solution)/shard_map/scatter_gradients/ppermute | solution.py:35
  134.0 21.4 %collective-permute-start.37 = (bf16[8,128,128]{2,1,0:T(8,128)(2,1)S(1)}, bf16[8,128,128]{2,1,0:T(8,128)(2,1)S(1)}, u32[]{:S(2)}, u32[]{:S(2)}) collective-permute-start(bf16[8,128,128]{2,1,0:T(8,128)(2,1)S(1)} %get-tuple-element.99), channel_id=1, source_target_pairs={{48,0},{56,8},{0,16},{8,24},{16,32},{24,40},{32,48},{40,56},{112,6... | collective-permute-start | bytes 786440 | tf_op jit(solution)/shard_map/scatter_gradients/ppermute | solution.py:31
  135.6 19.8 %collective-permute-start.40 = (bf16[8,128,128]{2,1,0:T(8,128)(2,1)S(1)}, bf16[8,128,128]{2,1,0:T(8,128)(2,1)S(1)}, u32[]{:S(2)}, u32[]{:S(2)}) collective-permute-start(bf16[8,128,128]{2,1,0:T(8,128)(2,1)S(1)} %get-tuple-element.102), channel_id=1, source_target_pairs={{32,0},{40,8},{48,16},{56,24},{0,32},{8,40},{16,48},{24,56},{96,64... | collective-permute-start | bytes 786440 | tf_op jit(solution)/shard_map/scatter_gradients/ppermute | solution.py:31
  137.5 18.0 %collective-permute-start.47 = (bf16[8,128,128]{2,1,0:T(8,128)(2,1)S(1)}, bf16[8,128,128]{2,1,0:T(8,128)(2,1)S(1)}, u32[]{:S(2)}, u32[]{:S(2)}) collective-permute-start(bf16[8,128,128]{2,1,0:T(8,128)(2,1)S(1)} %get-tuple-element.105), channel_id=1, source_target_pairs={{16,0},{24,8},{32,16},{40,24},{48,32},{56,40},{0,48},{8,56},{80,64... | collective-permute-start | bytes 786440 | tf_op jit(solution)/shard_map/scatter_gradients/ppermute | solution.py:31
  138.3 17.1 %collective-permute-start.48 = (bf16[8,128,128]{2,1,0:T(8,128)(2,1)S(1)}, bf16[8,128,128]{2,1,0:T(8,128)(2,1)S(1)}, u32[]{:S(2)}, u32[]{:S(2)}) collective-permute-start(bf16[8,128,128]{2,1,0:T(8,128)(2,1)S(1)} %get-tuple-element.107), channel_id=1, source_target_pairs={{112,0},{120,8},{64,16},{72,24},{80,32},{88,40},{96,48},{104,56},{... | collective-permute-start | bytes 786440 | tf_op jit(solution)/shard_map/scatter_gradients/ppermute | solution.py:31
  139.6 15.9 %collective-permute-start.49 = (bf16[8,128,128]{2,1,0:T(8,128)(2,1)S(1)}, bf16[8,128,128]{2,1,0:T(8,128)(2,1)S(1)}, u32[]{:S(2)}, u32[]{:S(2)}) collective-permute-start(bf16[8,128,128]{2,1,0:T(8,128)(2,1)S(1)} %get-tuple-element.109), channel_id=1, source_target_pairs={{80,0},{88,8},{96,16},{104,24},{112,32},{120,40},{64,48},{72,56},{... | collective-permute-start | bytes 786440 | tf_op jit(solution)/shard_map/scatter_gradients/ppermute | solution.py:31

commit v4 on v3

--- a/solution.py
+++ b/solution.py
@@ -383,7 +383,8 @@
             name="weight_gradients",
         )(meta, node_features, own_agg, grad_pre, weight_self)
 
-        part = slices[0] + sum(from_narrow(slices[dz], 0, -dz & 3) for dz in (1, 2, 3))
+        sent = [from_narrow(slices[dz].astype(bf16), 0, -dz & 3) for dz in (1, 2, 3)]
+        part = slices[0] + sum(v.astype(f32) for v in sent)
 
     with jax.named_scope("gather_gradients"):
         grads = gather_ring(back, from_narrow, lax.optimization_barrier)

time: 159 us -> 159 us (level)
  waiting for transfers between devices: 50.1 us -> 62.1 us
  Pallas kernels: 30.4 us -> 20 us
    ppermute x21, waiting for transfers between devices: 23.1 us -> 32.2 us  [from_narrow(): lax.ppermute(x, 'narrow', [(narrow_index(n, dx, dz), n) for n in range(8)])]
    pallas_call x1, Pallas kernels: 10.4 us -> 6.5 us  [local(): pl.pallas_call(backward_kernel, out_shape=[pieces, pieces], in_specs=[sme...]
    pallas_call x1, Pallas kernels: 10.2 us -> 6.32 us  [local(): pl.pallas_call(forward_kernel, out_shape=[jax.ShapeDtypeStruct((own_nodes...]
    ppermute x29, waiting for transfers between devices: 27.1 us -> 29.9 us  [from_wide(): lax.ppermute(x, 'wide', [(wide_index(w, dx, dy, dc), w) for w in range(16)])]
    pallas_call x1, Pallas kernels: 5.16 us -> 2.55 us  [local(): pl.pallas_call(plan_kernel, out_shape=[jax.ShapeDtypeStruct((3, (slots +...]
    ppermute x21, starting transfers between devices: 39.5 us -> 37.2 us  [from_narrow(): lax.ppermute(x, 'narrow', [(narrow_index(n, dx, dz), n) for n in range(8)])]
  transfers between devices with their start and end apart: 50 -> 50, of which waited for: 20 -> 24; matrix products, arithmetic and copies ran while one was open for 0% -> 0% of each run, Pallas kernels for 11% -> 6%
where the time goes in v4:
time: 159 us; the launch traced here: 158 us
  starting transfers between devices  70 us (44%)
  waiting for transfers between devices  62.1 us (39%)
  Pallas kernels  20 us (13%)
  local copies, waits for them, and re-layouts  3 us (2%)
    ppermute x21, starting transfers between devices, from_narrow(): lax.ppermute(x, 'narrow', [(narrow_index(n, dx, dz), n) for n in range(8)])  37.2 us
    ppermute x29, starting transfers between devices, from_wide(): lax.ppermute(x, 'wide', [(wide_index(w, dx, dy, dc), w) for w in range(16)])  32.8 us
    ppermute x21, waiting for transfers between devices, from_narrow(): lax.ppermute(x, 'narrow', [(narrow_index(n, dx, dz), n) for n in range(8)])  32.2 us
    ppermute x29, waiting for transfers between devices, from_wide(): lax.ppermute(x, 'wide', [(wide_index(w, dx, dy, dc), w) for w in range(16)])  29.9 us
    pallas_call x1, Pallas kernels, local(): pl.pallas_call(backward_kernel, out_shape=[pieces, pieces], in_specs=[sme...  6.5 us
    pallas_call x1, Pallas kernels, local(): pl.pallas_call(forward_kernel, out_shape=[jax.ShapeDtypeStruct((own_nodes...  6.32 us
  transfers between devices with their start and end apart: 50, of which 24 were waited for; matrix products, arithmetic and copies ran while one was open for 0% of the time, Pallas kernels for 6%

profile of v4, /device:TPU:0, one launch (start us, length us, event | category | flops | bytes accessed | tf_op | source)
XLA Modules:
  0.0 158.0 jit_solution(8784676244739899019)
XLA Ops:
  0.6 1.7 %collective-permute-start.3 = (bf16[1024,128]{1,0:T(8,128)(2,1)}, bf16[1024,128]{1,0:T(8,128)(2,1)S(1)}, u32[]{:S(2)}, u32[]{:S(2)}) collective-permute-start(bf16[1024,128]{1,0:T(8,128)(2,1)} %refs_1_.1), channel_id=1, source_target_pairs={{48,0},{56,8},{0,16},{8,24},{16,32},{24,40},{32,48},{40,56},{112,6... | collective-permute-start | bytes 786440 | tf_op jit(solution)/shard_map/gather_features/ppermute | solution.py:31
  2.4 1.6 collective-permute-start.2
  3.9 2.1 %collective-permute-start.1 = (bf16[1024,128]{1,0:T(8,128)(2,1)}, bf16[1024,128]{1,0:T(8,128)(2,1)S(1)}, u32[]{:S(2)}, u32[]{:S(2)}) collective-permute-start(bf16[1024,128]{1,0:T(8,128)(2,1)} %refs_1_.1), channel_id=1, source_target_pairs={{32,0},{40,8},{48,16},{56,24},{0,32},{8,40},{16,48},{24,56},{96,64... | collective-permute-start | bytes 786440 | tf_op jit(solution)/shard_map/gather_features/ppermute | solution.py:31
  6.0 1.5 collective-permute-start
  8.2 0.6 pad_add_fusion.meta.refs_0_
  8.7 2.5 %plan.1 = (s32[3,320]{1,0:T(4,128)}, s32[1]{0:T(128)}) custom-call(s32[4]{0:T(128)} %pad_add_fusion.meta.refs_0_, s32[512]{0:T(512)} %rows.1), custom_call_target="tpu_custom_call" | custom-call | tf_op jit(solution)/shard_map/plan/plan/pallas_call | solution.py:295
  11.3 4.1 %collective-permute-done.2.refs_1_ = bf16[1024,128]{1,0:T(8,128)(2,1)S(1)} collective-permute-done((bf16[1024,128]{1,0:T(8,128)(2,1)}, bf16[1024,128]{1,0:T(8,128)(2,1)S(1)}, u32[]{:S(2)}, u32[]{:S(2)}) %collective-permute-start.2) | collective-permute-done | bytes 262176 | tf_op jit(solution)/shard_map/gather_features/ppermute | solution.py:31
  15.4 1.7 %collective-permute-done.1.refs_2_ = bf16[1024,128]{1,0:T(8,128)(2,1)S(1)} collective-permute-done((bf16[1024,128]{1,0:T(8,128)(2,1)}, bf16[1024,128]{1,0:T(8,128)(2,1)S(1)}, u32[]{:S(2)}, u32[]{:S(2)}) %collective-permute-start.1) | collective-permute-done | bytes 262176 | tf_op jit(solution)/shard_map/gather_features/ppermute | solution.py:31
  17.6 1.5 collective-permute-start.5
  19.1 1.1 collective-permute-start.6
  20.3 2.1 %collective-permute-start.4 = (bf16[1024,128]{1,0:T(8,128)(2,1)S(1)}, bf16[1024,128]{1,0:T(8,128)(2,1)S(1)}, u32[]{:S(2)}, u32[]{:S(2)}) collective-permute-start(bf16[1024,128]{1,0:T(8,128)(2,1)S(1)} %collective-permute-done.refs_4_), channel_id=1, source_target_pairs={{16,0},{24,8},{32,16},{40,24},{48,32},{56,40},{0,48},{8,56},{80,64... | collective-permute-start | bytes 786440 | tf_op jit(solution)/shard_map/gather_features/ppermute | solution.py:31
  22.9 3.0 %collective-permute-done.5.refs_6_ = bf16[1024,128]{1,0:T(8,128)(2,1)S(1)} collective-permute-done((bf16[1024,128]{1,0:T(8,128)(2,1)S(1)}, bf16[1024,128]{1,0:T(8,128)(2,1)S(1)}, u32[]{:S(2)}, u32[]{:S(2)}) %collective-permute-start.5) | collective-permute-done | bytes 262176 | tf_op jit(solution)/shard_map/gather_features/ppermute | solution.py:31
  25.8 2.4 %collective-permute-done.6.refs_7_ = bf16[1024,128]{1,0:T(8,128)(2,1)S(1)} collective-permute-done((bf16[1024,128]{1,0:T(8,128)(2,1)S(1)}, bf16[1024,128]{1,0:T(8,128)(2,1)S(1)}, u32[]{:S(2)}, u32[]{:S(2)}) %collective-permute-start.6) | collective-permute-done | bytes 262176 | tf_op jit(solution)/shard_map/gather_features/ppermute | solution.py:31
  28.8 1.0 collective-permute-done.14.refs_15_
  30.2 0.9 copy-done
  31.1 0.7 copy-done.4
  31.8 0.7 copy-done.5
  32.5 0.7 copy-done.6
  33.2 6.3 %aggregate.1 = (bf16[1024,128]{1,0:T(8,128)(2,1)S(1)}, bf16[1024,128]{1,0:T(8,128)(2,1)S(1)}, bf16[1024,128]{1,0:T(8,128)(2,1)S(1)}, bf16[1024,128]{1,0:T(8,128)...) custom-call(s32[4]{0:T(128)S(1)} %copy-done.5, ...), custom_call_target="tpu_custom_call" | custom-call | flops 2147483648 | bytes 23068672 | tf_op jit(solution)/shard_map/aggregate/aggregate/pallas_call | solution.py:316
  39.5 5.4 %collective-permute-start.15 = (bf16[1024,128]{1,0:T(8,128)(2,1)S(1)}, bf16[1024,128]{1,0:T(8,128)(2,1)S(1)}, u32[]{:S(2)}, u32[]{:S(2)}) collective-permute-start(bf16[1024,128]{1,0:T(8,128)(2,1)S(1)} %get-tuple-element.69), channel_id=1, source_target_pairs={{6,0},{7,1},{4,2},{5,3},{2,4},{3,5},{0,6},{1,7},{14,8},{15,9},{12,... | collective-permute-start | bytes 786440 | tf_op jit(solution)/shard_map/scatter_aggregate/ppermute | solution.py:35
  44.8 0.8 collective-permute-start.16
  46.1 3.5 %collective-permute-start.18 = (bf16[1024,128]{1,0:T(8,128)(2,1)S(1)}, bf16[1024,128]{1,0:T(8,128)(2,1)S(1)}, u32[]{:S(2)}, u32[]{:S(2)}) collective-permute-start(bf16[1024,128]{1,0:T(8,128)(2,1)S(1)} %get-tuple-element.72), channel_id=1, source_target_pairs={{7,0},{4,1},{5,2},{6,3},{3,4},{0,5},{1,6},{2,7},{15,8},{12,9},{13,... | collective-permute-start | bytes 786440 | tf_op jit(solution)/shard_map/scatter_aggregate/ppermute | solution.py:35
  49.6 2.7 %collective-permute-start.19 = (bf16[1024,128]{1,0:T(8,128)(2,1)S(1)}, bf16[1024,128]{1,0:T(8,128)(2,1)S(1)}, u32[]{:S(2)}, u32[]{:S(2)}) collective-permute-start(bf16[1024,128]{1,0:T(8,128)(2,1)S(1)} %get-tuple-element.73), channel_id=1, source_target_pairs={{5,0},{6,1},{7,2},{4,3},{1,4},{2,5},{3,6},{0,7},{13,8},{14,9},{15,... | collective-permute-start | bytes 786440 | tf_op jit(solution)/shard_map/scatter_aggregate/ppermute | solution.py:35
  52.3 1.1 collective-permute-start.20
  53.4 2.0 %collective-permute-done.16.r2 = bf16[1024,128]{1,0:T(8,128)(2,1)S(1)} collective-permute-done((bf16[1024,128]{1,0:T(8,128)(2,1)S(1)}, bf16[1024,128]{1,0:T(8,128)(2,1)S(1)}, u32[]{:S(2)}, u32[]{:S(2)}) %collective-permute-start.16) | collective-permute-done | bytes 262176 | tf_op jit(solution)/shard_map/scatter_aggregate/ppermute | solution.py:35
  55.4 2.5 %collective-permute-start.21 = (bf16[1024,128]{1,0:T(8,128)(2,1)S(1)}, bf16[1024,128]{1,0:T(8,128)(2,1)S(1)}, u32[]{:S(2)}, u32[]{:S(2)}) collective-permute-start(bf16[1024,128]{1,0:T(8,128)(2,1)S(1)} %get-tuple-element.75), channel_id=1, source_target_pairs={{1,0},{2,1},{3,2},{0,3},{5,4},{6,5},{7,6},{4,7},{9,8},{10,9},{11,1... | collective-permute-start | bytes 786440 | tf_op jit(solution)/shard_map/scatter_aggregate/ppermute | solution.py:35
  57.9 1.4 collective-permute-done.17.r3
  59.3 1.1 collective-permute-done.18.r4
  60.4 9.3 %collective-permute-done.19.r5 = bf16[1024,128]{1,0:T(8,128)(2,1)S(1)} collective-permute-done((bf16[1024,128]{1,0:T(8,128)(2,1)S(1)}, bf16[1024,128]{1,0:T(8,128)(2,1)S(1)}, u32[]{:S(2)}, u32[]{:S(2)}) %collective-permute-start.19) | collective-permute-done | bytes 262176 | tf_op jit(solution)/shard_map/scatter_aggregate/ppermute | solution.py:35
  70.3 2.1 %collective-permute-done.21.r7 = bf16[1024,128]{1,0:T(8,128)(2,1)S(1)} collective-permute-done((bf16[1024,128]{1,0:T(8,128)(2,1)S(1)}, bf16[1024,128]{1,0:T(8,128)(2,1)S(1)}, u32[]{:S(2)}, u32[]{:S(2)}) %collective-permute-start.21) | collective-permute-done | bytes 262176 | tf_op jit(solution)/shard_map/scatter_aggregate/ppermute | solution.py:35
  72.4 1.8 %dense.1 = (bf16[1024,256]{1,0:T(8,128)(2,1)}, bf16[1024,128]{1,0:T(8,128)(2,1)S(1)}, bf16[1024,256]{1,0:T(8,128)(2,1)S(1)}, bf16[8,128,128]{2,1,0:T(8,128)(2,1)S(1)}) custom-call(bf16[1024,128]{1,0:T(8,128)(2,1)S(1)} %get-tuple-element.68.own, bf16[1024,128]{1,0:T(8,128)(2,1)S(1)} %collective-permute-done.15.r1, ...), custom_call_target="tpu_custom_call" | custom-call | tf_op jit(solution)/shard_map/dense/dense/pallas_call | solution.py:344
  74.1 0.8 collective-permute-start.25
  75.0 2.4 %collective-permute-start.24 = (bf16[8,128,128]{2,1,0:T(8,128)(2,1)S(1)}, bf16[8,128,128]{2,1,0:T(8,128)(2,1)S(1)}, u32[]{:S(2)}, u32[]{:S(2)}) collective-permute-start(bf16[8,128,128]{2,1,0:T(8,128)(2,1)S(1)} %get-tuple-element.85.refs_0_), channel_id=1, source_target_pairs={{1,0},{2,1},{3,2},{0,3},{5,4},{6,5},{7,6},{4,7},{9,8},{10,9},{11,1... | collective-permute-start | bytes 786440 | tf_op jit(solution)/shard_map/gather_gradients/ppermute | solution.py:35
  77.4 3.5 %collective-permute-start.22 = (bf16[8,128,128]{2,1,0:T(8,128)(2,1)S(1)}, bf16[8,128,128]{2,1,0:T(8,128)(2,1)S(1)}, u32[]{:S(2)}, u32[]{:S(2)}) collective-permute-start(bf16[8,128,128]{2,1,0:T(8,128)(2,1)S(1)} %get-tuple-element.85.refs_0_), channel_id=1, source_target_pairs={{4,0},{5,1},{6,2},{7,3},{0,4},{1,5},{2,6},{3,7},{12,8},{13,9},{14,... | collective-permute-start | bytes 786440 | tf_op jit(solution)/shard_map/gather_gradients/ppermute | solution.py:35
  80.9 1.0 weight_gradients.1
  82.0 0.9 collective-permute-start.29
  82.9 7.3 %collective-permute-done.25.refs_3_ = bf16[8,128,128]{2,1,0:T(8,128)(2,1)S(1)} collective-permute-done((bf16[8,128,128]{2,1,0:T(8,128)(2,1)S(1)}, bf16[8,128,128]{2,1,0:T(8,128)(2,1)S(1)}, u32[]{:S(2)}, u32[]{:S(2)}) %collective-permute-start.25) | collective-permute-done | bytes 262176 | tf_op jit(solution)/shard_map/gather_gradients/ppermute | solution.py:35
  90.2 3.6 %collective-permute-start.27 = (bf16[8,128,128]{2,1,0:T(8,128)(2,1)S(1)}, bf16[8,128,128]{2,1,0:T(8,128)(2,1)S(1)}, u32[]{:S(2)}, u32[]{:S(2)}) collective-permute-start(bf16[8,128,128]{2,1,0:T(8,128)(2,1)S(1)} %collective-permute-done.23.refs_2_), channel_id=1, source_target_pairs={{4,0},{5,1},{6,2},{7,3},{0,4},{1,5},{2,6},{3,7},{12,8},{13,9},{14,... | collective-permute-start | bytes 786440 | tf_op jit(solution)/shard_map/gather_gradients/ppermute | solution.py:35
  93.8 3.6 %collective-permute-start.28 = (bf16[8,128,128]{2,1,0:T(8,128)(2,1)S(1)}, bf16[8,128,128]{2,1,0:T(8,128)(2,1)S(1)}, u32[]{:S(2)}, u32[]{:S(2)}) collective-permute-start(bf16[8,128,128]{2,1,0:T(8,128)(2,1)S(1)} %collective-permute-done.22.refs_4_), channel_id=1, source_target_pairs={{3,0},{0,1},{1,2},{2,3},{7,4},{4,5},{5,6},{6,7},{11,8},{8,9},{9,10... | collective-permute-start | bytes 786440 | tf_op jit(solution)/shard_map/gather_gradients/ppermute | solution.py:35
  97.4 1.0 collective-permute-start.26
  98.4 1.8 %collective-permute-done.27.refs_6_ = bf16[8,128,128]{2,1,0:T(8,128)(2,1)S(1)} collective-permute-done((bf16[8,128,128]{2,1,0:T(8,128)(2,1)S(1)}, bf16[8,128,128]{2,1,0:T(8,128)(2,1)S(1)}, u32[]{:S(2)}, u32[]{:S(2)}) %collective-permute-start.27) | collective-permute-done | bytes 262176 | tf_op jit(solution)/shard_map/gather_gradients/ppermute | solution.py:35
  100.2 3.8 %collective-permute-done.28.refs_7_ = bf16[8,128,128]{2,1,0:T(8,128)(2,1)S(1)} collective-permute-done((bf16[8,128,128]{2,1,0:T(8,128)(2,1)S(1)}, bf16[8,128,128]{2,1,0:T(8,128)(2,1)S(1)}, u32[]{:S(2)}, u32[]{:S(2)}) %collective-permute-start.28) | collective-permute-done | bytes 262176 | tf_op jit(solution)/shard_map/gather_gradients/ppermute | solution.py:35
  104.0 0.6 collective-permute-done.26.refs_5_
  105.0 6.5 %column_gradients.1 = (bf16[8,8,128,128]{3,2,1,0:T(8,128)(2,1)S(1)}, bf16[8,8,128,128]{3,2,1,0:T(8,128)(2,1)S(1)}) custom-call(s32[4]{0:T(128)S(1)} %copy-done.5, s32[512]{0:T(512)S(1)} %copy-done.6, s32[3,320]{1,0:T(4,128)S(1)} %copy-done.4, s32[1]{0:T(128)} %get-tuple-element.63.total, bf16[512,128,128]{2,1,0:T(8,128)(2,1)} %tiles_hbm.3, ...), custom_call_target="tpu_custom_call" | custom-call | flops 2147483648 | bytes 23068672 | tf_op jit(solution)/shard_map/column_gradients/column_gradients/pallas_call | solution.py:395
  111.5 1.9 %collective-permute-start.33 = (bf16[8,8,128,128]{3,2,1,0:T(8,128)(2,1)S(1)}, bf16[8,8,128,128]{3,2,1,0:T(8,128)(2,1)S(1)}, u32[]{:S(2)}, u32[]{:S(2)}) collective-permute-start(bf16[8,8,128,128]{3,2,1,0:T(8,128)(2,1)S(1)} %get-tuple-element.97), channel_id=1, source_target_pairs={{8,0},{0,8},{24,16},{16,24},{40,32},{32,40},{56,48},{48,56},{72,64... | collective-permute-start | bytes 6291464 | tf_op jit(solution)/shard_map/scatter_gradients/ppermute | solution.py:31
  113.4 1.7 %collective-permute-start.35 = (f32[72,256]{1,0:T(8,128)S(1)}, f32[72,256]{1,0:T(8,128)S(1)}, u32[]{:S(2)}, u32[]{:S(2)}) collective-permute-start(f32[72,256]{1,0:T(8,128)S(1)} %add.62), channel_id=1, source_target_pairs={{64,0},{72,8},{80,16},{88,24},{96,32},{104,40},{112,48},{120,56},{... | collective-permute-start | bytes 221192 | tf_op jit(solution)/shard_map/scatter_gradients/ppermute | solution.py:31
  115.3 2.4 %collective-permute-done.36 = f32[72,256]{1,0:T(8,128)S(1)} collective-permute-done((f32[72,256]{1,0:T(8,128)S(1)}, f32[72,256]{1,0:T(8,128)S(1)}, u32[]{:S(2)}, u32[]{:S(2)}) %collective-permute-start.36) | collective-permute-done | bytes 73760 | tf_op jit(solution)/shard_map/scatter_gradients/ppermute | solution.py:31
  117.7 1.9 %collective-permute-done.35 = f32[72,256]{1,0:T(8,128)S(1)} collective-permute-done((f32[72,256]{1,0:T(8,128)S(1)}, f32[72,256]{1,0:T(8,128)S(1)}, u32[]{:S(2)}, u32[]{:S(2)}) %collective-permute-start.35) | collective-permute-done | bytes 73760 | tf_op jit(solution)/shard_map/scatter_gradients/ppermute | solution.py:31
  119.6 0.7 fusion.6
  120.3 4.9 %collective-permute-start.42 = (f32[72,256]{1,0:T(8,128)S(1)}, f32[72,256]{1,0:T(8,128)S(1)}, u32[]{:S(2)}, u32[]{:S(2)}) collective-permute-start(f32[72,256]{1,0:T(8,128)S(1)} %add_add_fusion.1), channel_id=1, source_target_pairs={{32,0},{40,8},{48,16},{56,24},{0,32},{8,40},{16,48},{24,56},{96,64... | collective-permute-start | bytes 221192 | tf_op jit(solution)/shard_map/scatter_gradients/ppermute | solution.py:31
  125.2 1.7 %collective-permute-start.38 = (bf16[8,128,128]{2,1,0:T(8,128)(2,1)S(1)}, bf16[8,128,128]{2,1,0:T(8,128)(2,1)S(1)}, u32[]{:S(2)}, u32[]{:S(2)}) collective-permute-start(bf16[8,128,128]{2,1,0:T(8,128)(2,1)S(1)} %get-tuple-element.100), channel_id=1, source_target_pairs={{64,0},{72,8},{80,16},{88,24},{96,32},{104,40},{112,48},{120,56},{... | collective-permute-start | bytes 786440 | tf_op jit(solution)/shard_map/scatter_gradients/ppermute | solution.py:31
  126.9 1.3 collective-permute-start.39
  128.3 1.2 collective-permute-done.41
  129.6 1.3 collective-permute-start.46
  130.9 1.1 collective-permute-start.45
  132.0 2.1 %collective-permute-start.44 = (f32[72,256]{1,0:T(8,128)S(1)}, f32[72,256]{1,0:T(8,128)S(1)}, u32[]{:S(2)}, u32[]{:S(2)}) collective-permute-start(f32[72,256]{1,0:T(8,128)S(1)} %add_add_fusion.s0), channel_id=1, source_target_pairs={{1,0},{2,1},{3,2},{0,3},{5,4},{6,5},{7,6},{4,7},{9,8},{10,9},{11,1... | collective-permute-start | bytes 221192 | tf_op jit(solution)/shard_map/scatter_gradients/ppermute | solution.py:35
  134.2 1.1 collective-permute-done.46.s3
  135.6 1.1 collective-permute-done.45.s2
  136.7 2.5 %collective-permute-start.40 = (bf16[8,128,128]{2,1,0:T(8,128)(2,1)S(1)}, bf16[8,128,128]{2,1,0:T(8,128)(2,1)S(1)}, u32[]{:S(2)}, u32[]{:S(2)}) collective-permute-start(bf16[8,128,128]{2,1,0:T(8,128)(2,1)S(1)} %get-tuple-element.102), channel_id=1, source_target_pairs={{32,0},{40,8},{48,16},{56,24},{0,32},{8,40},{16,48},{24,56},{96,64... | collective-permute-start | bytes 786440 | tf_op jit(solution)/shard_map/scatter_gradients/ppermute | solution.py:31
  139.2 1.0 collective-permute-start.47
  140.2 2.2 %collective-permute-start.48 = (bf16[8,128,128]{2,1,0:T(8,128)(2,1)S(1)}, bf16[8,128,128]{2,1,0:T(8,128)(2,1)S(1)}, u32[]{:S(2)}, u32[]{:S(2)}) collective-permute-start(bf16[8,128,128]{2,1,0:T(8,128)(2,1)S(1)} %get-tuple-element.107), channel_id=1, source_target_pairs={{112,0},{120,8},{64,16},{72,24},{80,32},{88,40},{96,48},{104,56},{... | collective-permute-start | bytes 786440 | tf_op jit(solution)/shard_map/scatter_gradients/ppermute | solution.py:31
  142.4 2.0 %collective-permute-start.49 = (bf16[8,128,128]{2,1,0:T(8,128)(2,1)S(1)}, bf16[8,128,128]{2,1,0:T(8,128)(2,1)S(1)}, u32[]{:S(2)}, u32[]{:S(2)}) collective-permute-start(bf16[8,128,128]{2,1,0:T(8,128)(2,1)S(1)} %get-tuple-element.109), channel_id=1, source_target_pairs={{80,0},{88,8},{96,16},{104,24},{112,32},{120,40},{64,48},{72,56},{... | collective-permute-start | bytes 786440 | tf_op jit(solution)/shard_map/scatter_gradients/ppermute | solution.py:31
  144.4 11.5 %collective-permute-done.40.r2 = bf16[8,128,128]{2,1,0:T(8,128)(2,1)S(1)} collective-permute-done((bf16[8,128,128]{2,1,0:T(8,128)(2,1)S(1)}, bf16[8,128,128]{2,1,0:T(8,128)(2,1)S(1)}, u32[]{:S(2)}, u32[]{:S(2)}) %collective-permute-start.40) | collective-permute-done | bytes 262176 | tf_op jit(solution)/shard_map/scatter_gradients/ppermute | solution.py:31
  156.1 1.9 %grad_input.1 = (bf16[1024,128]{1,0:T(8,128)(2,1)}, f32[128,256]{1,0:T(8,128)}, f32[128,256]{1,0:T(8,128)}, f32[1,256]{1,0:T(1,128)}) custom-call(s32[4]{0:T(128)S(1)} %copy-done.5, bf16[8,8,128,128]{3,2,1,0:T(8,128)(2,1)S(1)} %get-tuple-element.96.keep, bf16[8,8,128,128]{3,2,1,0:T(8,128)(2,1)S(1)} %collective-permute-done.33.swapped, ...), custom_call_target="tpu_custom_call" | custom-call | tf_op jit(solution)/shard_map/grad_input/grad_input/pallas_call | solution.py:445
  (66 shorter events, 4.4 us)
Async XLA Ops:
  0.6 10.7 %collective-permute-start.3 = (bf16[1024,128]{1,0:T(8,128)(2,1)}, bf16[1024,128]{1,0:T(8,128)(2,1)S(1)}, u32[]{:S(2)}, u32[]{:S(2)}) collective-permute-start(bf16[1024,128]{1,0:T(8,128)(2,1)} %refs_1_.1), channel_id=1, source_target_pairs={{48,0},{56,8},{0,16},{8,24},{16,32},{24,40},{32,48},{40,56},{112,6... | collective-permute-start | bytes 786440 | tf_op jit(solution)/shard_map/gather_features/ppermute | solution.py:31
  2.4 13.1 %collective-permute-start.2 = (bf16[1024,128]{1,0:T(8,128)(2,1)}, bf16[1024,128]{1,0:T(8,128)(2,1)S(1)}, u32[]{:S(2)}, u32[]{:S(2)}) collective-permute-start(bf16[1024,128]{1,0:T(8,128)(2,1)} %refs_1_.1), channel_id=1, source_target_pairs={{16,0},{24,8},{32,16},{40,24},{48,32},{56,40},{0,48},{8,56},{80,64... | collective-permute-start | bytes 786440 | tf_op jit(solution)/shard_map/gather_features/ppermute | solution.py:31
  3.9 13.2 %collective-permute-start.1 = (bf16[1024,128]{1,0:T(8,128)(2,1)}, bf16[1024,128]{1,0:T(8,128)(2,1)S(1)}, u32[]{:S(2)}, u32[]{:S(2)}) collective-permute-start(bf16[1024,128]{1,0:T(8,128)(2,1)} %refs_1_.1), channel_id=1, source_target_pairs={{32,0},{40,8},{48,16},{56,24},{0,32},{8,40},{16,48},{24,56},{96,64... | collective-permute-start | bytes 786440 | tf_op jit(solution)/shard_map/gather_features/ppermute | solution.py:31
  6.0 11.1 %collective-permute-start = (bf16[1024,128]{1,0:T(8,128)(2,1)}, bf16[1024,128]{1,0:T(8,128)(2,1)S(1)}, u32[]{:S(2)}, u32[]{:S(2)}) collective-permute-start(bf16[1024,128]{1,0:T(8,128)(2,1)} %refs_1_.1), channel_id=1, source_target_pairs={{64,0},{72,8},{80,16},{88,24},{96,32},{104,40},{112,48},{120,56},{... | collective-permute-start | bytes 786440 | tf_op jit(solution)/shard_map/gather_features/ppermute | solution.py:31
  7.5 12.8 %collective-permute-start.7 = (bf16[1024,128]{1,0:T(8,128)(2,1)}, bf16[1024,128]{1,0:T(8,128)(2,1)S(1)}, u32[]{:S(2)}, u32[]{:S(2)}) collective-permute-start(bf16[1024,128]{1,0:T(8,128)(2,1)} %refs_1_.1), channel_id=1, source_target_pairs={{8,0},{0,8},{24,16},{16,24},{40,32},{32,40},{56,48},{48,56},{72,64... | collective-permute-start | bytes 786440 | tf_op jit(solution)/shard_map/gather_features/ppermute | solution.py:31
  17.1 5.2 %collective-permute-start.8 = (bf16[1024,128]{1,0:T(8,128)(2,1)S(1)}, bf16[1024,128]{1,0:T(8,128)(2,1)S(1)}, u32[]{:S(2)}, u32[]{:S(2)}) collective-permute-start(bf16[1024,128]{1,0:T(8,128)(2,1)S(1)} %collective-permute-done.2.refs_1_), channel_id=1, source_target_pairs={{8,0},{0,8},{24,16},{16,24},{40,32},{32,40},{56,48},{48,56},{72,64... | collective-permute-start | bytes 786440 | tf_op jit(solution)/shard_map/gather_features/ppermute | solution.py:31
  17.1 5.3 %collective-permute-start.10 = (bf16[1024,128]{1,0:T(8,128)(2,1)S(1)}, bf16[1024,128]{1,0:T(8,128)(2,1)S(1)}, u32[]{:S(2)}, u32[]{:S(2)}) collective-permute-start(bf16[1024,128]{1,0:T(8,128)(2,1)S(1)} %collective-permute-done.3.refs_3_), channel_id=1, source_target_pairs={{8,0},{0,8},{24,16},{16,24},{40,32},{32,40},{56,48},{48,56},{72,64... | collective-permute-start | bytes 786440 | tf_op jit(solution)/shard_map/gather_features/ppermute | solution.py:31
  17.6 8.2 %collective-permute-start.5 = (bf16[1024,128]{1,0:T(8,128)(2,1)S(1)}, bf16[1024,128]{1,0:T(8,128)(2,1)S(1)}, u32[]{:S(2)}, u32[]{:S(2)}) collective-permute-start(bf16[1024,128]{1,0:T(8,128)(2,1)S(1)} %collective-permute-done.1.refs_2_), channel_id=1, source_target_pairs={{64,0},{72,8},{80,16},{88,24},{96,32},{104,40},{112,48},{120,56},{... | collective-permute-start | bytes 786440 | tf_op jit(solution)/shard_map/gather_features/ppermute | solution.py:31
  19.1 9.1 %collective-permute-start.6 = (bf16[1024,128]{1,0:T(8,128)(2,1)S(1)}, bf16[1024,128]{1,0:T(8,128)(2,1)S(1)}, u32[]{:S(2)}, u32[]{:S(2)}) collective-permute-start(bf16[1024,128]{1,0:T(8,128)(2,1)S(1)} %collective-permute-done.refs_4_), channel_id=1, source_target_pairs={{48,0},{56,8},{0,16},{8,24},{16,32},{24,40},{32,48},{40,56},{112,6... | collective-permute-start | bytes 786440 | tf_op jit(solution)/shard_map/gather_features/ppermute | solution.py:31
  20.3 8.0 %collective-permute-start.4 = (bf16[1024,128]{1,0:T(8,128)(2,1)S(1)}, bf16[1024,128]{1,0:T(8,128)(2,1)S(1)}, u32[]{:S(2)}, u32[]{:S(2)}) collective-permute-start(bf16[1024,128]{1,0:T(8,128)(2,1)S(1)} %collective-permute-done.refs_4_), channel_id=1, source_target_pairs={{16,0},{24,8},{32,16},{40,24},{48,32},{56,40},{0,48},{8,56},{80,64... | collective-permute-start | bytes 786440 | tf_op jit(solution)/shard_map/gather_features/ppermute | solution.py:31
  22.4 6.4 %collective-permute-start.9 = (bf16[1024,128]{1,0:T(8,128)(2,1)S(1)}, bf16[1024,128]{1,0:T(8,128)(2,1)S(1)}, u32[]{:S(2)}, u32[]{:S(2)}) collective-permute-start(bf16[1024,128]{1,0:T(8,128)(2,1)S(1)} %collective-permute-done.1.refs_2_), channel_id=1, source_target_pairs={{8,0},{0,8},{24,16},{16,24},{40,32},{32,40},{56,48},{48,56},{72,64... | collective-permute-start | bytes 786440 | tf_op jit(solution)/shard_map/gather_features/ppermute | solution.py:31
  22.4 6.4 %collective-permute-start.11 = (bf16[1024,128]{1,0:T(8,128)(2,1)S(1)}, bf16[1024,128]{1,0:T(8,128)(2,1)S(1)}, u32[]{:S(2)}, u32[]{:S(2)}) collective-permute-start(bf16[1024,128]{1,0:T(8,128)(2,1)S(1)} %collective-permute-done.refs_4_), channel_id=1, source_target_pairs={{8,0},{0,8},{24,16},{16,24},{40,32},{32,40},{56,48},{48,56},{72,64... | collective-permute-start | bytes 786440 | tf_op jit(solution)/shard_map/gather_features/ppermute | solution.py:31
  25.8 2.9 %collective-permute-start.13 = (bf16[1024,128]{1,0:T(8,128)(2,1)S(1)}, bf16[1024,128]{1,0:T(8,128)(2,1)S(1)}, u32[]{:S(2)}, u32[]{:S(2)}) collective-permute-start(bf16[1024,128]{1,0:T(8,128)(2,1)S(1)} %collective-permute-done.5.refs_6_), channel_id=1, source_target_pairs={{8,0},{0,8},{24,16},{16,24},{40,32},{32,40},{56,48},{48,56},{72,64... | collective-permute-start | bytes 786440 | tf_op jit(solution)/shard_map/gather_features/ppermute | solution.py:31
  28.3 1.5 collective-permute-start.14
  28.3 1.9 %collective-permute-start.12 = (bf16[1024,128]{1,0:T(8,128)(2,1)S(1)}, bf16[1024,128]{1,0:T(8,128)(2,1)S(1)}, u32[]{:S(2)}, u32[]{:S(2)}) collective-permute-start(bf16[1024,128]{1,0:T(8,128)(2,1)S(1)} %collective-permute-done.4.refs_5_), channel_id=1, source_target_pairs={{8,0},{0,8},{24,16},{16,24},{40,32},{32,40},{56,48},{48,56},{72,64... | collective-permute-start | bytes 786440 | tf_op jit(solution)/shard_map/gather_features/ppermute | solution.py:31
  30.2 1.0 copy-start
  31.1 0.7 copy-start.4
  31.8 0.7 copy-start.5
  32.5 0.7 copy-start.6
  33.2 39.2 %copy-start.1 = (bf16[1024,256]{1,0:T(8,128)(2,1)S(1)}, bf16[1024,256]{1,0:T(8,128)(2,1)}, u32[]{:S(2)}) copy-start(bf16[1024,256]{1,0:T(8,128)(2,1)} %grad.1) | copy-start | bytes 1572868
  33.2 39.2 %copy-start.2 = (bf16[128,256]{1,0:T(8,128)(2,1)S(1)}, bf16[128,256]{1,0:T(8,128)(2,1)}, u32[]{:S(2)}) copy-start(bf16[128,256]{1,0:T(8,128)(2,1)} %refs_4_.1) | copy-start | bytes 196612
  33.2 39.2 %copy-start.3 = (bf16[128,256]{1,0:T(8,128)(2,1)S(1)}, bf16[128,256]{1,0:T(8,128)(2,1)}, u32[]{:S(2)}) copy-start(bf16[128,256]{1,0:T(8,128)(2,1)} %wn.1) | copy-start | bytes 196612
  33.2 39.2 %copy-start.7 = (f32[256]{0:T(256)S(1)}, f32[256]{0:T(256)}, u32[]{:S(2)}) copy-start(f32[256]{0:T(256)} %param.16) | copy-start | bytes 3076
  39.5 12.8 %collective-permute-start.15 = (bf16[1024,128]{1,0:T(8,128)(2,1)S(1)}, bf16[1024,128]{1,0:T(8,128)(2,1)S(1)}, u32[]{:S(2)}, u32[]{:S(2)}) collective-permute-start(bf16[1024,128]{1,0:T(8,128)(2,1)S(1)} %get-tuple-element.69), channel_id=1, source_target_pairs={{6,0},{7,1},{4,2},{5,3},{2,4},{3,5},{0,6},{1,7},{14,8},{15,9},{12,... | collective-permute-start | bytes 786440 | tf_op jit(solution)/shard_map/scatter_aggregate/ppermute | solution.py:35
  44.8 10.6 %collective-permute-start.16 = (bf16[1024,128]{1,0:T(8,128)(2,1)S(1)}, bf16[1024,128]{1,0:T(8,128)(2,1)S(1)}, u32[]{:S(2)}, u32[]{:S(2)}) collective-permute-start(bf16[1024,128]{1,0:T(8,128)(2,1)S(1)} %get-tuple-element.70), channel_id=1, source_target_pairs={{4,0},{5,1},{6,2},{7,3},{0,4},{1,5},{2,6},{3,7},{12,8},{13,9},{14,... | collective-permute-start | bytes 786440 | tf_op jit(solution)/shard_map/scatter_aggregate/ppermute | solution.py:35
  45.6 13.7 %collective-permute-start.17 = (bf16[1024,128]{1,0:T(8,128)(2,1)S(1)}, bf16[1024,128]{1,0:T(8,128)(2,1)S(1)}, u32[]{:S(2)}, u32[]{:S(2)}) collective-permute-start(bf16[1024,128]{1,0:T(8,128)(2,1)S(1)} %get-tuple-element.71), channel_id=1, source_target_pairs={{2,0},{3,1},{0,2},{1,3},{6,4},{7,5},{4,6},{5,7},{10,8},{11,9},{8,1... | collective-permute-start | bytes 786440 | tf_op jit(solution)/shard_map/scatter_aggregate/ppermute | solution.py:35
  46.1 14.4 %collective-permute-start.18 = (bf16[1024,128]{1,0:T(8,128)(2,1)S(1)}, bf16[1024,128]{1,0:T(8,128)(2,1)S(1)}, u32[]{:S(2)}, u32[]{:S(2)}) collective-permute-start(bf16[1024,128]{1,0:T(8,128)(2,1)S(1)} %get-tuple-element.72), channel_id=1, source_target_pairs={{7,0},{4,1},{5,2},{6,3},{3,4},{0,5},{1,6},{2,7},{15,8},{12,9},{13,... | collective-permute-start | bytes 786440 | tf_op jit(solution)/shard_map/scatter_aggregate/ppermute | solution.py:35
  49.6 20.1 %collective-permute-start.19 = (bf16[1024,128]{1,0:T(8,128)(2,1)S(1)}, bf16[1024,128]{1,0:T(8,128)(2,1)S(1)}, u32[]{:S(2)}, u32[]{:S(2)}) collective-permute-start(bf16[1024,128]{1,0:T(8,128)(2,1)S(1)} %get-tuple-element.73), channel_id=1, source_target_pairs={{5,0},{6,1},{7,2},{4,3},{1,4},{2,5},{3,6},{0,7},{13,8},{14,9},{15,... | collective-permute-start | bytes 786440 | tf_op jit(solution)/shard_map/scatter_aggregate/ppermute | solution.py:35
  52.3 18.0 %collective-permute-start.20 = (bf16[1024,128]{1,0:T(8,128)(2,1)S(1)}, bf16[1024,128]{1,0:T(8,128)(2,1)S(1)}, u32[]{:S(2)}, u32[]{:S(2)}) collective-permute-start(bf16[1024,128]{1,0:T(8,128)(2,1)S(1)} %get-tuple-element.74), channel_id=1, source_target_pairs={{3,0},{0,1},{1,2},{2,3},{7,4},{4,5},{5,6},{6,7},{11,8},{8,9},{9,10... | collective-permute-start | bytes 786440 | tf_op jit(solution)/shard_map/scatter_aggregate/ppermute | solution.py:35
  55.4 17.0 %collective-permute-start.21 = (bf16[1024,128]{1,0:T(8,128)(2,1)S(1)}, bf16[1024,128]{1,0:T(8,128)(2,1)S(1)}, u32[]{:S(2)}, u32[]{:S(2)}) collective-permute-start(bf16[1024,128]{1,0:T(8,128)(2,1)S(1)} %get-tuple-element.75), channel_id=1, source_target_pairs={{1,0},{2,1},{3,2},{0,3},{5,4},{6,5},{7,6},{4,7},{9,8},{10,9},{11,1... | collective-permute-start | bytes 786440 | tf_op jit(solution)/shard_map/scatter_aggregate/ppermute | solution.py:35
  74.1 16.0 %collective-permute-start.25 = (bf16[8,128,128]{2,1,0:T(8,128)(2,1)S(1)}, bf16[8,128,128]{2,1,0:T(8,128)(2,1)S(1)}, u32[]{:S(2)}, u32[]{:S(2)}) collective-permute-start(bf16[8,128,128]{2,1,0:T(8,128)(2,1)S(1)} %get-tuple-element.85.refs_0_), channel_id=1, source_target_pairs={{3,0},{0,1},{1,2},{2,3},{7,4},{4,5},{5,6},{6,7},{11,8},{8,9},{9,10... | collective-permute-start | bytes 786440 | tf_op jit(solution)/shard_map/gather_gradients/ppermute | solution.py:35
  75.0 15.2 %collective-permute-start.24 = (bf16[8,128,128]{2,1,0:T(8,128)(2,1)S(1)}, bf16[8,128,128]{2,1,0:T(8,128)(2,1)S(1)}, u32[]{:S(2)}, u32[]{:S(2)}) collective-permute-start(bf16[8,128,128]{2,1,0:T(8,128)(2,1)S(1)} %get-tuple-element.85.refs_0_), channel_id=1, source_target_pairs={{1,0},{2,1},{3,2},{0,3},{5,4},{6,5},{7,6},{4,7},{9,8},{10,9},{11,1... | collective-permute-start | bytes 786440 | tf_op jit(solution)/shard_map/gather_gradients/ppermute | solution.py:35
  77.4 12.8 %collective-permute-start.23 = (bf16[8,128,128]{2,1,0:T(8,128)(2,1)S(1)}, bf16[8,128,128]{2,1,0:T(8,128)(2,1)S(1)}, u32[]{:S(2)}, u32[]{:S(2)}) collective-permute-start(bf16[8,128,128]{2,1,0:T(8,128)(2,1)S(1)} %get-tuple-element.85.refs_0_), channel_id=1, source_target_pairs={{2,0},{3,1},{0,2},{1,3},{6,4},{7,5},{4,6},{5,7},{10,8},{11,9},{8,1... | collective-permute-start | bytes 786440 | tf_op jit(solution)/shard_map/gather_gradients/ppermute | solution.py:35
  77.4 12.8 %collective-permute-start.22 = (bf16[8,128,128]{2,1,0:T(8,128)(2,1)S(1)}, bf16[8,128,128]{2,1,0:T(8,128)(2,1)S(1)}, u32[]{:S(2)}, u32[]{:S(2)}) collective-permute-start(bf16[8,128,128]{2,1,0:T(8,128)(2,1)S(1)} %get-tuple-element.85.refs_0_), channel_id=1, source_target_pairs={{4,0},{5,1},{6,2},{7,3},{0,4},{1,5},{2,6},{3,7},{12,8},{13,9},{14,... | collective-permute-start | bytes 786440 | tf_op jit(solution)/shard_map/gather_gradients/ppermute | solution.py:35
  82.0 15.5 %collective-permute-start.29 = (bf16[72,256]{1,0:T(8,128)(2,1)S(1)}, bf16[72,256]{1,0:T(8,128)(2,1)S(1)}, u32[]{:S(2)}, u32[]{:S(2)}) collective-permute-start(bf16[72,256]{1,0:T(8,128)(2,1)S(1)} %get-tuple-element.126), channel_id=1, source_target_pairs={{3,0},{0,1},{1,2},{2,3},{7,4},{4,5},{5,6},{6,7},{11,8},{8,9},{9,10... | collective-permute-start | bytes 110600 | tf_op jit(solution)/shard_map/weight_gradients/ppermute | solution.py:35
  90.2 8.2 %collective-permute-start.31 = (bf16[72,256]{1,0:T(8,128)(2,1)S(1)}, bf16[72,256]{1,0:T(8,128)(2,1)S(1)}, u32[]{:S(2)}, u32[]{:S(2)}) collective-permute-start(bf16[72,256]{1,0:T(8,128)(2,1)S(1)} %get-tuple-element.127), channel_id=1, source_target_pairs={{1,0},{2,1},{3,2},{0,3},{5,4},{6,5},{7,6},{4,7},{9,8},{10,9},{11,1... | collective-permute-start | bytes 110600 | tf_op jit(solution)/shard_map/weight_gradients/ppermute | solution.py:35
  90.2 8.2 %collective-permute-start.30 = (bf16[72,256]{1,0:T(8,128)(2,1)S(1)}, bf16[72,256]{1,0:T(8,128)(2,1)S(1)}, u32[]{:S(2)}, u32[]{:S(2)}) collective-permute-start(bf16[72,256]{1,0:T(8,128)(2,1)S(1)} %get-tuple-element.128), channel_id=1, source_target_pairs={{2,0},{3,1},{0,2},{1,3},{6,4},{7,5},{4,6},{5,7},{10,8},{11,9},{8,1... | collective-permute-start | bytes 110600 | tf_op jit(solution)/shard_map/weight_gradients/ppermute | solution.py:35
  90.2 10.0 %collective-permute-start.27 = (bf16[8,128,128]{2,1,0:T(8,128)(2,1)S(1)}, bf16[8,128,128]{2,1,0:T(8,128)(2,1)S(1)}, u32[]{:S(2)}, u32[]{:S(2)}) collective-permute-start(bf16[8,128,128]{2,1,0:T(8,128)(2,1)S(1)} %collective-permute-done.23.refs_2_), channel_id=1, source_target_pairs={{4,0},{5,1},{6,2},{7,3},{0,4},{1,5},{2,6},{3,7},{12,8},{13,9},{14,... | collective-permute-start | bytes 786440 | tf_op jit(solution)/shard_map/gather_gradients/ppermute | solution.py:35
  93.8 10.2 %collective-permute-start.28 = (bf16[8,128,128]{2,1,0:T(8,128)(2,1)S(1)}, bf16[8,128,128]{2,1,0:T(8,128)(2,1)S(1)}, u32[]{:S(2)}, u32[]{:S(2)}) collective-permute-start(bf16[8,128,128]{2,1,0:T(8,128)(2,1)S(1)} %collective-permute-done.22.refs_4_), channel_id=1, source_target_pairs={{3,0},{0,1},{1,2},{2,3},{7,4},{4,5},{5,6},{6,7},{11,8},{8,9},{9,10... | collective-permute-start | bytes 786440 | tf_op jit(solution)/shard_map/gather_gradients/ppermute | solution.py:35
  97.4 7.1 %collective-permute-start.26 = (bf16[8,128,128]{2,1,0:T(8,128)(2,1)S(1)}, bf16[8,128,128]{2,1,0:T(8,128)(2,1)S(1)}, u32[]{:S(2)}, u32[]{:S(2)}) collective-permute-start(bf16[8,128,128]{2,1,0:T(8,128)(2,1)S(1)} %collective-permute-done.22.refs_4_), channel_id=1, source_target_pairs={{1,0},{2,1},{3,2},{0,3},{5,4},{6,5},{7,6},{4,7},{9,8},{10,9},{11,1... | collective-permute-start | bytes 786440 | tf_op jit(solution)/shard_map/gather_gradients/ppermute | solution.py:35
  104.6 6.9 %collective-permute-start.32 = (f32[72,256]{1,0:T(8,128)S(1)}, f32[72,256]{1,0:T(8,128)S(1)}, u32[]{:S(2)}, u32[]{:S(2)}) collective-permute-start(f32[72,256]{1,0:T(8,128)S(1)} %bitcast_add_fusion), channel_id=1, source_target_pairs={{4,0},{5,1},{6,2},{7,3},{0,4},{1,5},{2,6},{3,7},{12,8},{13,9},{14,... | collective-permute-start | bytes 221192 | tf_op jit(solution)/shard_map/scatter_gradients/ppermute | solution.py:35
  111.5 8.1 %collective-permute-start.33 = (bf16[8,8,128,128]{3,2,1,0:T(8,128)(2,1)S(1)}, bf16[8,8,128,128]{3,2,1,0:T(8,128)(2,1)S(1)}, u32[]{:S(2)}, u32[]{:S(2)}) collective-permute-start(bf16[8,8,128,128]{3,2,1,0:T(8,128)(2,1)S(1)} %get-tuple-element.97), channel_id=1, source_target_pairs={{8,0},{0,8},{24,16},{16,24},{40,32},{32,40},{56,48},{48,56},{72,64... | collective-permute-start | bytes 6291464 | tf_op jit(solution)/shard_map/scatter_gradients/ppermute | solution.py:31
  113.4 4.3 %collective-permute-start.36 = (f32[72,256]{1,0:T(8,128)S(1)}, f32[72,256]{1,0:T(8,128)S(1)}, u32[]{:S(2)}, u32[]{:S(2)}) collective-permute-start(f32[72,256]{1,0:T(8,128)S(1)} %add.62), channel_id=1, source_target_pairs={{72,0},{64,8},{88,16},{80,24},{104,32},{96,40},{120,48},{112,56},{... | collective-permute-start | bytes 221192 | tf_op jit(solution)/shard_map/scatter_gradients/ppermute | solution.py:31
  113.4 6.1 %collective-permute-start.35 = (f32[72,256]{1,0:T(8,128)S(1)}, f32[72,256]{1,0:T(8,128)S(1)}, u32[]{:S(2)}, u32[]{:S(2)}) collective-permute-start(f32[72,256]{1,0:T(8,128)S(1)} %add.62), channel_id=1, source_target_pairs={{64,0},{72,8},{80,16},{88,24},{96,32},{104,40},{112,48},{120,56},{... | collective-permute-start | bytes 221192 | tf_op jit(solution)/shard_map/scatter_gradients/ppermute | solution.py:31
  115.1 4.4 %collective-permute-start.34 = (f32[72,256]{1,0:T(8,128)S(1)}, f32[72,256]{1,0:T(8,128)S(1)}, u32[]{:S(2)}, u32[]{:S(2)}) collective-permute-start(f32[72,256]{1,0:T(8,128)S(1)} %add.62), channel_id=1, source_target_pairs={{8,0},{0,8},{24,16},{16,24},{40,32},{32,40},{56,48},{48,56},{72,64... | collective-permute-start | bytes 221192 | tf_op jit(solution)/shard_map/scatter_gradients/ppermute | solution.py:31
  120.3 8.0 %collective-permute-start.43 = (f32[72,256]{1,0:T(8,128)S(1)}, f32[72,256]{1,0:T(8,128)S(1)}, u32[]{:S(2)}, u32[]{:S(2)}) collective-permute-start(f32[72,256]{1,0:T(8,128)S(1)} %add_add_fusion.1), channel_id=1, source_target_pairs={{48,0},{56,8},{0,16},{8,24},{16,32},{24,40},{32,48},{40,56},{112,6... | collective-permute-start | bytes 221192 | tf_op jit(solution)/shard_map/scatter_gradients/ppermute | solution.py:31
  120.3 8.0 %collective-permute-start.42 = (f32[72,256]{1,0:T(8,128)S(1)}, f32[72,256]{1,0:T(8,128)S(1)}, u32[]{:S(2)}, u32[]{:S(2)}) collective-permute-start(f32[72,256]{1,0:T(8,128)S(1)} %add_add_fusion.1), channel_id=1, source_target_pairs={{32,0},{40,8},{48,16},{56,24},{0,32},{8,40},{16,48},{24,56},{96,64... | collective-permute-start | bytes 221192 | tf_op jit(solution)/shard_map/scatter_gradients/ppermute | solution.py:31
  125.2 4.4 %collective-permute-start.41 = (f32[72,256]{1,0:T(8,128)S(1)}, f32[72,256]{1,0:T(8,128)S(1)}, u32[]{:S(2)}, u32[]{:S(2)}) collective-permute-start(f32[72,256]{1,0:T(8,128)S(1)} %add_add_fusion.1), channel_id=1, source_target_pairs={{16,0},{24,8},{32,16},{40,24},{48,32},{56,40},{0,48},{8,56},{80,64... | collective-permute-start | bytes 221192 | tf_op jit(solution)/shard_map/scatter_gradients/ppermute | solution.py:31
  125.2 15.0 %collective-permute-start.38 = (bf16[8,128,128]{2,1,0:T(8,128)(2,1)S(1)}, bf16[8,128,128]{2,1,0:T(8,128)(2,1)S(1)}, u32[]{:S(2)}, u32[]{:S(2)}) collective-permute-start(bf16[8,128,128]{2,1,0:T(8,128)(2,1)S(1)} %get-tuple-element.100), channel_id=1, source_target_pairs={{64,0},{72,8},{80,16},{88,24},{96,32},{104,40},{112,48},{120,56},{... | collective-permute-start | bytes 786440 | tf_op jit(solution)/shard_map/scatter_gradients/ppermute | solution.py:31
  126.9 15.5 %collective-permute-start.39 = (bf16[8,128,128]{2,1,0:T(8,128)(2,1)S(1)}, bf16[8,128,128]{2,1,0:T(8,128)(2,1)S(1)}, u32[]{:S(2)}, u32[]{:S(2)}) collective-permute-start(bf16[8,128,128]{2,1,0:T(8,128)(2,1)S(1)} %get-tuple-element.101), channel_id=1, source_target_pairs={{96,0},{104,8},{112,16},{120,24},{64,32},{72,40},{80,48},{88,56},{... | collective-permute-start | bytes 786440 | tf_op jit(solution)/shard_map/scatter_gradients/ppermute | solution.py:31
  129.6 5.7 %collective-permute-start.46 = (f32[72,256]{1,0:T(8,128)S(1)}, f32[72,256]{1,0:T(8,128)S(1)}, u32[]{:S(2)}, u32[]{:S(2)}) collective-permute-start(f32[72,256]{1,0:T(8,128)S(1)} %add_add_fusion.s0), channel_id=1, source_target_pairs={{3,0},{0,1},{1,2},{2,3},{7,4},{4,5},{5,6},{6,7},{11,8},{8,9},{9,10... | collective-permute-start | bytes 221192 | tf_op jit(solution)/shard_map/scatter_gradients/ppermute | solution.py:35
  130.9 5.9 %collective-permute-start.45 = (f32[72,256]{1,0:T(8,128)S(1)}, f32[72,256]{1,0:T(8,128)S(1)}, u32[]{:S(2)}, u32[]{:S(2)}) collective-permute-start(f32[72,256]{1,0:T(8,128)S(1)} %add_add_fusion.s0), channel_id=1, source_target_pairs={{2,0},{3,1},{0,2},{1,3},{6,4},{7,5},{4,6},{5,7},{10,8},{11,9},{8,1... | collective-permute-start | bytes 221192 | tf_op jit(solution)/shard_map/scatter_gradients/ppermute | solution.py:35
  132.0 7.2 %collective-permute-start.44 = (f32[72,256]{1,0:T(8,128)S(1)}, f32[72,256]{1,0:T(8,128)S(1)}, u32[]{:S(2)}, u32[]{:S(2)}) collective-permute-start(f32[72,256]{1,0:T(8,128)S(1)} %add_add_fusion.s0), channel_id=1, source_target_pairs={{1,0},{2,1},{3,2},{0,3},{5,4},{6,5},{7,6},{4,7},{9,8},{10,9},{11,1... | collective-permute-start | bytes 221192 | tf_op jit(solution)/shard_map/scatter_gradients/ppermute | solution.py:35
  135.3 20.6 %collective-permute-start.37 = (bf16[8,128,128]{2,1,0:T(8,128)(2,1)S(1)}, bf16[8,128,128]{2,1,0:T(8,128)(2,1)S(1)}, u32[]{:S(2)}, u32[]{:S(2)}) collective-permute-start(bf16[8,128,128]{2,1,0:T(8,128)(2,1)S(1)} %get-tuple-element.99), channel_id=1, source_target_pairs={{48,0},{56,8},{0,16},{8,24},{16,32},{24,40},{32,48},{40,56},{112,6... | collective-permute-start | bytes 786440 | tf_op jit(solution)/shard_map/scatter_gradients/ppermute | solution.py:31
  136.7 19.1 %collective-permute-start.40 = (bf16[8,128,128]{2,1,0:T(8,128)(2,1)S(1)}, bf16[8,128,128]{2,1,0:T(8,128)(2,1)S(1)}, u32[]{:S(2)}, u32[]{:S(2)}) collective-permute-start(bf16[8,128,128]{2,1,0:T(8,128)(2,1)S(1)} %get-tuple-element.102), channel_id=1, source_target_pairs={{32,0},{40,8},{48,16},{56,24},{0,32},{8,40},{16,48},{24,56},{96,64... | collective-permute-start | bytes 786440 | tf_op jit(solution)/shard_map/scatter_gradients/ppermute | solution.py:31
  139.2 16.9 %collective-permute-start.47 = (bf16[8,128,128]{2,1,0:T(8,128)(2,1)S(1)}, bf16[8,128,128]{2,1,0:T(8,128)(2,1)S(1)}, u32[]{:S(2)}, u32[]{:S(2)}) collective-permute-start(bf16[8,128,128]{2,1,0:T(8,128)(2,1)S(1)} %get-tuple-element.105), channel_id=1, source_target_pairs={{16,0},{24,8},{32,16},{40,24},{48,32},{56,40},{0,48},{8,56},{80,64... | collective-permute-start | bytes 786440 | tf_op jit(solution)/shard_map/scatter_gradients/ppermute | solution.py:31
  140.2 15.9 %collective-permute-start.48 = (bf16[8,128,128]{2,1,0:T(8,128)(2,1)S(1)}, bf16[8,128,128]{2,1,0:T(8,128)(2,1)S(1)}, u32[]{:S(2)}, u32[]{:S(2)}) collective-permute-start(bf16[8,128,128]{2,1,0:T(8,128)(2,1)S(1)} %get-tuple-element.107), channel_id=1, source_target_pairs={{112,0},{120,8},{64,16},{72,24},{80,32},{88,40},{96,48},{104,56},{... | collective-permute-start | bytes 786440 | tf_op jit(solution)/shard_map/scatter_gradients/ppermute | solution.py:31
  142.4 13.7 %collective-permute-start.49 = (bf16[8,128,128]{2,1,0:T(8,128)(2,1)S(1)}, bf16[8,128,128]{2,1,0:T(8,128)(2,1)S(1)}, u32[]{:S(2)}, u32[]{:S(2)}) collective-permute-start(bf16[8,128,128]{2,1,0:T(8,128)(2,1)S(1)} %get-tuple-element.109), channel_id=1, source_target_pairs={{80,0},{88,8},{96,16},{104,24},{112,32},{120,40},{64,48},{72,56},{... | collective-permute-start | bytes 786440 | tf_op jit(solution)/shard_map/scatter_gradients/ppermute | solution.py:31
